TPU v7x, 32 devices: a whole 2x2x4 slice. The times are simulated.
32 devices in a mesh: snp: 8 (over y, x, core), samp: 4 (over z).
Axes of the slice: x: 2, y: 2, z: 4, core: 2. Of those that a mesh axis runs over, the one named last changes fastest.
Arguments:
- genotypes: float32 [8192, 2048], P('snp', 'samp'), may hold values from -1 to 2, as said below
- pcs: float32 [20, 2048], P(None, 'samp'), may hold values from -6 to 6
Outputs:
- kinship: float32 [2048, 2048], P('snp', 'samp')
Inputs may be any that keep to these rules, and one draw needn't show every extreme that they name: `genotypes`: observed entries are real-valued dosages from 0 to 2 and -1 marks a missing entry; SNPs whose index is a multiple of 16 are never missing.
All inputs are finite; a program needn't handle non-finite values.
Results may differ from a plain program's by a relative error of at most 0.0015.
Values may be sent and summed in bfloat16 or wider, within the bound.
No kernel may reach another device: no remote copies, remote signals or barrier semaphores. Data moves between devices by JAX's collectives and lax.ppermute only.
A program may use at most 64 MiB of HBM per device.

v0:
```python
import jax
import jax.numpy as jnp
from jax import lax
from jax.sharding import PartitionSpec as P


def tile_terms(piece, resid, spread):
    dims = (((0,), (0,)), ((), ()))
    numer = lax.dot_general(piece[0], resid, dims, preferred_element_type=jnp.float32)
    denom = lax.dot_general(piece[1], spread, dims, preferred_element_type=jnp.float32)
    return jnp.concatenate([numer, denom], axis=1)


def body(genotypes, pcs):
    samp_here = genotypes.shape[1]
    design = jnp.concatenate([jnp.ones((1, samp_here), jnp.float32), pcs], axis=0)
    observed = genotypes >= 0.0
    dosage = jnp.where(observed, genotypes, 0.0)
    gram_part = jnp.dot(design, design.T, precision=lax.Precision.HIGHEST)
    cross_part = jnp.dot(design, dosage.T, precision=lax.Precision.HIGHEST)
    design_gram, cross = lax.psum((gram_part, cross_part), "samp")
    factor = jnp.linalg.cholesky(design_gram)
    coef = jax.scipy.linalg.cho_solve((factor, True), cross)
    fitted = jnp.dot(coef.T, design, precision=lax.Precision.HIGHEST)
    freq = jnp.clip(0.5 * fitted, 0.02, 0.98)
    resid = jnp.where(observed, dosage - 2.0 * freq, 0.0).astype(jnp.bfloat16)
    spread = jnp.where(observed, jnp.sqrt(freq * (1.0 - freq)), 0.0).astype(jnp.bfloat16)
    paired = jnp.stack([resid, spread])
    terms = tile_terms(lax.all_gather(paired, "samp", axis=2, tiled=True), resid, spread)
    sums = lax.psum_scatter(terms, "snp", scatter_dimension=0, tiled=True)
    numer = sums[:, :samp_here]
    denom = sums[:, samp_here:]
    return numer / (4.0 * denom)


def solution(mesh):
    in_specs = (P("snp", "samp"), P(None, "samp"))
    out_specs = P("snp", "samp")
    return jax.shard_map(body, mesh=mesh, in_specs=in_specs, out_specs=out_specs, check_vma=False)
```

profile of v0, /device:TPU:16, one launch (start us, length us, event | category | flops | bytes accessed | tf_op | source)
XLA Modules:
  0.0 292.5 jit_solution(15404692595171027437)
XLA Ops:
  6.5 4.2 %fusion.5 = f32[21,1024]{1,0:T(8,128)} fusion(f32[1024,512]{1,0:T(8,128)} %param.2, f32[20,512]{1,0:T(8,128)} %param.3), kind=kOutput, calls=%fused_computation.14 | convolution fusion | flops 133169152 | bytes 2224128 | tf_op jit(solution)/shard_map/dot_general | solution.py:20
  10.8 0.0 all-reduce.3.cloned.1.call-update
  10.8 0.0 all-gather.2.cloned.1.call-start
  10.8 0.2 fusion.10
  11.0 16.0 %psum.14 = f32[21,21]{0,1:T(8,128)S(1)} all-reduce(f32[21,21]{0,1:T(8,128)S(1)} %fusion.10), channel_id=1, replica_groups=mesh['snp'=8,'samp'=4] {'samp'}, use_global_device_ids=true, to_apply=%region_0.1 | all-reduce | flops 441 | bytes 3528 | tf_op jit(solution)/shard_map/psum | solution.py:21
  27.0 0.1 copy.4
  27.2 1.9 cholesky.16
  29.1 0.7 compare_reduce_fusion
  29.8 0.7 fusion.12
  30.5 1.6 custom-call.10
  32.1 14.0 %all-reduce.3.cloned.1.call-done = f32[21,1024]{1,0:T(8,128)} async-done(((f32[21,1024]{1,0:T(8,128)}), f32[21,1024]{1,0:T(8,128)}) %all-reduce.3.cloned.1.call-update) | async-done | bytes 86032 | tf_op jit(solution)/shard_map/psum | solution.py:21
  46.1 1.2 fusion.15
  47.3 0.2 fusion.13
  47.5 3.0 %select_convert_fusion = (bf16[1024,512]{1,0:T(8,128)(2,1)S(1)}, bf16[1024,512]{1,0:T(8,128)(2,1)S(1)}) fusion(f32[1024,512]{1,0:T(8,128)S(1)} %copy-done, f32[21,1024]{1,0:T(8,128)S(1)} %fusion.13, f32[20,512]{1,0:T(8,128)S(1)} %copy-done.3), kind=kOutput, calls=%fused_computation.10 | convolution fusion | flops 138412032 | bytes 4321280 | tf_op jit(solution)/shard_map/dot_general | solution.py:24
  50.6 1.0 copy-done.1
  51.6 1.6 pad_maximum_fusion.1
  53.2 0.0 reduce-scatter.2.cloned.1.call-start
  53.2 148.0 %all-gather.2.cloned.1.call-done = bf16[2,1024,2048]{2,1,0:T(8,128)(2,1)} async-done(((bf16[2,1024,512]{2,1,0:T(8,128)(2,1)}), bf16[2,1024,2048]{2,1,0:T(8,128)(2,1)}) %all-gather.2.cloned.1.call-update) | async-done | bytes 8388624 | tf_op jit(solution)/shard_map/all_gather | solution.py:29
  201.2 4.7 %fusion = f32[2048,512]{0,1:T(8,128)S(1)} fusion(bf16[1024,512]{1,0:T(8,128)(2,1)S(1)} %copy-done.2, bf16[2,1024,2048]{2,1,0:T(8,128)(2,1)} %all-gather.2.cloned.1.call-done), kind=kOutput, calls=%fused_computation.2 | convolution fusion | flops 2147483648 | bytes 9437184 | tf_op jit(solution)/shard_map/dot_general | solution.py:10
  206.0 2.5 fusion.1
  208.4 3.8 %pad_maximum_fusion = f32[2048,1024]{0,1:T(8,128)} fusion(f32[2048,512]{0,1:T(8,128)S(1)} %fusion, f32[2048,512]{0,1:T(8,128)S(1)} %fusion.1), kind=kLoop, calls=%fused_computation | loop fusion | flops 2097152 | bytes 16777216 | tf_op jit(solution)/shard_map/concatenate | solution.py:11
  212.3 71.4 %reduce-scatter.2.cloned.1.call-done = f32[256,1024]{0,1:T(8,128)} async-done(((f32[2048,1024]{0,1:T(8,128)}), f32[256,1024]{0,1:T(8,128)}) %reduce-scatter.2.cloned.1.call-update) | async-done | bytes 1048592 | tf_op jit(solution)/shard_map/reduce_scatter | solution.py:30
  283.7 1.3 fusion.6
  284.9 1.0 copy.5
  (14 shorter events, 0.1 us)
Async XLA Ops:
  6.5 4.3 %copy-start.3 = (f32[20,512]{1,0:T(8,128)S(1)}, f32[20,512]{1,0:T(8,128)}, u32[]{:S(2)}) copy-start(f32[20,512]{1,0:T(8,128)} %param.3) | copy-start | bytes 122884
  6.5 41.0 %copy-start = (f32[1024,512]{1,0:T(8,128)S(1)}, f32[1024,512]{1,0:T(8,128)}, u32[]{:S(2)}) copy-start(f32[1024,512]{1,0:T(8,128)} %param.2) | copy-start | bytes 6291460
  6.5 39.6 %all-reduce.3.cloned.1.call-start = ((), (), s32[]{:S(2)}) async-start(), calls=%async_computation.1 | async-start | bytes 196608 | tf_op jit(solution)/shard_map/psum | solution.py:21
  10.8 190.4 %all-gather.2.cloned.1.call-start = ((), (), s32[]{:S(2)}) async-start(), calls=%async_computation.2 | async-start | bytes 10485760 | tf_op jit(solution)/shard_map/all_gather | solution.py:29
  50.6 1.0 copy-start.1
  53.1 148.1 %copy-start.2 = (bf16[1024,512]{1,0:T(8,128)(2,1)S(1)}, bf16[1024,512]{1,0:T(8,128)(2,1)}, u32[]{:S(2)}) copy-start(bf16[1024,512]{1,0:T(8,128)(2,1)} %copy-done.1) | copy-start | bytes 3145732
  53.2 230.5 %reduce-scatter.2.cloned.1.call-start = ((), (), s32[]{:S(2)}) async-start(), calls=%async_computation.3 | async-start | bytes 9437184 | tf_op jit(solution)/shard_map/reduce_scatter | solution.py:30
  201.2 4.7 %copy-start.4 = (bf16[2,1024,2048]{2,1,0:T(8,128)(2,1)S(1)}, bf16[2,1024,2048]{2,1,0:T(8,128)(2,1)}, u32[]{:S(2)}) copy-start(bf16[2,1024,2048]{2,1,0:T(8,128)(2,1)} %all-gather.2.cloned.1.call-done) | copy-start | bytes 25165828
Sparse Core Ops, SparseCore 0:
  10.9 35.1 all-reduce.2
  53.3 147.8 all-gather.1
  212.4 71.2 reduce-scatter.1
where the time goes:
time: 294 us; the launch traced here: 292 us
  waiting for transfers between devices  233 us (79%)
  matrix products  16 us (5%)
  blocking collectives  16 us (5%)
  between operations  13.2 us (4%)
  other arithmetic  11.6 us (4%)
    all_gather x1, waiting for transfers between devices, body(): lax.all_gather(paired, 'samp', axis=2, tiled=True)  148 us
    reduce_scatter x1, waiting for transfers between devices, body(): sums = lax.psum_scatter(terms, 'snp', scatter_dimension=0, tiled=True)  71.4 us
    psum x1, blocking collectives, body(): design_gram, cross = lax.psum((gram_part, cross_part), 'samp')  16 us
    psum x1, waiting for transfers between devices, body(): design_gram, cross = lax.psum((gram_part, cross_part), 'samp')  14 us
  transfers between devices with their start and end apart: 3, of which 3 were waited for; matrix products, arithmetic and copies ran while one was open for 2% of the time, Pallas kernels for 0%

commit v1 on v0

v1 whole, which is shorter than its diff:
```python
import jax
import jax.numpy as jnp
from jax import lax
from jax.sharding import PartitionSpec as P

HIGH = lax.Precision.HIGHEST
LINK = jnp.float16
OVER_ROWS = (((0,), (0,)), ((), ()))


def solve_coef(design, cross):
    gram = jnp.dot(design, design.T, precision=HIGH)
    factor = jnp.linalg.cholesky(gram)
    return jax.scipy.linalg.cho_solve((factor, True), cross)


def resid_spread(shifted, coef, design):
    observed = shifted >= -1.5
    fitted = lax.dot_general(coef, design, OVER_ROWS, precision=HIGH)
    freq = jnp.clip(0.5 * fitted, 0.02, 0.98)
    resid = jnp.where(observed, (shifted + 1.0) - 2.0 * freq, 0.0)
    spread = jnp.where(observed, jnp.sqrt(freq * (1.0 - freq)), 0.0)
    return resid.astype(jnp.bfloat16), spread.astype(jnp.bfloat16)


def pair_sums(left, right):
    numer = lax.dot_general(left[0], right[0], OVER_ROWS, preferred_element_type=jnp.float32)
    denom = lax.dot_general(left[1], right[1], OVER_ROWS, preferred_element_type=jnp.float32)
    return jnp.stack([numer, denom])


def pick(index, options):
    items = sorted(options.items())
    out = items[0][1]
    for value, array in items[1:]:
        if array is not out:
            out = jnp.where(index == value, array, out)
    return out


def make_body(snp_n, samp_n):
    both = ("snp", "samp")

    def flat(s, z):
        return s * samp_n + z

    def body(genotypes, pcs):
        width = genotypes.shape[1]
        half = width // 2
        s = lax.axis_index("snp")
        z = lax.axis_index("samp")
        core = lax.rem(s, 2)
        chip = lax.div(s, 2)

        coded = (genotypes - 1.0).astype(LINK)
        halves = [coded[:, :half], coded[:, half:]]
        right = {0: halves}
        left = {0: halves}
        for k in range(1, samp_n):
            up = [(i, i + 1) for i in range(k - 1, samp_n - 1)]
            down = [(samp_n - 1 - a, samp_n - 1 - b) for a, b in up]
            right[k], left[k] = [], []
            for h in range(2):
                right[k].append(lax.ppermute(right[k - 1][h], "samp", up))
                left[k].append(lax.ppermute(left[k - 1][h], "samp", down))

        design = jnp.concatenate([jnp.ones((1, width), jnp.float32), pcs], axis=0)
        dosage = jnp.where(genotypes >= 0.0, genotypes, 0.0)
        cross_part = lax.dot_general(design, dosage, (((1,), (1,)), ((), ())), precision=HIGH)
        mine = jnp.concatenate([cross_part, design], axis=1)
        theirs = [mine]
        for j in range(1, samp_n):
            theirs.append(lax.ppermute(mine, "samp", [(i, i ^ j) for i in range(samp_n)]))
        snps = cross_part.shape[1]
        cross = sum(t[:, :snps] for t in theirs)
        designs = [t[:, snps:] for t in theirs]
        coef = solve_coef(jnp.concatenate(designs, axis=1), cross)

        own = resid_spread(genotypes - 1.0, coef, design)

        units = []
        for j in range(samp_n):
            keep, give = None, None
            parts = []
            for h in range(2):
                if j == 0:
                    rows = (own[0][:, h * half:(h + 1) * half], own[1][:, h * half:(h + 1) * half])
                else:
                    options = {}
                    for i in range(samp_n):
                        b = i ^ j
                        options[i] = left[b - i][h] if b > i else right[i - b][h]
                    block = pick(z, options).astype(jnp.float32)
                    rows = resid_spread(block, coef, designs[j][:, h * half:(h + 1) * half])
                parts.append(pair_sums(rows, own))
            give = jnp.where(core == 0, parts[1], parts[0]).astype(LINK)
            keep = jnp.where(core == 0, parts[0], parts[1])
            got = lax.ppermute(give, "snp", [(i, i ^ 1) for i in range(snp_n)])
            units.append(keep + got.astype(jnp.float32))

        stacked = jnp.stack([u.astype(LINK) for u in units])
        last = samp_n - 1
        total = pick(chip ^ z, {j: units[j] for j in range(samp_n)})
        for d in range(1, samp_n):
            chosen = lax.dynamic_index_in_dim(stacked[:last], jnp.minimum(chip ^ z ^ d, last - 1), 0, keepdims=False)
            early, late = [], []
            for i in range(snp_n):
                for k in range(samp_n):
                    pair = (flat(i, k), flat(i ^ (2 * d), k))
                    (late if (i // 2) ^ k ^ d == last else early).append(pair)
            total = total + lax.ppermute(chosen, both, early).astype(jnp.float32)
            total = total + lax.ppermute(stacked[last], both, late).astype(jnp.float32)
        return total[0] / (4.0 * total[1])

    return body


def plain(genotypes, pcs):
    width = genotypes.shape[1]
    design = jnp.concatenate([jnp.ones((1, width), jnp.float32), pcs], axis=0)
    dosage = jnp.where(genotypes >= 0.0, genotypes, 0.0)
    cross_part = lax.dot_general(design, dosage, (((1,), (1,)), ((), ())), precision=HIGH)
    cross = lax.psum(cross_part, "samp")
    full = lax.all_gather(design, "samp", axis=1, tiled=True)
    coef = solve_coef(full, cross)
    own = resid_spread(genotypes - 1.0, coef, design)
    rows = lax.all_gather(jnp.stack(own), "samp", axis=2, tiled=True)
    sums = lax.psum_scatter(pair_sums(rows, own), "snp", scatter_dimension=1, tiled=True)
    return sums[0] / (4.0 * sums[1])


def solution(mesh):
    snp_n, samp_n = mesh.shape["snp"], mesh.shape["samp"]
    paired = snp_n == 2 * samp_n and samp_n & (samp_n - 1) == 0
    body = make_body(snp_n, samp_n) if paired else plain
    in_specs = (P("snp", "samp"), P(None, "samp"))
    return jax.shard_map(body, mesh=mesh, in_specs=in_specs, out_specs=P("snp", "samp"), check_vma=False)
```

time: 294 us -> 152 us (0.52)
  the two profiles are of different devices: /device:TPU:16 before, /device:TPU:6 now
where the time goes in v1:
time: 152 us; the launch traced here: 151 us
  waiting for transfers between devices  73.5 us (48%)
  starting transfers between devices  34.4 us (23%)
  matrix products  25.1 us (17%)
  other arithmetic  14.7 us (10%)
  local copies, waits for them, and re-layouts  2.74 us (2%)
    ppermute x6, waiting for transfers between devices, body(): left[k].append(lax.ppermute(left[k - 1][h], 'samp', down))  36.3 us
    ppermute x3, waiting for transfers between devices, body(): total = total + lax.ppermute(chosen, both, early).astype(jnp.float32)  12.7 us
    ppermute x3, waiting for transfers between devices, body(): total = total + lax.ppermute(stacked[last], both, late).astype(jnp.float32)  11.9 us
    ppermute x3, waiting for transfers between devices, body(): lax.ppermute(mine, 'samp', [(i, i ^ j) for i in range(samp_n)])  11.7 us
    dot_general x7, matrix products, resid_spread(): fitted = lax.dot_general(coef, design, OVER_ROWS, precision=HIGH)  10.8 us
    ppermute x6, starting transfers between devices, body(): right[k].append(lax.ppermute(right[k - 1][h], 'samp', up))  8.98 us
    ppermute x3, starting transfers between devices, body(): total = total + lax.ppermute(chosen, both, early).astype(jnp.float32)  8.72 us
    ppermute x6, starting transfers between devices, body(): left[k].append(lax.ppermute(left[k - 1][h], 'samp', down))  8.14 us
  transfers between devices with their start and end apart: 25, of which 12 were waited for; matrix products, arithmetic and copies ran while one was open for 15% of the time, Pallas kernels for 0%

profile of v1, /device:TPU:6, one launch (start us, length us, event | category | flops | bytes accessed | tf_op | source)
XLA Modules:
  0.0 151.2 jit_solution(11719784560220428546)
XLA Ops:
  1.0 3.4 %fusion.3 = f32[21,1024]{1,0:T(8,128)S(1)} fusion(f32[1024,512]{1,0:T(8,128)} %param.2, f32[20,512]{1,0:T(8,128)} %param.3), kind=kOutput, calls=%fused_computation.5 | convolution fusion | flops 133169152 | bytes 2224128 | tf_op jit(solution)/shard_map/dot_general | solution.py:69
  4.4 3.7 %collective-permute-start.8 = (f32[21,1536]{1,0:T(8,128)S(1)}, f32[21,1536]{1,0:T(8,128)S(1)}, u32[]{:S(2)}, u32[]{:S(2)}) collective-permute-start(f32[21,1536]{1,0:T(8,128)S(1)} %pad_maximum_fusion.9), channel_id=1, source_target_pairs={{0,3},{1,2},{2,1},{3,0},{4,7},{5,6},{6,5},{7,4},{8,11},{9,10},{10,... | collective-permute-start | bytes 387080 | tf_op jit(solution)/shard_map/ppermute | solution.py:73
  8.8 4.2 %collective-permute-done.8 = f32[21,1536]{1,0:T(8,128)S(1)} collective-permute-done((f32[21,1536]{1,0:T(8,128)S(1)}, f32[21,1536]{1,0:T(8,128)S(1)}, u32[]{:S(2)}, u32[]{:S(2)}) %collective-permute-start.8) | collective-permute-done | bytes 129056 | tf_op jit(solution)/shard_map/ppermute | solution.py:73
  13.0 7.5 %collective-permute-done.7 = f32[21,1536]{1,0:T(8,128)S(1)} collective-permute-done((f32[21,1536]{1,0:T(8,128)S(1)}, f32[21,1536]{1,0:T(8,128)S(1)}, u32[]{:S(2)}, u32[]{:S(2)}) %collective-permute-start.7) | collective-permute-done | bytes 129056 | tf_op jit(solution)/shard_map/ppermute | solution.py:73
  21.0 1.9 %cholesky.16 = f32[21,21]{1,0:T(8,128)S(1)} custom-call(f32[21,21]{1,0:T(8,128)S(1)} %fusion.120), custom_call_target="Cholesky" | custom-call | tf_op jit(solution)/shard_map/jit(cholesky)/cholesky | solution.py:13
  24.2 1.6 %custom-call.10 = f32[1,21,21]{1,2,0:T(8,128)S(1)} custom-call(f32[1,21,21]{2,1,0:T(8,128)S(1)} %fusion.116), custom_call_target="InvertDiagBlocksLowerTriangular" | custom-call | tf_op jit(solution)/shard_map/jit(_cho_solve)/triangular_solve | solution.py:14
  26.4 3.1 %select_convert_fusion = (bf16[1024,512]{1,0:T(8,128)(2,1)S(1)}, bf16[1024,512]{1,0:T(8,128)(2,1)S(1)}, f16[1024,512]{1,0:T(8,128)(2,1)S(1)}) fusion(f32[1024,512]{1,0:T(8,128)S(1)} %copy-done.10, f32[21,1024]{1,0:T(8,128)S(1)} %fusion.117, f32[20,512]{1,0:T(8,128)S(1)} %copy-done.16), kind=kOutput, calls=%fused_computation.6 | convolution fusion | flops 138936320 | bytes 5369856 | tf_op jit(solution)/shard_map/dot_general | solution.py:19
  29.8 1.6 %collective-permute-start.9 = (f16[1024,256]{1,0:T(8,128)(2,1)S(1)}, f16[1024,256]{1,0:T(8,128)(2,1)S(1)}, u32[]{:S(2)}, u32[]{:S(2)}) collective-permute-start(f16[1024,256]{1,0:T(8,128)(2,1)S(1)} %get-tuple-element.12), channel_id=1, source_target_pairs={{0,1},{1,2},{2,3},{4,5},{5,6},{6,7},{8,9},{9,10},{10,11},{12,13},{... | collective-permute-start | bytes 1572872 | tf_op jit(solution)/shard_map/ppermute | solution.py:64
  32.7 4.6 %collective-permute-start = (f16[1024,256]{1,0:T(8,128)(2,1)S(1)}, f16[1024,256]{1,0:T(8,128)(2,1)S(1)}, u32[]{:S(2)}, u32[]{:S(2)}) collective-permute-start(f16[1024,256]{1,0:T(8,128)(2,1)S(1)} %get-tuple-element.11), channel_id=1, source_target_pairs={{0,1},{1,2},{2,3},{4,5},{5,6},{6,7},{8,9},{9,10},{10,11},{12,13},{... | collective-permute-start | bytes 1572872 | tf_op jit(solution)/shard_map/ppermute | solution.py:64
  45.2 1.8 %fusion.9 = f32[1024,256]{1,0:T(8,128)S(1)} fusion(f32[21,1024]{1,0:T(8,128)S(1)} %fusion.117, f32[21,1536]{1,0:T(8,128)} %copy-done.15), kind=kOutput, calls=%fused_computation.28 | convolution fusion | flops 66584576 | bytes 1159168 | tf_op jit(solution)/shard_map/dot_general | solution.py:19
  46.9 1.8 %fusion.8 = f32[1024,256]{1,0:T(8,128)S(1)} fusion(f32[21,1024]{1,0:T(8,128)S(1)} %fusion.117, f32[21,1536]{1,0:T(8,128)} %copy-done.15), kind=kOutput, calls=%fused_computation.27 | convolution fusion | flops 66584576 | bytes 1159168 | tf_op jit(solution)/shard_map/dot_general | solution.py:19
  53.1 4.1 %collective-permute-done.3 = f16[1024,256]{1,0:T(8,128)(2,1)S(1)} collective-permute-done((f16[1024,256]{1,0:T(8,128)(2,1)S(1)}, f16[1024,256]{1,0:T(8,128)(2,1)S(1)}, u32[]{:S(2)}, u32[]{:S(2)}) %collective-permute-start.3) | collective-permute-done | bytes 524320 | tf_op jit(solution)/shard_map/ppermute | solution.py:65
  62.2 7.6 %collective-permute-done.13 = f16[1024,256]{1,0:T(8,128)(2,1)S(1)} collective-permute-done((f16[1024,256]{1,0:T(8,128)(2,1)S(1)}, f16[1024,256]{1,0:T(8,128)(2,1)S(1)}, u32[]{:S(2)}, u32[]{:S(2)}) %collective-permute-start.13) | collective-permute-done | bytes 524320 | tf_op jit(solution)/shard_map/ppermute | solution.py:65
  72.8 8.3 %collective-permute-done.4 = f16[1024,256]{1,0:T(8,128)(2,1)S(1)} collective-permute-done((f16[1024,256]{1,0:T(8,128)(2,1)S(1)}, f16[1024,256]{1,0:T(8,128)(2,1)S(1)}, u32[]{:S(2)}, u32[]{:S(2)}) %collective-permute-start.4) | collective-permute-done | bytes 524320 | tf_op jit(solution)/shard_map/ppermute | solution.py:65
  85.2 7.1 %collective-permute-done.14 = f16[1024,256]{1,0:T(8,128)(2,1)S(1)} collective-permute-done((f16[1024,256]{1,0:T(8,128)(2,1)S(1)}, f16[1024,256]{1,0:T(8,128)(2,1)S(1)}, u32[]{:S(2)}, u32[]{:S(2)}) %collective-permute-start.14) | collective-permute-done | bytes 524320 | tf_op jit(solution)/shard_map/ppermute | solution.py:65
  93.9 9.3 %collective-permute-done.5 = f16[1024,256]{1,0:T(8,128)(2,1)S(1)} collective-permute-done((f16[1024,256]{1,0:T(8,128)(2,1)S(1)}, f16[1024,256]{1,0:T(8,128)(2,1)S(1)}, u32[]{:S(2)}, u32[]{:S(2)}) %collective-permute-start.5) | collective-permute-done | bytes 524320 | tf_op jit(solution)/shard_map/ppermute | solution.py:65
  107.2 3.2 %collective-permute-start.23 = (f16[2,256,512]{2,1,0:T(8,128)(2,1)S(1)}, f16[2,256,512]{2,1,0:T(8,128)(2,1)}, u32[]{:S(2)}, u32[]{:S(2)}) collective-permute-start(f16[2,256,512]{2,1,0:T(8,128)(2,1)S(1)} %get-tuple-element.9), channel_id=1, source_target_pairs={{1,25},{2,26},{3,27},{5,29},{6,30},{7,31},{8,16},{10,18},{11,19},{... | collective-permute-start | bytes 1572872 | tf_op jit(solution)/shard_map/ppermute | solution.py:111
  110.5 3.4 %collective-permute-start.21 = (f16[2,256,512]{2,1,0:T(8,128)(2,1)}, f16[2,256,512]{2,1,0:T(8,128)(2,1)}, u32[]{:S(2)}, u32[]{:S(2)}) collective-permute-start(f16[2,256,512]{2,1,0:T(8,128)(2,1)} %get-tuple-element.10), channel_id=1, source_target_pairs={{0,16},{2,18},{3,19},{4,20},{6,22},{7,23},{9,25},{10,26},{11,27},{... | collective-permute-start | bytes 1572872 | tf_op jit(solution)/shard_map/ppermute | solution.py:111
  113.9 2.1 %collective-permute-start.19 = (f16[2,256,512]{2,1,0:T(8,128)(2,1)}, f16[2,256,512]{2,1,0:T(8,128)(2,1)}, u32[]{:S(2)}, u32[]{:S(2)}) collective-permute-start(f16[2,256,512]{2,1,0:T(8,128)(2,1)} %get-tuple-element.8), channel_id=1, source_target_pairs={{0,8},{1,9},{3,11},{4,12},{5,13},{7,15},{8,0},{9,1},{10,2},{12,4},... | collective-permute-start | bytes 1572872 | tf_op jit(solution)/shard_map/ppermute | solution.py:111
  119.7 2.2 %collective-permute-done.23 = f16[2,256,512]{2,1,0:T(8,128)(2,1)} collective-permute-done((f16[2,256,512]{2,1,0:T(8,128)(2,1)S(1)}, f16[2,256,512]{2,1,0:T(8,128)(2,1)}, u32[]{:S(2)}, u32[]{:S(2)}) %collective-permute-start.23) | collective-permute-done | bytes 524320 | tf_op jit(solution)/shard_map/ppermute | solution.py:111
  123.2 10.5 %collective-permute-done.21 = f16[2,256,512]{2,1,0:T(8,128)(2,1)} collective-permute-done((f16[2,256,512]{2,1,0:T(8,128)(2,1)}, f16[2,256,512]{2,1,0:T(8,128)(2,1)}, u32[]{:S(2)}, u32[]{:S(2)}) %collective-permute-start.21) | collective-permute-done | bytes 524320 | tf_op jit(solution)/shard_map/ppermute | solution.py:111
  133.7 6.4 %collective-permute-done.24 = f16[2,256,512]{2,1,0:T(8,128)(2,1)} collective-permute-done((f16[2,256,512]{2,1,0:T(8,128)(2,1)}, f16[2,256,512]{2,1,0:T(8,128)(2,1)}, u32[]{:S(2)}, u32[]{:S(2)}) %collective-permute-start.24) | collective-permute-done | bytes 524320 | tf_op jit(solution)/shard_map/ppermute | solution.py:112
  140.0 5.5 %collective-permute-done.22 = f16[2,256,512]{2,1,0:T(8,128)(2,1)} collective-permute-done((f16[2,256,512]{2,1,0:T(8,128)(2,1)}, f16[2,256,512]{2,1,0:T(8,128)(2,1)}, u32[]{:S(2)}, u32[]{:S(2)}) %collective-permute-start.22) | collective-permute-done | bytes 524320 | tf_op jit(solution)/shard_map/ppermute | solution.py:112
  145.6 4.7 %convert_add_fusion.6 = f32[2,256,512]{2,1,0:T(8,128)S(1)} fusion(f16[2,256,512]{2,1,0:T(8,128)(2,1)} %collective-permute-done.24, f16[2,256,512]{2,1,0:T(8,128)(2,1)} %collective-permute-done.23, f16[2,256,512]{2,1,0:T(8,128)(2,1)} %collective-permute-done.22, f16[2,256,512]{2,1,0:T(8,128)(2,1)} %collective-permute-done.21, ...), kind=kLoop, calls=%fused_computation.101 | loop fusion | flops 9175040 | bytes 14680068 | tf_op jit(solution)/shard_map/add | solution.py:112
  (114 shorter events, 40.9 us)
Async XLA Ops:
  8.1 12.5 %collective-permute-start.7 = (f32[21,1536]{1,0:T(8,128)S(1)}, f32[21,1536]{1,0:T(8,128)S(1)}, u32[]{:S(2)}, u32[]{:S(2)}) collective-permute-start(f32[21,1536]{1,0:T(8,128)S(1)} %pad_maximum_fusion.9), channel_id=1, source_target_pairs={{0,2},{1,3},{2,0},{3,1},{4,6},{5,7},{6,4},{7,5},{8,10},{9,11},{10,... | collective-permute-start | bytes 387080 | tf_op jit(solution)/shard_map/ppermute | solution.py:73
  8.1 12.5 %collective-permute-start.6 = (f32[21,1536]{1,0:T(8,128)S(1)}, f32[21,1536]{1,0:T(8,128)S(1)}, u32[]{:S(2)}, u32[]{:S(2)}) collective-permute-start(f32[21,1536]{1,0:T(8,128)S(1)} %pad_maximum_fusion.9), channel_id=1, source_target_pairs={{0,1},{1,0},{2,3},{3,2},{4,5},{5,4},{6,7},{7,6},{8,9},{9,8},{10,11... | collective-permute-start | bytes 387080 | tf_op jit(solution)/shard_map/ppermute | solution.py:73
  29.8 18.9 %collective-permute-start.9 = (f16[1024,256]{1,0:T(8,128)(2,1)S(1)}, f16[1024,256]{1,0:T(8,128)(2,1)S(1)}, u32[]{:S(2)}, u32[]{:S(2)}) collective-permute-start(f16[1024,256]{1,0:T(8,128)(2,1)S(1)} %get-tuple-element.12), channel_id=1, source_target_pairs={{0,1},{1,2},{2,3},{4,5},{5,6},{6,7},{8,9},{9,10},{10,11},{12,13},{... | collective-permute-start | bytes 1572872 | tf_op jit(solution)/shard_map/ppermute | solution.py:64
  31.4 18.0 %collective-permute-start.12 = (f16[1024,256]{1,0:T(8,128)(2,1)S(1)}, f16[1024,256]{1,0:T(8,128)(2,1)S(1)}, u32[]{:S(2)}, u32[]{:S(2)}) collective-permute-start(f16[1024,256]{1,0:T(8,128)(2,1)S(1)} %get-tuple-element.12), channel_id=1, source_target_pairs={{3,2},{2,1},{1,0},{7,6},{6,5},{5,4},{11,10},{10,9},{9,8},{15,14},{... | collective-permute-start | bytes 1572872 | tf_op jit(solution)/shard_map/ppermute | solution.py:65
  32.7 20.4 %collective-permute-start = (f16[1024,256]{1,0:T(8,128)(2,1)S(1)}, f16[1024,256]{1,0:T(8,128)(2,1)S(1)}, u32[]{:S(2)}, u32[]{:S(2)}) collective-permute-start(f16[1024,256]{1,0:T(8,128)(2,1)S(1)} %get-tuple-element.11), channel_id=1, source_target_pairs={{0,1},{1,2},{2,3},{4,5},{5,6},{6,7},{8,9},{9,10},{10,11},{12,13},{... | collective-permute-start | bytes 1572872 | tf_op jit(solution)/shard_map/ppermute | solution.py:64
  37.3 19.9 %collective-permute-start.3 = (f16[1024,256]{1,0:T(8,128)(2,1)S(1)}, f16[1024,256]{1,0:T(8,128)(2,1)S(1)}, u32[]{:S(2)}, u32[]{:S(2)}) collective-permute-start(f16[1024,256]{1,0:T(8,128)(2,1)S(1)} %get-tuple-element.11), channel_id=1, source_target_pairs={{3,2},{2,1},{1,0},{7,6},{6,5},{5,4},{11,10},{10,9},{9,8},{15,14},{... | collective-permute-start | bytes 1572872 | tf_op jit(solution)/shard_map/ppermute | solution.py:65
  40.9 18.9 %collective-permute-start.18 = (f16[2,256,512]{2,1,0:T(8,128)(2,1)S(1)}, f16[2,256,512]{2,1,0:T(8,128)(2,1)S(1)}, u32[]{:S(2)}, u32[]{:S(2)}) collective-permute-start(f16[2,256,512]{2,1,0:T(8,128)(2,1)S(1)} %select_convert_fusion.1), channel_id=1, source_target_pairs={{0,4},{4,0},{8,12},{12,8},{16,20},{20,16},{24,28},{28,24},{1,5},{5... | collective-permute-start | bytes 1572872 | tf_op jit(solution)/shard_map/ppermute | solution.py:98
  48.7 12.8 %collective-permute-start.10 = (f16[1024,256]{1,0:T(8,128)(2,1)S(1)}, f16[1024,256]{1,0:T(8,128)(2,1)S(1)}, u32[]{:S(2)}, u32[]{:S(2)}) collective-permute-start(f16[1024,256]{1,0:T(8,128)(2,1)S(1)} %collective-permute-done.9), channel_id=1, source_target_pairs={{1,2},{2,3},{5,6},{6,7},{9,10},{10,11},{13,14},{14,15},{17,18},{18... | collective-permute-start | bytes 1572872 | tf_op jit(solution)/shard_map/ppermute | solution.py:64
  49.4 20.4 %collective-permute-start.13 = (f16[1024,256]{1,0:T(8,128)(2,1)S(1)}, f16[1024,256]{1,0:T(8,128)(2,1)S(1)}, u32[]{:S(2)}, u32[]{:S(2)}) collective-permute-start(f16[1024,256]{1,0:T(8,128)(2,1)S(1)} %collective-permute-done.12), channel_id=1, source_target_pairs={{2,1},{1,0},{6,5},{5,4},{10,9},{9,8},{14,13},{13,12},{18,17},{17,1... | collective-permute-start | bytes 1572872 | tf_op jit(solution)/shard_map/ppermute | solution.py:65
  59.1 24.4 %collective-permute-start.17 = (f16[2,256,512]{2,1,0:T(8,128)(2,1)S(1)}, f16[2,256,512]{2,1,0:T(8,128)(2,1)S(1)}, u32[]{:S(2)}, u32[]{:S(2)}) collective-permute-start(f16[2,256,512]{2,1,0:T(8,128)(2,1)S(1)} %select_convert_fusion.2), channel_id=1, source_target_pairs={{0,4},{4,0},{8,12},{12,8},{16,20},{20,16},{24,28},{28,24},{1,5},{5... | collective-permute-start | bytes 1572872 | tf_op jit(solution)/shard_map/ppermute | solution.py:98
  59.2 13.6 %collective-permute-start.1 = (f16[1024,256]{1,0:T(8,128)(2,1)S(1)}, f16[1024,256]{1,0:T(8,128)(2,1)S(1)}, u32[]{:S(2)}, u32[]{:S(2)}) collective-permute-start(f16[1024,256]{1,0:T(8,128)(2,1)S(1)} %collective-permute-done), channel_id=1, source_target_pairs={{1,2},{2,3},{5,6},{6,7},{9,10},{10,11},{13,14},{14,15},{17,18},{18... | collective-permute-start | bytes 1572872 | tf_op jit(solution)/shard_map/ppermute | solution.py:64
  59.9 21.2 %collective-permute-start.4 = (f16[1024,256]{1,0:T(8,128)(2,1)S(1)}, f16[1024,256]{1,0:T(8,128)(2,1)S(1)}, u32[]{:S(2)}, u32[]{:S(2)}) collective-permute-start(f16[1024,256]{1,0:T(8,128)(2,1)S(1)} %collective-permute-done.3), channel_id=1, source_target_pairs={{2,1},{1,0},{6,5},{5,4},{10,9},{9,8},{14,13},{13,12},{18,17},{17,1... | collective-permute-start | bytes 1572872 | tf_op jit(solution)/shard_map/ppermute | solution.py:65
  61.5 23.7 %collective-permute-start.11 = (f16[1024,256]{1,0:T(8,128)(2,1)S(1)}, f16[1024,256]{1,0:T(8,128)(2,1)S(1)}, u32[]{:S(2)}, u32[]{:S(2)}) collective-permute-start(f16[1024,256]{1,0:T(8,128)(2,1)S(1)} %collective-permute-done.10), channel_id=1, source_target_pairs={{2,3},{6,7},{10,11},{14,15},{18,19},{22,23},{26,27},{30,31}} | collective-permute-start | bytes 1572872 | tf_op jit(solution)/shard_map/ppermute | solution.py:64
  69.8 22.5 %collective-permute-start.14 = (f16[1024,256]{1,0:T(8,128)(2,1)S(1)}, f16[1024,256]{1,0:T(8,128)(2,1)S(1)}, u32[]{:S(2)}, u32[]{:S(2)}) collective-permute-start(f16[1024,256]{1,0:T(8,128)(2,1)S(1)} %collective-permute-done.13), channel_id=1, source_target_pairs={{1,0},{5,4},{9,8},{13,12},{17,16},{21,20},{25,24},{29,28}} | collective-permute-start | bytes 1572872 | tf_op jit(solution)/shard_map/ppermute | solution.py:65
  82.8 22.3 %collective-permute-start.16 = (f16[2,256,512]{2,1,0:T(8,128)(2,1)S(1)}, f16[2,256,512]{2,1,0:T(8,128)(2,1)S(1)}, u32[]{:S(2)}, u32[]{:S(2)}) collective-permute-start(f16[2,256,512]{2,1,0:T(8,128)(2,1)S(1)} %select_convert_fusion.3), channel_id=1, source_target_pairs={{0,4},{4,0},{8,12},{12,8},{16,20},{20,16},{24,28},{28,24},{1,5},{5... | collective-permute-start | bytes 1572872 | tf_op jit(solution)/shard_map/ppermute | solution.py:98
  82.8 11.0 %collective-permute-start.2 = (f16[1024,256]{1,0:T(8,128)(2,1)S(1)}, f16[1024,256]{1,0:T(8,128)(2,1)S(1)}, u32[]{:S(2)}, u32[]{:S(2)}) collective-permute-start(f16[1024,256]{1,0:T(8,128)(2,1)S(1)} %collective-permute-done.1), channel_id=1, source_target_pairs={{2,3},{6,7},{10,11},{14,15},{18,19},{22,23},{26,27},{30,31}} | collective-permute-start | bytes 1572872 | tf_op jit(solution)/shard_map/ppermute | solution.py:64
  83.6 19.6 %collective-permute-start.5 = (f16[1024,256]{1,0:T(8,128)(2,1)S(1)}, f16[1024,256]{1,0:T(8,128)(2,1)S(1)}, u32[]{:S(2)}, u32[]{:S(2)}) collective-permute-start(f16[1024,256]{1,0:T(8,128)(2,1)S(1)} %collective-permute-done.4), channel_id=1, source_target_pairs={{1,0},{5,4},{9,8},{13,12},{17,16},{21,20},{25,24},{29,28}} | collective-permute-start | bytes 1572872 | tf_op jit(solution)/shard_map/ppermute | solution.py:65
  105.0 11.0 %collective-permute-start.15 = (f16[2,256,512]{2,1,0:T(8,128)(2,1)S(1)}, f16[2,256,512]{2,1,0:T(8,128)(2,1)S(1)}, u32[]{:S(2)}, u32[]{:S(2)}) collective-permute-start(f16[2,256,512]{2,1,0:T(8,128)(2,1)S(1)} %select_convert_fusion.4), channel_id=1, source_target_pairs={{0,4},{4,0},{8,12},{12,8},{16,20},{20,16},{24,28},{28,24},{1,5},{5... | collective-permute-start | bytes 1572872 | tf_op jit(solution)/shard_map/ppermute | solution.py:98
  107.2 14.7 %collective-permute-start.23 = (f16[2,256,512]{2,1,0:T(8,128)(2,1)S(1)}, f16[2,256,512]{2,1,0:T(8,128)(2,1)}, u32[]{:S(2)}, u32[]{:S(2)}) collective-permute-start(f16[2,256,512]{2,1,0:T(8,128)(2,1)S(1)} %get-tuple-element.9), channel_id=1, source_target_pairs={{1,25},{2,26},{3,27},{5,29},{6,30},{7,31},{8,16},{10,18},{11,19},{... | collective-permute-start | bytes 1572872 | tf_op jit(solution)/shard_map/ppermute | solution.py:111
  110.5 23.2 %collective-permute-start.21 = (f16[2,256,512]{2,1,0:T(8,128)(2,1)}, f16[2,256,512]{2,1,0:T(8,128)(2,1)}, u32[]{:S(2)}, u32[]{:S(2)}) collective-permute-start(f16[2,256,512]{2,1,0:T(8,128)(2,1)} %get-tuple-element.10), channel_id=1, source_target_pairs={{0,16},{2,18},{3,19},{4,20},{6,22},{7,23},{9,25},{10,26},{11,27},{... | collective-permute-start | bytes 1572872 | tf_op jit(solution)/shard_map/ppermute | solution.py:111
  113.9 19.8 %collective-permute-start.19 = (f16[2,256,512]{2,1,0:T(8,128)(2,1)}, f16[2,256,512]{2,1,0:T(8,128)(2,1)}, u32[]{:S(2)}, u32[]{:S(2)}) collective-permute-start(f16[2,256,512]{2,1,0:T(8,128)(2,1)} %get-tuple-element.8), channel_id=1, source_target_pairs={{0,8},{1,9},{3,11},{4,12},{5,13},{7,15},{8,0},{9,1},{10,2},{12,4},... | collective-permute-start | bytes 1572872 | tf_op jit(solution)/shard_map/ppermute | solution.py:111
  117.1 23.0 %collective-permute-start.24 = (f16[2,256,512]{2,1,0:T(8,128)(2,1)}, f16[2,256,512]{2,1,0:T(8,128)(2,1)}, u32[]{:S(2)}, u32[]{:S(2)}) collective-permute-start(f16[2,256,512]{2,1,0:T(8,128)(2,1)} %fusion.168), channel_id=1, source_target_pairs={{0,24},{4,28},{9,17},{13,21},{18,10},{22,14},{27,3},{31,7}} | collective-permute-start | bytes 1572872 | tf_op jit(solution)/shard_map/ppermute | solution.py:112
  118.4 27.2 %collective-permute-start.22 = (f16[2,256,512]{2,1,0:T(8,128)(2,1)}, f16[2,256,512]{2,1,0:T(8,128)(2,1)}, u32[]{:S(2)}, u32[]{:S(2)}) collective-permute-start(f16[2,256,512]{2,1,0:T(8,128)(2,1)} %fusion.168), channel_id=1, source_target_pairs={{1,17},{5,21},{8,24},{12,28},{19,3},{23,7},{26,10},{30,14}} | collective-permute-start | bytes 1572872 | tf_op jit(solution)/shard_map/ppermute | solution.py:112
  121.9 23.7 %collective-permute-start.20 = (f16[2,256,512]{2,1,0:T(8,128)(2,1)}, f16[2,256,512]{2,1,0:T(8,128)(2,1)}, u32[]{:S(2)}, u32[]{:S(2)}) collective-permute-start(f16[2,256,512]{2,1,0:T(8,128)(2,1)} %fusion.168), channel_id=1, source_target_pairs={{2,10},{6,14},{11,3},{15,7},{16,24},{20,28},{25,17},{29,21}} | collective-permute-start | bytes 1572872 | tf_op jit(solution)/shard_map/ppermute | solution.py:112
  (18 other events, 320.7 us)

commit v2 on v0

v2 whole, which is shorter than its diff:
```python
import functools

import jax
import jax.numpy as jnp
from jax import lax
from jax.experimental import pallas as pl
from jax.experimental.pallas import tpu as pltpu
from jax.sharding import PartitionSpec as P

HIGH = lax.Precision.HIGHEST
LINK = jnp.float16
OVER_ROWS = (((0,), (0,)), ((), ()))
RANGE = 120.0
PAD = 32
VMEM_BYTES = 56 * 2**20
DESIGN_ROWS = 21
STEP = 256
FREE = pl.CostEstimate(flops=0, bytes_accessed=0, transcendentals=0)


def solve_coef(design, cross):
    gram = jnp.dot(design, design.T, precision=HIGH)
    factor = jnp.linalg.cholesky(gram)
    return jax.scipy.linalg.cho_solve((factor, True), cross)


def encode(genotypes):
    return jnp.where(genotypes >= 0.0, jnp.exp2(RANGE * genotypes - RANGE), 0.0).astype(jnp.bfloat16)


def decode(coded):
    value = coded.astype(jnp.float32)
    observed = value > 0.0
    return jnp.log2(jnp.where(observed, value, 1.0)) * (1.0 / RANGE) + 1.0, observed


def thirds(x):
    a = x.astype(jnp.bfloat16)
    rest = x - a.astype(jnp.float32)
    b = rest.astype(jnp.bfloat16)
    return a, b, (rest - b.astype(jnp.float32)).astype(jnp.bfloat16)


def left_stack(x):
    a, b, c = thirds(x)
    return jnp.concatenate([a, a, b, b, a, c], axis=0)


def right_stack(y):
    a, b, c = thirds(y)
    return jnp.concatenate([a, b, a, b, c, a], axis=0)


def resid_spread(dosage, observed, fitted):
    twice = jnp.clip(fitted, 0.04, 1.96)
    product = twice * (2.0 - twice)
    resid = jnp.where(observed, dosage - twice, 0.0)
    spread = jnp.where(observed, 0.5 * jnp.sqrt(product), 0.0)
    return resid.astype(jnp.bfloat16), spread.astype(jnp.bfloat16)


def product(left, right):
    return lax.dot_general(left, right, OVER_ROWS, preferred_element_type=jnp.float32)


def coef_kernel(mine_ref, a_ref, b_ref, c_ref, coef_ref):
    rows, snps = mine_ref.shape[0], coef_ref.shape[1]
    across_lanes = (((1,), (1,)), ((), ()))
    cross = mine_ref[:, :snps] + a_ref[:, :snps] + b_ref[:, :snps] + c_ref[:, :snps]
    gram = jnp.zeros((rows, rows), jnp.float32)
    for ref in (mine_ref, a_ref, b_ref, c_ref):
        design = ref[:, snps:]
        gram = gram + lax.dot_general(design, design, across_lanes, precision=HIGH, preferred_element_type=jnp.float32)
    row = lax.broadcasted_iota(jnp.int32, (rows, rows), 0)
    unit = (row == lax.broadcasted_iota(jnp.int32, (rows, rows), 1)).astype(jnp.float32)
    gram = gram + jnp.where(row >= DESIGN_ROWS, unit, 0.0)
    left, inverse = gram, unit
    for j in range(DESIGN_ROWS):
        pivot = 1.0 / left[j:j + 1, j:j + 1]
        factor = (left[:, j:j + 1] - unit[:, j:j + 1]) * pivot
        left, inverse = left - factor * left[j:j + 1, :], inverse - factor * inverse[j:j + 1, :]
    coef = jnp.dot(inverse, cross, precision=HIGH, preferred_element_type=jnp.float32)
    rest = cross - jnp.dot(gram, coef, precision=HIGH, preferred_element_type=jnp.float32)
    coef = coef + jnp.dot(inverse, rest, precision=HIGH, preferred_element_type=jnp.float32)
    coef_ref[...] = jnp.concatenate([coef, jnp.zeros((PAD - rows, snps), jnp.float32)], axis=0)


def coefficients(theirs, snps):
    vmem = pl.BlockSpec(memory_space=pltpu.VMEM)
    return pl.pallas_call(
        coef_kernel,
        out_shape=jax.ShapeDtypeStruct((PAD, snps), jnp.float32),
        in_specs=[vmem] * 4,
        out_specs=vmem,
        compiler_params=pltpu.CompilerParams(vmem_limit_bytes=VMEM_BYTES),
        cost_estimate=FREE,
    )(*theirs)


def own_kernel(core_ref, own_ref, coef_ref, design_ref, terms_ref, sums_ref, coefs, designs):
    _, _, _, quarter, width = sums_ref.shape
    snps = coef_ref.shape[1]
    coefs[...] = left_stack(coef_ref[...])
    designs[...] = right_stack(design_ref[...])

    def terms(k, _):
        at = pl.ds(pl.multiple_of(k * STEP, STEP), STEP)
        dosage = own_ref[at, :]
        fitted = product(coefs[:, at], designs[...])
        terms_ref[0, at, :], terms_ref[1, at, :] = resid_spread(dosage, dosage >= 0.0, fitted)
        return 0

    lax.fori_loop(0, snps // STEP, terms, 0)
    for p in range(2):
        for h in range(2):
            first = (2 * h + p) * quarter
            for t in range(2):
                sums_ref[jnp.bitwise_xor(core_ref[0], h), p, t] = product(terms_ref[t, :, first:first + quarter], terms_ref[t])


def block_kernel(sources, place_ref, terms_ref, coef_ref, design_ref, *refs):
    *coded, sums_ref, coefs, designs, rows_ref = refs
    _, _, _, quarter, width = sums_ref.shape
    snps = coef_ref.shape[1]
    coefs[...] = left_stack(coef_ref[...])
    designs[...] = right_stack(design_ref[...])

    def terms(k, _):
        at = pl.ds(pl.multiple_of(k * STEP, STEP), STEP)
        fitted = product(coefs[:, at], designs[...])
        for g, choices in enumerate(sources):
            here = slice(2 * g * quarter, 2 * (g + 1) * quarter)
            values = [coded[i][at, first:first + 2 * quarter] for i, first in choices]
            value = values[0] if len(values) == 1 else jnp.where(place_ref[1] == 1, values[0], values[1])
            dosage, observed = decode(value)
            rows_ref[0, at, here], rows_ref[1, at, here] = resid_spread(dosage, observed, fitted[:, here])
        return 0

    lax.fori_loop(0, snps // STEP, terms, 0)
    for g in range(2):
        for h in range(2):
            first = (2 * g + h) * quarter
            for t in range(2):
                sums_ref[jnp.bitwise_xor(place_ref[0], h), g, t] = product(rows_ref[t, :, first:first + quarter], terms_ref[t])


def block_sums(place, coef, design, own=None, terms=None, coded=(), sources=None):
    snps, width = coef.shape[1], design.shape[1]
    vmem = pl.BlockSpec(memory_space=pltpu.VMEM)
    pair = (2, snps, width)
    sums = jax.ShapeDtypeStruct((2, 2, 2, width // 4, width), jnp.float32)
    scratch = [pltpu.VMEM((6 * PAD, snps), jnp.bfloat16), pltpu.VMEM((6 * PAD, width), jnp.bfloat16)]
    if own is not None:
        kernel, operands = own_kernel, (place, own, coef, design)
        out = (jax.ShapeDtypeStruct(pair, jnp.bfloat16), sums)
    else:
        kernel, operands = functools.partial(block_kernel, sources), (place, terms, coef, design, *coded)
        out = sums
        scratch.append(pltpu.VMEM(pair, jnp.bfloat16))
    return pl.pallas_call(
        kernel,
        out_shape=out,
        in_specs=[pl.BlockSpec(memory_space=pltpu.SMEM)] + [vmem] * (len(operands) - 1),
        out_specs=jax.tree.map(lambda _: vmem, out),
        scratch_shapes=scratch,
        compiler_params=pltpu.CompilerParams(vmem_limit_bytes=VMEM_BYTES),
        cost_estimate=FREE,
    )(*operands)


def kinship(sums):
    return sums[0] / (4.0 * sums[1])


def after(value, *earlier):
    return lax.optimization_barrier((value, *earlier))[0]


def padded(x):
    return jnp.pad(x, ((0, PAD - x.shape[0]), (0, 0)))


def line_of_four(genotypes, pcs):
    both = ("snp", "samp")
    width = genotypes.shape[1]
    half, quarter = width // 2, width // 4
    s = lax.axis_index("snp")
    z = lax.axis_index("samp")
    core = lax.rem(s, 2)
    chip = lax.div(s, 2)
    inner = jnp.logical_or(z == 1, z == 2).astype(jnp.int32)
    place = jnp.stack([core, inner])
    other_core = [(i, i ^ 1) for i in range(8)]

    def by_parts(array):
        return jnp.concatenate([array[:, i * quarter:(i + 1) * quarter] for i in (0, 2, 1, 3)], axis=1)

    def part(array, p):
        return array[:, p * half:(p + 1) * half]

    swap = [(0, 1), (1, 0), (2, 3), (3, 2)]
    middle = [(1, 2), (2, 1)]
    outward = [(1, 0), (2, 3)]
    ends = [(0, 3), (3, 0)]
    coded = encode(by_parts(genotypes))
    near = lax.ppermute(coded, "samp", swap)
    across = lax.ppermute(coded, "samp", middle)
    far = [lax.ppermute(part(near, p), "samp", middle) for p in range(2)]
    out = [lax.ppermute(part(across, p), "samp", outward) for p in range(2)]
    direct = after(coded, near, across)
    end = [lax.ppermute(part(direct, p), "samp", ends) for p in range(2)]

    design = jnp.concatenate([jnp.ones((1, width), jnp.float32), pcs], axis=0)
    design = jnp.pad(design, ((0, -DESIGN_ROWS % 8), (0, 0)))
    dosage = jnp.where(genotypes >= 0.0, genotypes, 0.0)
    cross_part = lax.dot_general(design, dosage, (((1,), (1,)), ((), ())), precision=HIGH)
    snps = cross_part.shape[1]
    mine = jnp.concatenate([cross_part, design], axis=1)
    theirs = [mine] + [lax.ppermute(mine, "samp", [(i, i ^ j) for i in range(4)]) for j in range(1, 4)]
    theirs = [after(t, near, across) for t in theirs]
    coef = coefficients(theirs, snps)
    designs = [padded(t[:, snps:]) for t in theirs]

    terms, own = block_sums(place, coef, designs[0], own=genotypes)
    first = block_sums(place, coef, by_parts(designs[1]), terms=terms, coded=(near,), sources=(((0, 0),), ((0, half),)))
    two, three = by_parts(designs[2]), by_parts(designs[3])
    rows = []
    for p in range(2):
        late = block_sums(
            place,
            coef,
            jnp.concatenate([part(two, p), part(three, p)], axis=1),
            terms=terms,
            coded=(far[p], out[p], across, end[p]),
            sources=(((0, 0), (1, 0)), ((2, p * half), (3, 0))),
        )

        def units(side):
            return jnp.concatenate([own[side, p:p + 1], first[side, p:p + 1], late[side]])

        got = lax.ppermute(units(1).astype(LINK), "snp", other_core)
        sums = units(0) + got.astype(jnp.float32)
        total = lax.dynamic_index_in_dim(sums, chip ^ z, 0, keepdims=False)
        for d in range(1, 4):
            chosen = lax.dynamic_index_in_dim(sums, chip ^ z ^ d, 0, keepdims=False).astype(LINK)
            total = total + lax.ppermute(chosen, "snp", [(i, i ^ (2 * d)) for i in range(8)]).astype(jnp.float32)
        rows.append(kinship(total))
    return jnp.concatenate(rows, axis=0)


def any_mesh(genotypes, pcs):
    width = genotypes.shape[1]
    design = jnp.concatenate([jnp.ones((1, width), jnp.float32), pcs], axis=0)
    observed = genotypes >= 0.0
    dosage = jnp.where(observed, genotypes, 0.0)
    cross_part = lax.dot_general(design, dosage, (((1,), (1,)), ((), ())), precision=HIGH)
    cross = lax.psum(cross_part, "samp")
    full = lax.all_gather(design, "samp", axis=1, tiled=True)
    fitted = lax.dot_general(solve_coef(full, cross), design, OVER_ROWS, precision=HIGH)
    own = resid_spread(dosage, observed, fitted)
    rows = lax.all_gather(jnp.stack(own), "samp", axis=2, tiled=True)
    sums = jnp.stack([product(rows[t], own[t]) for t in range(2)])
    return kinship(lax.psum_scatter(sums, "snp", scatter_dimension=1, tiled=True))


def solution(mesh):
    body = line_of_four if (mesh.shape["snp"], mesh.shape["samp"]) == (8, 4) else any_mesh
    in_specs = (P("snp", "samp"), P(None, "samp"))
    return jax.shard_map(body, mesh=mesh, in_specs=in_specs, out_specs=P("snp", "samp"), check_vma=False)
```

time: 294 us -> 146 us (0.50)
  waiting for transfers between devices: 233 us -> 54.3 us
  Pallas kernels: 0 us -> 32.4 us
  starting transfers between devices: 0.09 us -> 27.7 us
  blocking collectives: 16 us -> 0 us
  matrix products: 16 us -> 1.78 us
  between operations: 13.2 us -> 0.36 us
  local copies, waits for them, and re-layouts: 2.07 us -> 9.73 us
  other arithmetic: 11.6 us -> 17.2 us
    all_gather x1 -> x0, waiting for transfers between devices: 148 us -> none  [body(): lax.all_gather(paired, 'samp', axis=2, tiled=True)]
    reduce_scatter x1 -> x0, waiting for transfers between devices: 71.4 us -> none  [body(): sums = lax.psum_scatter(terms, 'snp', scatter_dimension=0, tiled=True)]
    ppermute x0 -> x19, waiting for transfers between devices: none -> 54.3 us  [the longest x1 19.8 us: line_of_four(): across = lax.ppermute(coded, 'samp', middle)]
    pallas_call x0 -> x5, Pallas kernels: none -> 32.4 us  [the longest x4 27.8 us: block_sums(): pl.pallas_call(kernel, out_shape=out, in_specs=[pl.BlockSpec(memory_space...]
    ppermute x0 -> x19, starting transfers between devices: none -> 27.7 us  [the longest x6 8.14 us: line_of_four(): lax.ppermute(chosen, 'snp', [(i, i ^ 2 * d) for i in range(8)])]
    psum x1 -> x0, blocking collectives: 16 us -> none  [body(): design_gram, cross = lax.psum((gram_part, cross_part), 'samp')]
    psum x1 -> x0, waiting for transfers between devices: 14 us -> none  [body(): design_gram, cross = lax.psum((gram_part, cross_part), 'samp')]
    dot_general x5 -> x1, matrix products: 14.6 us -> 1.78 us  [line_of_four(): lax.dot_general(design, dosage, (((1,), (1,)), ((), ())), precision=HIGH)]
  transfers between devices with their start and end apart: 3 -> 19, of which waited for: 3 -> 9; matrix products, arithmetic and copies ran while one was open for 2% -> 15% of each run, Pallas kernels for 0% -> 23%
where the time goes in v2:
time: 146 us; the launch traced here: 143 us
  waiting for transfers between devices  54.3 us (37%)
  Pallas kernels  32.4 us (22%)
  starting transfers between devices  27.7 us (19%)
  other arithmetic  17.2 us (12%)
  local copies, waits for them, and re-layouts  9.73 us (7%)
  matrix products  1.78 us (1%)
    pallas_call x4, Pallas kernels, block_sums(): pl.pallas_call(kernel, out_shape=out, in_specs=[pl.BlockSpec(memory_space...  27.8 us
    ppermute x1, waiting for transfers between devices, line_of_four(): across = lax.ppermute(coded, 'samp', middle)  19.8 us
    ppermute x6, waiting for transfers between devices, line_of_four(): lax.ppermute(chosen, 'snp', [(i, i ^ 2 * d) for i in range(8)])  17.4 us
    ppermute x2, waiting for transfers between devices, line_of_four(): out = [lax.ppermute(part(across, p), 'samp', outward) for p in range(2)]  12.4 us
    ppermute x6, starting transfers between devices, line_of_four(): lax.ppermute(chosen, 'snp', [(i, i ^ 2 * d) for i in range(8)])  8.14 us
    ppermute x2, starting transfers between devices, line_of_four(): far = [lax.ppermute(part(near, p), 'samp', middle) for p in range(2)]  7.14 us
    squeeze x2, other arithmetic, units(): late[side]  4.64 us
    pallas_call x1, Pallas kernels, coefficients(): pl.pallas_call(coef_kernel, out_shape=jax.ShapeDtypeStruct((PAD, snps), j...  4.64 us
  transfers between devices with their start and end apart: 19, of which 9 were waited for; matrix products, arithmetic and copies ran while one was open for 15% of the time, Pallas kernels for 23%

profile of v2, /device:TPU:16, one launch (start us, length us, event | category | flops | bytes accessed | tf_op | source)
XLA Modules:
  0.0 143.5 jit_solution(17975881763238727851)
XLA Ops:
  0.0 1.7 %fusion.19 = (f32[1024,128]{1,0:T(8,128)S(1)}, f32[1024,128]{1,0:T(8,128)S(1)}, f32[1024,128]{1,0:T(8,128)S(1)}, f32[1024,128]{1,0:T(8,128)S(1)}) fusion(f32[1024,512]{1,0:T(8,128)} %own_ref.1), kind=kLoop, calls=%fused_computation.68 | loop fusion | bytes 4194304 | tf_op jit(solution)/shard_map/slice | solution.py:196
  2.2 2.5 %collective-permute-start.1 = (bf16[1024,512]{1,0:T(8,128)(2,1)S(1)}, bf16[1024,512]{1,0:T(8,128)(2,1)S(1)}, u32[]{:S(2)}, u32[]{:S(2)}) collective-permute-start(bf16[1024,512]{1,0:T(8,128)(2,1)S(1)} %select_convert_fusion), channel_id=1, source_target_pairs={{1,2},{2,1},{5,6},{6,5},{9,10},{10,9},{13,14},{14,13},{17,18},{18,... | collective-permute-start | bytes 3145736 | tf_op jit(solution)/shard_map/ppermute | solution.py:207
  4.9 1.8 %fusion = f32[24,1024]{1,0:T(8,128)S(1)} fusion(f32[1024,512]{1,0:T(8,128)S(1)} %copy-done, f32[20,512]{1,0:T(8,128)S(1)} %copy-done.13), kind=kOutput, calls=%fused_computation.1 | convolution fusion | flops 152068096 | bytes 2236416 | tf_op jit(solution)/shard_map/dot_general | solution.py:216
  6.7 1.6 %collective-permute-start.4 = (f32[24,1536]{1,0:T(8,128)S(1)}, f32[24,1536]{1,0:T(8,128)S(1)}, u32[]{:S(2)}, u32[]{:S(2)}) collective-permute-start(f32[24,1536]{1,0:T(8,128)S(1)} %pad_maximum_fusion.4.mine_ref), channel_id=1, source_target_pairs={{0,3},{1,2},{2,1},{3,0},{4,7},{5,6},{6,5},{7,4},{8,11},{9,10},{10,... | collective-permute-start | bytes 442376 | tf_op jit(solution)/shard_map/ppermute | solution.py:219
  8.3 2.8 %collective-permute-start.3 = (f32[24,1536]{1,0:T(8,128)S(1)}, f32[24,1536]{1,0:T(8,128)}, u32[]{:S(2)}, u32[]{:S(2)}) collective-permute-start(f32[24,1536]{1,0:T(8,128)S(1)} %pad_maximum_fusion.4.mine_ref), channel_id=1, source_target_pairs={{0,2},{1,3},{2,0},{3,1},{4,6},{5,7},{6,4},{7,5},{8,10},{9,11},{10,... | collective-permute-start | bytes 442376 | tf_op jit(solution)/shard_map/ppermute | solution.py:219
  11.8 19.8 %collective-permute-done.1.refs_2_ = bf16[1024,512]{1,0:T(8,128)(2,1)S(1)} collective-permute-done((bf16[1024,512]{1,0:T(8,128)(2,1)S(1)}, bf16[1024,512]{1,0:T(8,128)(2,1)S(1)}, u32[]{:S(2)}, u32[]{:S(2)}) %collective-permute-start.1) | collective-permute-done | bytes 1048608 | tf_op jit(solution)/shard_map/ppermute | solution.py:207
  33.1 2.1 %collective-permute-start.13 = (bf16[1024,256]{1,0:T(8,128)(2,1)S(1)}, bf16[1024,256]{1,0:T(8,128)(2,1)}, u32[]{:S(2)}, u32[]{:S(2)}) collective-permute-start(bf16[1024,256]{1,0:T(8,128)(2,1)S(1)} %get-tuple-element.44), channel_id=1, source_target_pairs={{1,0},{2,3},{5,4},{6,7},{9,8},{10,11},{13,12},{14,15},{17,16},{18,... | collective-permute-start | bytes 1572872 | tf_op jit(solution)/shard_map/ppermute | solution.py:209
  35.2 4.6 %collective-permute-done.4.c_ref = f32[24,1536]{1,0:T(8,128)S(1)} collective-permute-done((f32[24,1536]{1,0:T(8,128)S(1)}, f32[24,1536]{1,0:T(8,128)S(1)}, u32[]{:S(2)}, u32[]{:S(2)}) %collective-permute-start.4) | collective-permute-done | bytes 147488 | tf_op jit(solution)/shard_map/ppermute | solution.py:219
  43.0 3.5 %collective-permute-start.12 = (bf16[1024,256]{1,0:T(8,128)(2,1)S(1)}, bf16[1024,256]{1,0:T(8,128)(2,1)S(1)}, u32[]{:S(2)}, u32[]{:S(2)}) collective-permute-start(bf16[1024,256]{1,0:T(8,128)(2,1)S(1)} %get-tuple-element.46), channel_id=1, source_target_pairs={{1,2},{2,1},{5,6},{6,5},{9,10},{10,9},{13,14},{14,13},{17,18},{18,... | collective-permute-start | bytes 1572872 | tf_op jit(solution)/shard_map/ppermute | solution.py:208
  47.2 4.6 %shard_map.28.coef_ref = f32[32,1024]{1,0:T(8,128)} custom-call(f32[24,1536]{1,0:T(8,128)} %copy-done.6, f32[24,1536]{1,0:T(8,128)} %collective-permute-done.2.a_ref, f32[24,1536]{1,0:T(8,128)} %collective-permute-done.3.b_ref, f32[24,1536]{1,0:T(8,128)} %copy-done.12), custom_call_target="tpu_custom_call" | custom-call | tf_op jit(solution)/shard_map/pallas_call | solution.py:90
  52.4 6.3 %shard_map.29 = (bf16[2,1024,512]{2,1,0:T(8,128)(2,1)}, f32[2,2,2,128,512]{4,3,2,1,0:T(8,128)}) custom-call(s32[2]{0:T(128)} %pad_add_fusion.core_ref.place_ref, f32[1024,512]{1,0:T(8,128)} %own_ref.1, f32[32,1024]{1,0:T(8,128)} %shard_map.28.coef_ref, f32[32,512]{1,0:T(8,128)} %pad.19.design_ref), custom_call_target="tpu_custom_call" | custom-call | tf_op jit(solution)/shard_map/pallas_call | solution.py:160
  58.7 6.8 %shard_map.30 = f32[2,2,2,128,512]{4,3,2,1,0:T(8,128)} custom-call(s32[2]{0:T(128)} %pad_add_fusion.core_ref.place_ref, bf16[2,1024,512]{2,1,0:T(8,128)(2,1)} %get-tuple-element.17.terms_ref, f32[32,1024]{1,0:T(8,128)} %shard_map.28.coef_ref, f32[32,512]{1,0:T(8,128)} %pad_maximum_fusion.5.design_ref, bf16[1024,512]{1,0:T(8,128)(2,1)} %copy-done.5), custom_call_target="tpu_custom_call" | custom-call | tf_op jit(solution)/shard_map/pallas_call | solution.py:160
  65.5 2.0 %convert.28 = f16[2,2,2,128,512]{4,3,2,1,0:T(8,128)(2,1)S(1)} convert(f32[2,2,2,128,512]{4,3,2,1,0:T(8,128)} %shard_map.30) | non-fusion elementwise | flops 524288 | bytes 3145728 | tf_op jit(solution)/shard_map/convert.16
  69.2 12.4 %collective-permute-done.13.refs_1_ = bf16[1024,256]{1,0:T(8,128)(2,1)} collective-permute-done((bf16[1024,256]{1,0:T(8,128)(2,1)S(1)}, bf16[1024,256]{1,0:T(8,128)(2,1)}, u32[]{:S(2)}, u32[]{:S(2)}) %collective-permute-start.13) | collective-permute-done | bytes 524320 | tf_op jit(solution)/shard_map/ppermute | solution.py:209
  81.6 3.7 %collective-permute-start.5 = (bf16[1024,256]{1,0:T(8,128)(2,1)S(1)}, bf16[1024,256]{1,0:T(8,128)(2,1)S(1)}, u32[]{:S(2)}, u32[]{:S(2)}) collective-permute-start(bf16[1024,256]{1,0:T(8,128)(2,1)S(1)} %get-tuple-element.45), channel_id=1, source_target_pairs={{1,2},{2,1},{5,6},{6,5},{9,10},{10,9},{13,14},{14,13},{17,18},{18,... | collective-permute-start | bytes 1572872 | tf_op jit(solution)/shard_map/ppermute | solution.py:208
  86.9 7.3 %shard_map.32 = f32[2,2,2,128,512]{4,3,2,1,0:T(8,128)} custom-call(s32[2]{0:T(128)} %pad_add_fusion.core_ref.place_ref, bf16[2,1024,512]{2,1,0:T(8,128)(2,1)} %get-tuple-element.17.terms_ref, f32[32,1024]{1,0:T(8,128)} %shard_map.28.coef_ref, f32[32,512]{1,0:T(8,128)} %pad_maximum_fusion.7.design_ref, bf16[1024,256]{1,0:T(8,128)(2,1)} %copy-done.10, ...), custom_call_target="tpu_custom_call" | custom-call | tf_op jit(solution)/shard_map/pallas_call | solution.py:160
  94.2 1.8 %fusion.3 = (f16[2,2,128,512]{3,2,1,0:T(8,128)(2,1)S(1)}, f32[2,2,128,512]{3,2,1,0:T(8,128)S(1)}) fusion(f32[2,2,2,128,512]{4,3,2,1,0:T(8,128)} %shard_map.32), kind=kLoop, calls=%fused_computation.14 | loop fusion | flops 262144 | bytes 3670016 | tf_op jit(solution)/shard_map/squeeze | solution.py:239
  99.7 7.3 %shard_map.31 = f32[2,2,2,128,512]{4,3,2,1,0:T(8,128)} custom-call(s32[2]{0:T(128)} %pad_add_fusion.core_ref.place_ref, bf16[2,1024,512]{2,1,0:T(8,128)(2,1)} %get-tuple-element.17.terms_ref, f32[32,1024]{1,0:T(8,128)} %shard_map.28.coef_ref, f32[32,512]{1,0:T(8,128)} %pad_maximum_fusion.6.design_ref, bf16[1024,256]{1,0:T(8,128)(2,1)} %copy-done.11, ...), custom_call_target="tpu_custom_call" | custom-call | tf_op jit(solution)/shard_map/pallas_call | solution.py:160
  107.0 2.9 %fusion.2 = (f16[2,2,128,512]{3,2,1,0:T(8,128)(2,1)S(1)}, f32[2,2,128,512]{3,2,1,0:T(8,128)}) fusion(f32[2,2,2,128,512]{4,3,2,1,0:T(8,128)} %shard_map.31), kind=kLoop, calls=%fused_computation.13 | loop fusion | flops 262144 | bytes 3670016 | tf_op jit(solution)/shard_map/squeeze | solution.py:239
  118.5 1.7 %maximum_add_fusion = f32[4,2,128,512]{3,2,1,0:T(8,128)S(1)} fusion(f32[2,2,128,512]{3,2,1,0:T(8,128)S(1)} %copy-done.4, f32[1,2,128,512]{3,2,1,0:T(8,128)S(1)} %get-tuple-element.26, f32[1,2,128,512]{3,2,1,0:T(8,128)S(1)} %get-tuple-element.66, f16[4,2,128,512]{3,2,1,0:T(8,128)(2,1)} %collective-permute-done.8), kind=kLoop, calls=%fused_computation.3 | loop fusion | flops 2097152 | bytes 5242880 | tf_op jit(solution)/shard_map/add | solution.py:242
  125.7 5.1 %collective-permute-done.18 = f16[2,128,512]{2,1,0:T(8,128)(2,1)S(1)} collective-permute-done((f16[2,128,512]{2,1,0:T(8,128)(2,1)S(1)}, f16[2,128,512]{2,1,0:T(8,128)(2,1)S(1)}, u32[]{:S(2)}, u32[]{:S(2)}) %collective-permute-start.18) | collective-permute-done | bytes 262176 | tf_op jit(solution)/shard_map/ppermute | solution.py:246
  130.8 1.9 %collective-permute-done.17 = f16[2,128,512]{2,1,0:T(8,128)(2,1)S(1)} collective-permute-done((f16[2,128,512]{2,1,0:T(8,128)(2,1)S(1)}, f16[2,128,512]{2,1,0:T(8,128)(2,1)S(1)}, u32[]{:S(2)}, u32[]{:S(2)}) %collective-permute-start.17) | collective-permute-done | bytes 262176 | tf_op jit(solution)/shard_map/ppermute | solution.py:246
  132.9 2.5 %collective-permute-done.9 = f16[2,128,512]{2,1,0:T(8,128)(2,1)S(1)} collective-permute-done((f16[2,128,512]{2,1,0:T(8,128)(2,1)S(1)}, f16[2,128,512]{2,1,0:T(8,128)(2,1)S(1)}, u32[]{:S(2)}, u32[]{:S(2)}) %collective-permute-start.9) | collective-permute-done | bytes 262176 | tf_op jit(solution)/shard_map/ppermute | solution.py:246
  135.4 5.7 %collective-permute-done.11 = f16[2,128,512]{2,1,0:T(8,128)(2,1)S(1)} collective-permute-done((f16[2,128,512]{2,1,0:T(8,128)(2,1)S(1)}, f16[2,128,512]{2,1,0:T(8,128)(2,1)S(1)}, u32[]{:S(2)}, u32[]{:S(2)}) %collective-permute-start.11) | collective-permute-done | bytes 262176 | tf_op jit(solution)/shard_map/ppermute | solution.py:246
  (84 shorter events, 30.7 us)
Async XLA Ops:
  2.2 29.4 %collective-permute-start.1 = (bf16[1024,512]{1,0:T(8,128)(2,1)S(1)}, bf16[1024,512]{1,0:T(8,128)(2,1)S(1)}, u32[]{:S(2)}, u32[]{:S(2)}) collective-permute-start(bf16[1024,512]{1,0:T(8,128)(2,1)S(1)} %select_convert_fusion), channel_id=1, source_target_pairs={{1,2},{2,1},{5,6},{6,5},{9,10},{10,9},{13,14},{14,13},{17,18},{18,... | collective-permute-start | bytes 3145736 | tf_op jit(solution)/shard_map/ppermute | solution.py:207
  4.7 28.3 %collective-permute-start = (bf16[1024,512]{1,0:T(8,128)(2,1)S(1)}, bf16[1024,512]{1,0:T(8,128)(2,1)S(1)}, u32[]{:S(2)}, u32[]{:S(2)}) collective-permute-start(bf16[1024,512]{1,0:T(8,128)(2,1)S(1)} %select_convert_fusion), channel_id=1, source_target_pairs={{0,1},{1,0},{2,3},{3,2},{4,5},{5,4},{6,7},{7,6},{8,9},{9,8},{10,11... | collective-permute-start | bytes 3145736 | tf_op jit(solution)/shard_map/ppermute | solution.py:206
  6.7 40.5 %copy-start.6 = (f32[24,1536]{1,0:T(8,128)}, f32[24,1536]{1,0:T(8,128)S(1)}, u32[]{:S(2)}) copy-start(f32[24,1536]{1,0:T(8,128)S(1)} %pad_maximum_fusion.4.mine_ref) | copy-start | bytes 442372
  6.7 33.1 %collective-permute-start.4 = (f32[24,1536]{1,0:T(8,128)S(1)}, f32[24,1536]{1,0:T(8,128)S(1)}, u32[]{:S(2)}, u32[]{:S(2)}) collective-permute-start(f32[24,1536]{1,0:T(8,128)S(1)} %pad_maximum_fusion.4.mine_ref), channel_id=1, source_target_pairs={{0,3},{1,2},{2,1},{3,0},{4,7},{5,6},{6,5},{7,4},{8,11},{9,10},{10,... | collective-permute-start | bytes 442376 | tf_op jit(solution)/shard_map/ppermute | solution.py:219
  8.3 31.5 %collective-permute-start.3 = (f32[24,1536]{1,0:T(8,128)S(1)}, f32[24,1536]{1,0:T(8,128)}, u32[]{:S(2)}, u32[]{:S(2)}) collective-permute-start(f32[24,1536]{1,0:T(8,128)S(1)} %pad_maximum_fusion.4.mine_ref), channel_id=1, source_target_pairs={{0,2},{1,3},{2,0},{3,1},{4,6},{5,7},{6,4},{7,5},{8,10},{9,11},{10,... | collective-permute-start | bytes 442376 | tf_op jit(solution)/shard_map/ppermute | solution.py:219
  11.1 28.8 %collective-permute-start.2 = (f32[24,1536]{1,0:T(8,128)S(1)}, f32[24,1536]{1,0:T(8,128)}, u32[]{:S(2)}, u32[]{:S(2)}) collective-permute-start(f32[24,1536]{1,0:T(8,128)S(1)} %pad_maximum_fusion.4.mine_ref), channel_id=1, source_target_pairs={{0,1},{1,0},{2,3},{3,2},{4,5},{5,4},{6,7},{7,6},{8,9},{9,8},{10,11... | collective-permute-start | bytes 442376 | tf_op jit(solution)/shard_map/ppermute | solution.py:219
  31.6 8.2 %copy-start.2 = (bf16[1024,512]{1,0:T(8,128)(2,1)}, bf16[1024,512]{1,0:T(8,128)(2,1)S(1)}, u32[]{:S(2)}) copy-start(bf16[1024,512]{1,0:T(8,128)(2,1)S(1)} %collective-permute-done.1.refs_2_) | copy-start | bytes 3145732
  31.7 66.2 %collective-permute-start.6 = (bf16[1024,256]{1,0:T(8,128)(2,1)S(1)}, bf16[1024,256]{1,0:T(8,128)(2,1)S(1)}, u32[]{:S(2)}, u32[]{:S(2)}) collective-permute-start(bf16[1024,256]{1,0:T(8,128)(2,1)S(1)} %get-tuple-element.43), channel_id=1, source_target_pairs={{1,0},{2,3},{5,4},{6,7},{9,8},{10,11},{13,12},{14,15},{17,16},{18,... | collective-permute-start | bytes 1572872 | tf_op jit(solution)/shard_map/ppermute | solution.py:209
  33.1 9.9 %copy-start.5 = (bf16[1024,512]{1,0:T(8,128)(2,1)}, bf16[1024,512]{1,0:T(8,128)(2,1)S(1)}, u32[]{:S(2)}) copy-start(bf16[1024,512]{1,0:T(8,128)(2,1)S(1)} %collective-permute-done.refs_0_) | copy-start | bytes 3145732
  33.1 48.6 %collective-permute-start.13 = (bf16[1024,256]{1,0:T(8,128)(2,1)S(1)}, bf16[1024,256]{1,0:T(8,128)(2,1)}, u32[]{:S(2)}, u32[]{:S(2)}) collective-permute-start(bf16[1024,256]{1,0:T(8,128)(2,1)S(1)} %get-tuple-element.44), channel_id=1, source_target_pairs={{1,0},{2,3},{5,4},{6,7},{9,8},{10,11},{13,12},{14,15},{17,16},{18,... | collective-permute-start | bytes 1572872 | tf_op jit(solution)/shard_map/ppermute | solution.py:209
  41.5 56.4 %collective-permute-start.7 = (bf16[1024,256]{1,0:T(8,128)(2,1)S(1)}, bf16[1024,256]{1,0:T(8,128)(2,1)S(1)}, u32[]{:S(2)}, u32[]{:S(2)}) collective-permute-start(bf16[1024,256]{1,0:T(8,128)(2,1)S(1)} %get-tuple-element.41), channel_id=1, source_target_pairs={{0,3},{3,0},{4,7},{7,4},{8,11},{11,8},{12,15},{15,12},{16,19},{19,... | collective-permute-start | bytes 1572872 | tf_op jit(solution)/shard_map/ppermute | solution.py:211
  42.2 43.1 %collective-permute-start.14 = (bf16[1024,256]{1,0:T(8,128)(2,1)S(1)}, bf16[1024,256]{1,0:T(8,128)(2,1)S(1)}, u32[]{:S(2)}, u32[]{:S(2)}) collective-permute-start(bf16[1024,256]{1,0:T(8,128)(2,1)S(1)} %get-tuple-element.42), channel_id=1, source_target_pairs={{0,3},{3,0},{4,7},{7,4},{8,11},{11,8},{12,15},{15,12},{16,19},{19,... | collective-permute-start | bytes 1572872 | tf_op jit(solution)/shard_map/ppermute | solution.py:211
  43.0 42.3 %collective-permute-start.12 = (bf16[1024,256]{1,0:T(8,128)(2,1)S(1)}, bf16[1024,256]{1,0:T(8,128)(2,1)S(1)}, u32[]{:S(2)}, u32[]{:S(2)}) collective-permute-start(bf16[1024,256]{1,0:T(8,128)(2,1)S(1)} %get-tuple-element.46), channel_id=1, source_target_pairs={{1,2},{2,1},{5,6},{6,5},{9,10},{10,9},{13,14},{14,13},{17,18},{18,... | collective-permute-start | bytes 1572872 | tf_op jit(solution)/shard_map/ppermute | solution.py:208
  81.6 16.3 %collective-permute-start.5 = (bf16[1024,256]{1,0:T(8,128)(2,1)S(1)}, bf16[1024,256]{1,0:T(8,128)(2,1)S(1)}, u32[]{:S(2)}, u32[]{:S(2)}) collective-permute-start(bf16[1024,256]{1,0:T(8,128)(2,1)S(1)} %get-tuple-element.45), channel_id=1, source_target_pairs={{1,2},{2,1},{5,6},{6,5},{9,10},{10,9},{13,14},{14,13},{17,18},{18,... | collective-permute-start | bytes 1572872 | tf_op jit(solution)/shard_map/ppermute | solution.py:208
  97.3 15.8 %collective-permute-start.15 = (f16[4,2,128,512]{3,2,1,0:T(8,128)(2,1)}, f16[4,2,128,512]{3,2,1,0:T(8,128)(2,1)}, u32[]{:S(2)}, u32[]{:S(2)}) collective-permute-start(f16[4,2,128,512]{3,2,1,0:T(8,128)(2,1)} %pad_maximum_fusion.2), channel_id=1, source_target_pairs={{0,4},{4,0},{8,12},{12,8},{16,20},{20,16},{24,28},{28,24},{1,5},{5... | collective-permute-start | bytes 3145736 | tf_op jit(solution)/shard_map/ppermute | solution.py:241
  107.0 4.6 %copy-start.1 = (f32[2,2,2,128,512]{4,3,2,1,0:T(8,128)S(1)}, f32[2,2,2,128,512]{4,3,2,1,0:T(8,128)}, u32[]{:S(2)}) copy-start(f32[2,2,2,128,512]{4,3,2,1,0:T(8,128)} %shard_map.30) | copy-start | bytes 6291460
  111.2 7.3 %collective-permute-start.8 = (f16[4,2,128,512]{3,2,1,0:T(8,128)(2,1)}, f16[4,2,128,512]{3,2,1,0:T(8,128)(2,1)}, u32[]{:S(2)}, u32[]{:S(2)}) collective-permute-start(f16[4,2,128,512]{3,2,1,0:T(8,128)(2,1)} %pad_maximum_fusion.1), channel_id=1, source_target_pairs={{0,4},{4,0},{8,12},{12,8},{16,20},{20,16},{24,28},{28,24},{1,5},{5... | collective-permute-start | bytes 3145736 | tf_op jit(solution)/shard_map/ppermute | solution.py:241
  114.7 3.8 %copy-start.4 = (f32[2,2,128,512]{3,2,1,0:T(8,128)S(1)}, f32[2,2,128,512]{3,2,1,0:T(8,128)}, u32[]{:S(2)}) copy-start(f32[2,2,128,512]{3,2,1,0:T(8,128)} %get-tuple-element.23) | copy-start | bytes 3145732
  114.9 9.2 %collective-permute-start.16 = (f16[2,128,512]{2,1,0:T(8,128)(2,1)S(1)}, f16[2,128,512]{2,1,0:T(8,128)(2,1)S(1)}, u32[]{:S(2)}, u32[]{:S(2)}) collective-permute-start(f16[2,128,512]{2,1,0:T(8,128)(2,1)S(1)} %get-tuple-element.28), channel_id=1, source_target_pairs={{0,8},{4,12},{8,0},{12,4},{16,24},{20,28},{24,16},{28,20},{1,9},{5... | collective-permute-start | bytes 786440 | tf_op jit(solution)/shard_map/ppermute | solution.py:246
  116.5 14.3 %collective-permute-start.18 = (f16[2,128,512]{2,1,0:T(8,128)(2,1)S(1)}, f16[2,128,512]{2,1,0:T(8,128)(2,1)S(1)}, u32[]{:S(2)}, u32[]{:S(2)}) collective-permute-start(f16[2,128,512]{2,1,0:T(8,128)(2,1)S(1)} %get-tuple-element.29), channel_id=1, source_target_pairs={{0,24},{4,28},{8,16},{12,20},{16,8},{20,12},{24,0},{28,4},{1,25},{... | collective-permute-start | bytes 786440 | tf_op jit(solution)/shard_map/ppermute | solution.py:246
  118.0 14.7 %collective-permute-start.17 = (f16[2,128,512]{2,1,0:T(8,128)(2,1)S(1)}, f16[2,128,512]{2,1,0:T(8,128)(2,1)S(1)}, u32[]{:S(2)}, u32[]{:S(2)}) collective-permute-start(f16[2,128,512]{2,1,0:T(8,128)(2,1)S(1)} %get-tuple-element.30), channel_id=1, source_target_pairs={{0,16},{4,20},{8,24},{12,28},{16,0},{20,4},{24,8},{28,12},{1,17},{... | collective-permute-start | bytes 786440 | tf_op jit(solution)/shard_map/ppermute | solution.py:246
  120.3 15.1 %collective-permute-start.9 = (f16[2,128,512]{2,1,0:T(8,128)(2,1)S(1)}, f16[2,128,512]{2,1,0:T(8,128)(2,1)S(1)}, u32[]{:S(2)}, u32[]{:S(2)}) collective-permute-start(f16[2,128,512]{2,1,0:T(8,128)(2,1)S(1)} %get-tuple-element.19), channel_id=1, source_target_pairs={{0,8},{4,12},{8,0},{12,4},{16,24},{20,28},{24,16},{28,20},{1,9},{5... | collective-permute-start | bytes 786440 | tf_op jit(solution)/shard_map/ppermute | solution.py:246
  121.9 19.3 %collective-permute-start.11 = (f16[2,128,512]{2,1,0:T(8,128)(2,1)S(1)}, f16[2,128,512]{2,1,0:T(8,128)(2,1)S(1)}, u32[]{:S(2)}, u32[]{:S(2)}) collective-permute-start(f16[2,128,512]{2,1,0:T(8,128)(2,1)S(1)} %get-tuple-element.20), channel_id=1, source_target_pairs={{0,24},{4,28},{8,16},{12,20},{16,8},{20,12},{24,0},{28,4},{1,25},{... | collective-permute-start | bytes 786440 | tf_op jit(solution)/shard_map/ppermute | solution.py:246
  124.1 18.3 %collective-permute-start.10 = (f16[2,128,512]{2,1,0:T(8,128)(2,1)S(1)}, f16[2,128,512]{2,1,0:T(8,128)(2,1)S(1)}, u32[]{:S(2)}, u32[]{:S(2)}) collective-permute-start(f16[2,128,512]{2,1,0:T(8,128)(2,1)S(1)} %get-tuple-element.21), channel_id=1, source_target_pairs={{0,16},{4,20},{8,24},{12,28},{16,0},{20,4},{24,8},{28,12},{1,17},{... | collective-permute-start | bytes 786440 | tf_op jit(solution)/shard_map/ppermute | solution.py:246
  (10 other events, 16.8 us)

commit v3 on v2

--- a/solution.py
+++ b/solution.py
@@ -12,7 +12,7 @@
 OVER_ROWS = (((0,), (0,)), ((), ()))
 RANGE = 120.0
 PAD = 32
-VMEM_BYTES = 56 * 2**20
+VMEM_BYTES = 24 * 2**20
 DESIGN_ROWS = 21
 STEP = 256
 FREE = pl.CostEstimate(flops=0, bytes_accessed=0, transcendentals=0)
@@ -97,8 +97,28 @@
     )(*theirs)
 
 
-def own_kernel(core_ref, own_ref, coef_ref, design_ref, terms_ref, sums_ref, coefs, designs):
-    _, _, _, quarter, width = sums_ref.shape
+def pack(sums):
+    size = jnp.exp2(8.0 * jnp.log2(jnp.maximum(jnp.abs(sums), 1e-30)) + 20.0)
+    return jnp.where(sums < 0.0, -size, size).astype(jnp.bfloat16)
+
+
+def unpack(packed):
+    value = packed.astype(jnp.float32)
+    size = jnp.abs(value)
+    sums = jnp.exp2(jnp.log2(jnp.where(size > 0.0, size, 1.0)) * 0.125 - 2.5)
+    return jnp.where(size > 0.0, jnp.where(value < 0.0, -sums, sums), 0.0)
+
+
+def split_cores(first_core, left, right, keep_ref, give_ref, g, order):
+    quarter = keep_ref.shape[2]
+    for t in range(2):
+        a, b = [product(left[t, :, first:first + quarter], right[t]) for first in order]
+        keep_ref[g, t] = jnp.where(first_core, a, b)
+        give_ref[g, t] = pack(jnp.where(first_core, b, a))
+
+
+def own_kernel(place_ref, own_ref, coef_ref, design_ref, terms_ref, keep_ref, give_ref, coefs, designs):
+    quarter = keep_ref.shape[2]
     snps = coef_ref.shape[1]
     coefs[...] = left_stack(coef_ref[...])
     designs[...] = right_stack(design_ref[...])
@@ -112,15 +132,12 @@
 
     lax.fori_loop(0, snps // STEP, terms, 0)
     for p in range(2):
-        for h in range(2):
-            first = (2 * h + p) * quarter
-            for t in range(2):
-                sums_ref[jnp.bitwise_xor(core_ref[0], h), p, t] = product(terms_ref[t, :, first:first + quarter], terms_ref[t])
+        split_cores(place_ref[0] == 0, terms_ref, terms_ref, keep_ref, give_ref, p, (p * quarter, (2 + p) * quarter))
 
 
 def block_kernel(sources, place_ref, terms_ref, coef_ref, design_ref, *refs):
-    *coded, sums_ref, coefs, designs, rows_ref = refs
-    _, _, _, quarter, width = sums_ref.shape
+    *coded, keep_ref, give_ref, coefs, designs, rows_ref = refs
+    quarter = keep_ref.shape[2]
     snps = coef_ref.shape[1]
     coefs[...] = left_stack(coef_ref[...])
     designs[...] = right_stack(design_ref[...])
@@ -130,7 +147,7 @@
         fitted = product(coefs[:, at], designs[...])
         for g, choices in enumerate(sources):
             here = slice(2 * g * quarter, 2 * (g + 1) * quarter)
-            values = [coded[i][at, first:first + 2 * quarter] for i, first in choices]
+            values = [coded[i][at, :] for i in choices]
             value = values[0] if len(values) == 1 else jnp.where(place_ref[1] == 1, values[0], values[1])
             dosage, observed = decode(value)
             rows_ref[0, at, here], rows_ref[1, at, here] = resid_spread(dosage, observed, fitted[:, here])
@@ -138,36 +155,82 @@
 
     lax.fori_loop(0, snps // STEP, terms, 0)
     for g in range(2):
-        for h in range(2):
-            first = (2 * g + h) * quarter
-            for t in range(2):
-                sums_ref[jnp.bitwise_xor(place_ref[0], h), g, t] = product(rows_ref[t, :, first:first + quarter], terms_ref[t])
+        split_cores(place_ref[0] == 0, rows_ref, terms_ref, keep_ref, give_ref, g, (2 * g * quarter, (2 * g + 1) * quarter))
 
 
 def block_sums(place, coef, design, own=None, terms=None, coded=(), sources=None):
     snps, width = coef.shape[1], design.shape[1]
     vmem = pl.BlockSpec(memory_space=pltpu.VMEM)
     pair = (2, snps, width)
-    sums = jax.ShapeDtypeStruct((2, 2, 2, width // 4, width), jnp.float32)
+    sums = (2, 2, width // 4, width)
+    out = (jax.ShapeDtypeStruct(sums, jnp.float32), jax.ShapeDtypeStruct(sums, jnp.bfloat16))
     scratch = [pltpu.VMEM((6 * PAD, snps), jnp.bfloat16), pltpu.VMEM((6 * PAD, width), jnp.bfloat16)]
     if own is not None:
         kernel, operands = own_kernel, (place, own, coef, design)
-        out = (jax.ShapeDtypeStruct(pair, jnp.bfloat16), sums)
+        out = (jax.ShapeDtypeStruct(pair, jnp.bfloat16),) + out
     else:
         kernel, operands = functools.partial(block_kernel, sources), (place, terms, coef, design, *coded)
-        out = sums
         scratch.append(pltpu.VMEM(pair, jnp.bfloat16))
     return pl.pallas_call(
         kernel,
         out_shape=out,
         in_specs=[pl.BlockSpec(memory_space=pltpu.SMEM)] + [vmem] * (len(operands) - 1),
-        out_specs=jax.tree.map(lambda _: vmem, out),
+        out_specs=tuple(vmem for _ in out),
         scratch_shapes=scratch,
         compiler_params=pltpu.CompilerParams(vmem_limit_bytes=VMEM_BYTES),
         cost_estimate=FREE,
     )(*operands)
 
 
+def add_kernel(place_ref, own_ref, near_ref, late_ref, got_own_ref, got_near_ref, got_late_ref, mine_ref, *refs):
+    *sent, sums = refs
+    pairs = ((own_ref, 0, got_own_ref), (near_ref, 0, got_near_ref), (late_ref, 0, got_late_ref), (late_ref, 1, got_late_ref))
+    for j, (kept, i, got) in enumerate(pairs):
+        sums[j] = kept[i] + unpack(got[i])
+    mine_ref[...] = sums[place_ref[2]]
+    for d, ref in enumerate(sent, 1):
+        ref[...] = pack(sums[jnp.bitwise_xor(place_ref[2], d)])
+
+
+def add_cores(place, p, own, near, late, got_own, got_near, got_late):
+    shape = late.shape[1:]
+    one = pl.BlockSpec((1,) + shape, lambda i: (p, 0, 0, 0))
+    both = pl.BlockSpec((2,) + shape, lambda i: (0, 0, 0, 0))
+    whole = pl.BlockSpec(shape, lambda i: (0, 0, 0))
+    return pl.pallas_call(
+        add_kernel,
+        grid=(1,),
+        out_shape=(jax.ShapeDtypeStruct(shape, jnp.float32),) + (jax.ShapeDtypeStruct(shape, jnp.bfloat16),) * 3,
+        in_specs=[pl.BlockSpec(memory_space=pltpu.SMEM), one, one, both, one, one, both],
+        out_specs=(whole,) * 4,
+        scratch_shapes=[pltpu.VMEM((4,) + shape, jnp.float32)],
+        compiler_params=pltpu.CompilerParams(vmem_limit_bytes=VMEM_BYTES),
+        cost_estimate=FREE,
+    )(place, own, near, late, got_own, got_near, got_late)
+
+
+def divide_kernel(*refs):
+    *parts, out_ref = refs
+    quarter = out_ref.shape[0] // 2
+    for p in range(2):
+        mine, *got = parts[4 * p:4 * p + 4]
+        sums = [mine[t] + unpack(got[0][t]) + unpack(got[1][t]) + unpack(got[2][t]) for t in range(2)]
+        out_ref[p * quarter:(p + 1) * quarter, :] = sums[0] / (4.0 * sums[1])
+
+
+def divide(parts):
+    _, quarter, width = parts[0].shape
+    vmem = pl.BlockSpec(memory_space=pltpu.VMEM)
+    return pl.pallas_call(
+        divide_kernel,
+        out_shape=jax.ShapeDtypeStruct((2 * quarter, width), jnp.float32),
+        in_specs=[vmem] * len(parts),
+        out_specs=vmem,
+        compiler_params=pltpu.CompilerParams(vmem_limit_bytes=VMEM_BYTES),
+        cost_estimate=FREE,
+    )(*parts)
+
+
 def kinship(sums):
     return sums[0] / (4.0 * sums[1])
 
@@ -181,34 +244,23 @@
 
 
 def line_of_four(genotypes, pcs):
-    both = ("snp", "samp")
     width = genotypes.shape[1]
     half, quarter = width // 2, width // 4
     s = lax.axis_index("snp")
     z = lax.axis_index("samp")
-    core = lax.rem(s, 2)
     chip = lax.div(s, 2)
-    inner = jnp.logical_or(z == 1, z == 2).astype(jnp.int32)
-    place = jnp.stack([core, inner])
+    place = jnp.stack([lax.rem(s, 2), jnp.logical_or(z == 1, z == 2).astype(jnp.int32), chip ^ z])
     other_core = [(i, i ^ 1) for i in range(8)]
 
-    def by_parts(array):
-        return jnp.concatenate([array[:, i * quarter:(i + 1) * quarter] for i in (0, 2, 1, 3)], axis=1)
-
     def part(array, p):
-        return array[:, p * half:(p + 1) * half]
-
-    swap = [(0, 1), (1, 0), (2, 3), (3, 2)]
-    middle = [(1, 2), (2, 1)]
-    outward = [(1, 0), (2, 3)]
-    ends = [(0, 3), (3, 0)]
-    coded = encode(by_parts(genotypes))
-    near = lax.ppermute(coded, "samp", swap)
-    across = lax.ppermute(coded, "samp", middle)
-    far = [lax.ppermute(part(near, p), "samp", middle) for p in range(2)]
-    out = [lax.ppermute(part(across, p), "samp", outward) for p in range(2)]
-    direct = after(coded, near, across)
-    end = [lax.ppermute(part(direct, p), "samp", ends) for p in range(2)]
+        a, b = p * quarter, p * quarter + half
+        return jnp.concatenate([array[:, a:a + quarter], array[:, b:b + quarter]], axis=1)
+
+    coded = [encode(part(genotypes, p)) for p in range(2)]
+    near = [lax.ppermute(c, "samp", [(i, i ^ 1) for i in range(4)]) for c in coded]
+    three = [lax.ppermute(c, "samp", [(i, i ^ 3) for i in range(4)]) for c in coded]
+    far = [lax.ppermute(c, "samp", [(1, 2), (2, 1)]) for c in near]
+    out = [lax.ppermute(c, "samp", [(1, 0), (2, 3)]) for c in three]
 
     design = jnp.concatenate([jnp.ones((1, width), jnp.float32), pcs], axis=0)
     design = jnp.pad(design, ((0, -DESIGN_ROWS % 8), (0, 0)))
@@ -217,35 +269,23 @@
     snps = cross_part.shape[1]
     mine = jnp.concatenate([cross_part, design], axis=1)
     theirs = [mine] + [lax.ppermute(mine, "samp", [(i, i ^ j) for i in range(4)]) for j in range(1, 4)]
-    theirs = [after(t, near, across) for t in theirs]
     coef = coefficients(theirs, snps)
     designs = [padded(t[:, snps:]) for t in theirs]
 
-    terms, own = block_sums(place, coef, designs[0], own=genotypes)
-    first = block_sums(place, coef, by_parts(designs[1]), terms=terms, coded=(near,), sources=(((0, 0),), ((0, half),)))
-    two, three = by_parts(designs[2]), by_parts(designs[3])
-    rows = []
+    terms, keep_own, give_own = block_sums(place, coef, designs[0], own=genotypes)
+    near_design = jnp.concatenate([part(designs[1], 0), part(designs[1], 1)], axis=1)
+    keep_near, give_near = block_sums(place, coef, near_design, terms=terms, coded=near, sources=((0,), (1,)))
+    got_own, got_near = [lax.ppermute(g, "snp", other_core) for g in (give_own, give_near)]
+    parts = []
     for p in range(2):
-        late = block_sums(
-            place,
-            coef,
-            jnp.concatenate([part(two, p), part(three, p)], axis=1),
-            terms=terms,
-            coded=(far[p], out[p], across, end[p]),
-            sources=(((0, 0), (1, 0)), ((2, p * half), (3, 0))),
-        )
-
-        def units(side):
-            return jnp.concatenate([own[side, p:p + 1], first[side, p:p + 1], late[side]])
-
-        got = lax.ppermute(units(1).astype(LINK), "snp", other_core)
-        sums = units(0) + got.astype(jnp.float32)
-        total = lax.dynamic_index_in_dim(sums, chip ^ z, 0, keepdims=False)
+        late_design = jnp.concatenate([part(designs[2], p), part(designs[3], p)], axis=1)
+        keep, give = block_sums(place, coef, late_design, terms=terms, coded=(far[p], out[p], three[p]), sources=((0, 1), (2,)))
+        got = lax.ppermute(give, "snp", other_core)
+        mine, *sent = add_cores(place, p, keep_own, keep_near, keep, got_own, got_near, got)
+        parts.append(mine)
         for d in range(1, 4):
-            chosen = lax.dynamic_index_in_dim(sums, chip ^ z ^ d, 0, keepdims=False).astype(LINK)
-            total = total + lax.ppermute(chosen, "snp", [(i, i ^ (2 * d)) for i in range(8)]).astype(jnp.float32)
-        rows.append(kinship(total))
-    return jnp.concatenate(rows, axis=0)
+            parts.append(lax.ppermute(sent[d - 1], "snp", [(i, i ^ (2 * d)) for i in range(8)]))
+    return divide(parts)
 
 
 def any_mesh(genotypes, pcs):

time: 146 us -> 135 us (0.925); the launches traced: 143 us -> 135 us
  other arithmetic: 17.2 us -> 2.27 us
  waiting for transfers between devices: 54.3 us -> 66 us
  local copies, waits for them, and re-layouts: 9.73 us -> 5.03 us
  Pallas kernels: 32.4 us -> 28.5 us
  starting transfers between devices: 27.7 us -> 31.2 us
    ppermute x3, waiting for transfers between devices: 4.63 us -> 51.2 us  [line_of_four(): lax.ppermute(mine, 'samp', [(i, i ^ j) for i in range(4)])]
    ppermute x16 -> x18, waiting for transfers between devices: 49.6 us -> 14.7 us  [the longest x6 14.7 us: line_of_four(): lax.ppermute(sent[d - 1], 'snp', [(i, i ^ 2 * d) for i in range(8)])]
    pallas_call x4, Pallas kernels: 27.8 us -> 17.2 us  [block_sums(): pl.pallas_call(kernel, out_shape=out, in_specs=[pl.BlockSpec(memory_space...]
    pallas_call x0 -> x3, Pallas kernels: none -> 7.53 us  [the longest x2 5.33 us: add_cores(): pl.pallas_call(add_kernel, grid=(1,), out_shape=(jax.ShapeDtypeStruct(sha...]
    concatenate x6 -> x3, other arithmetic: 5.2 us -> 0.02 us  [the longest x2 0.01 us: line_of_four(): jnp.concatenate([part(designs[2], p), part(designs[3], p)], axis=1)]
    squeeze x2 -> x0, other arithmetic: 4.64 us -> none  [units(): late[side]]
    add x4 -> x0, other arithmetic: 3.56 us -> none  [the longest x2 3.29 us: line_of_four(): sums = units(0) + got.astype(jnp.float32)]
    another operation x3 -> x1, other arithmetic: 2.82 us -> 0.08 us  [line_of_four(): jnp.stack([lax.rem(s, 2), jnp.logical_or(z == 1, z == 2).astype(jnp.int32...]
  transfers between devices with their start and end apart: 19 -> 21, of which waited for: 9 -> 7; matrix products, arithmetic and copies ran while one was open for 15% -> 3% of each run, Pallas kernels for 23% -> 19%
where the time goes in v3:
time: 135 us
  waiting for transfers between devices  66 us (49%)
  starting transfers between devices  31.2 us (23%)
  Pallas kernels  28.5 us (21%)
  local copies, waits for them, and re-layouts  5.03 us (4%)
  other arithmetic  2.27 us (2%)
  matrix products  1.78 us (1%)
    ppermute x3, waiting for transfers between devices, line_of_four(): lax.ppermute(mine, 'samp', [(i, i ^ j) for i in range(4)])  51.2 us
    pallas_call x4, Pallas kernels, block_sums(): pl.pallas_call(kernel, out_shape=out, in_specs=[pl.BlockSpec(memory_space...  17.2 us
    ppermute x6, waiting for transfers between devices, line_of_four(): lax.ppermute(sent[d - 1], 'snp', [(i, i ^ 2 * d) for i in range(8)])  14.7 us
    ppermute x6, starting transfers between devices, line_of_four(): lax.ppermute(sent[d - 1], 'snp', [(i, i ^ 2 * d) for i in range(8)])  8.99 us
    ppermute x3, starting transfers between devices, line_of_four(): lax.ppermute(mine, 'samp', [(i, i ^ j) for i in range(4)])  6.5 us
    ppermute x2, starting transfers between devices, line_of_four(): far = [lax.ppermute(c, 'samp', [(1, 2), (2, 1)]) for c in near]  5.84 us
    pallas_call x2, Pallas kernels, add_cores(): pl.pallas_call(add_kernel, grid=(1,), out_shape=(jax.ShapeDtypeStruct(sha...  5.33 us
    ppermute x2, starting transfers between devices, line_of_four(): out = [lax.ppermute(c, 'samp', [(1, 0), (2, 3)]) for c in three]  5.27 us
  transfers between devices with their start and end apart: 21, of which 7 were waited for; matrix products, arithmetic and copies ran while one was open for 3% of the time, Pallas kernels for 19%

profile of v3, /device:TPU:16, one launch (start us, length us, event | category | flops | bytes accessed | tf_op | source)
XLA Modules:
  0.0 135.0 jit_solution(4738601450114603083)
XLA Ops:
  0.0 1.8 %fusion.3 = (f32[1024,128]{1,0:T(8,128)S(1)}, f32[1024,128]{1,0:T(8,128)S(1)}, f32[1024,128]{1,0:T(8,128)S(1)}, f32[1024,128]{1,0:T(8,128)S(1)}) fusion(f32[1024,512]{1,0:T(8,128)} %own_ref.1), kind=kLoop, calls=%fused_computation.27 | loop fusion | bytes 4194304 | tf_op jit(solution)/shard_map/slice | solution.py:257
  4.5 1.8 %fusion = f32[24,1024]{1,0:T(8,128)S(1)} fusion(f32[1024,512]{1,0:T(8,128)S(1)} %copy-done, f32[20,512]{1,0:T(8,128)S(1)} %copy-done.3), kind=kOutput, calls=%fused_computation.1 | convolution fusion | flops 152068096 | bytes 2236416 | tf_op jit(solution)/shard_map/dot_general | solution.py:268
  6.3 3.0 %collective-permute-start.2 = (f32[24,1536]{1,0:T(8,128)S(1)}, f32[24,1536]{1,0:T(8,128)S(1)}, u32[]{:S(2)}, u32[]{:S(2)}) collective-permute-start(f32[24,1536]{1,0:T(8,128)S(1)} %pad_maximum_fusion.2.mine_ref), channel_id=1, source_target_pairs={{0,3},{1,2},{2,1},{3,0},{4,7},{5,6},{6,5},{7,4},{8,11},{9,10},{10,... | collective-permute-start | bytes 442376 | tf_op jit(solution)/shard_map/ppermute | solution.py:271
  10.4 1.8 %collective-permute-start.3 = (bf16[1024,256]{1,0:T(8,128)(2,1)}, bf16[1024,256]{1,0:T(8,128)(2,1)}, u32[]{:S(2)}, u32[]{:S(2)}) collective-permute-start(bf16[1024,256]{1,0:T(8,128)(2,1)} %select_convert_fusion.1), channel_id=1, source_target_pairs={{0,1},{1,0},{2,3},{3,2},{4,5},{5,4},{6,7},{7,6},{8,9},{9,8},{10,11... | collective-permute-start | bytes 1572872 | tf_op jit(solution)/shard_map/ppermute | solution.py:260
  12.2 34.5 %collective-permute-done.2.c_ref = f32[24,1536]{1,0:T(8,128)S(1)} collective-permute-done((f32[24,1536]{1,0:T(8,128)S(1)}, f32[24,1536]{1,0:T(8,128)S(1)}, u32[]{:S(2)}, u32[]{:S(2)}) %collective-permute-start.2) | collective-permute-done | bytes 147488 | tf_op jit(solution)/shard_map/ppermute | solution.py:271
  46.7 14.4 %collective-permute-done.1.b_ref = f32[24,1536]{1,0:T(8,128)S(1)} collective-permute-done((f32[24,1536]{1,0:T(8,128)S(1)}, f32[24,1536]{1,0:T(8,128)S(1)}, u32[]{:S(2)}, u32[]{:S(2)}) %collective-permute-start.1) | collective-permute-done | bytes 147488 | tf_op jit(solution)/shard_map/ppermute | solution.py:271
  61.8 3.5 %collective-permute-start = (f32[24,1536]{1,0:T(8,128)S(1)}, f32[24,1536]{1,0:T(8,128)}, u32[]{:S(2)}, u32[]{:S(2)}) collective-permute-start(f32[24,1536]{1,0:T(8,128)S(1)} %pad_maximum_fusion.2.mine_ref), channel_id=1, source_target_pairs={{0,1},{1,0},{2,3},{3,2},{4,5},{5,4},{6,7},{7,6},{8,9},{9,8},{10,11... | collective-permute-start | bytes 442376 | tf_op jit(solution)/shard_map/ppermute | solution.py:271
  66.1 2.3 %collective-permute-done.a_ref = f32[24,1536]{1,0:T(8,128)} collective-permute-done((f32[24,1536]{1,0:T(8,128)S(1)}, f32[24,1536]{1,0:T(8,128)}, u32[]{:S(2)}, u32[]{:S(2)}) %collective-permute-start) | collective-permute-done | bytes 147488 | tf_op jit(solution)/shard_map/ppermute | solution.py:271
  69.3 3.9 %collective-permute-start.16 = (bf16[1024,256]{1,0:T(8,128)(2,1)S(1)}, bf16[1024,256]{1,0:T(8,128)(2,1)S(1)}, u32[]{:S(2)}, u32[]{:S(2)}) collective-permute-start(bf16[1024,256]{1,0:T(8,128)(2,1)S(1)} %collective-permute-done.15.refs_2_), channel_id=1, source_target_pairs={{1,0},{2,3},{5,4},{6,7},{9,8},{10,11},{13,12},{14,15},{17,16},{18,... | collective-permute-start | bytes 1572872 | tf_op jit(solution)/shard_map/ppermute | solution.py:263
  73.2 2.4 %collective-permute-start.14 = (bf16[1024,256]{1,0:T(8,128)(2,1)}, bf16[1024,256]{1,0:T(8,128)(2,1)S(1)}, u32[]{:S(2)}, u32[]{:S(2)}) collective-permute-start(bf16[1024,256]{1,0:T(8,128)(2,1)} %collective-permute-done.4.refs_1_), channel_id=1, source_target_pairs={{1,2},{2,1},{5,6},{6,5},{9,10},{10,9},{13,14},{14,13},{17,18},{18,... | collective-permute-start | bytes 1572872 | tf_op jit(solution)/shard_map/ppermute | solution.py:262
  77.0 3.5 %collective-permute-start.5 = (bf16[1024,256]{1,0:T(8,128)(2,1)}, bf16[1024,256]{1,0:T(8,128)(2,1)S(1)}, u32[]{:S(2)}, u32[]{:S(2)}) collective-permute-start(bf16[1024,256]{1,0:T(8,128)(2,1)} %collective-permute-done.3.refs_0_), channel_id=1, source_target_pairs={{1,2},{2,1},{5,6},{6,5},{9,10},{10,9},{13,14},{14,13},{17,18},{18,... | collective-permute-start | bytes 1572872 | tf_op jit(solution)/shard_map/ppermute | solution.py:262
  81.4 3.8 %shard_map.28.coef_ref = f32[32,1024]{1,0:T(8,128)S(1)} custom-call(f32[24,1536]{1,0:T(8,128)S(1)} %pad_maximum_fusion.2.mine_ref, f32[24,1536]{1,0:T(8,128)} %collective-permute-done.a_ref, f32[24,1536]{1,0:T(8,128)S(1)} %copy-done.2, f32[24,1536]{1,0:T(8,128)S(1)} %collective-permute-done.2.c_ref), custom_call_target="tpu_custom_call" | custom-call | tf_op jit(solution)/shard_map/pallas_call | solution.py:90
  85.2 3.9 %shard_map.29 = (bf16[2,1024,512]{2,1,0:T(8,128)(2,1)S(1)}, f32[2,2,128,512]{3,2,1,0:T(8,128)S(1)}, bf16[2,2,128,512]{3,2,1,0:T(8,128)(2,1)S(1)}) custom-call(s32[3]{0:T(128)S(1)} %pad_add_fusion.place_ref, f32[1024,512]{1,0:T(8,128)S(1)} %copy-done, f32[32,1024]{1,0:T(8,128)S(1)} %shard_map.28.coef_ref, f32[32,512]{1,0:T(8,128)S(1)} %pad.19.design_ref), custom_call_target="tpu_custom_call" | custom-call | tf_op jit(solution)/shard_map/pallas_call | solution.py:174
  89.2 4.8 %shard_map.30 = (f32[2,2,128,512]{3,2,1,0:T(8,128)S(1)}, bf16[2,2,128,512]{3,2,1,0:T(8,128)(2,1)S(1)}) custom-call(s32[3]{0:T(128)S(1)} %pad_add_fusion.place_ref, bf16[2,1024,512]{2,1,0:T(8,128)(2,1)S(1)} %get-tuple-element.23.terms_ref, f32[32,1024]{1,0:T(8,128)S(1)} %shard_map.28.coef_ref, f32[32,512]{1,0:T(8,128)S(1)} %pad_maximum_fusion.3.design_ref, ...), custom_call_target="tpu_custom_call" | custom-call | tf_op jit(solution)/shard_map/pallas_call | solution.py:174
  94.6 4.2 %shard_map.33 = (f32[2,2,128,512]{3,2,1,0:T(8,128)S(1)}, bf16[2,2,128,512]{3,2,1,0:T(8,128)(2,1)S(1)}) custom-call(s32[3]{0:T(128)S(1)} %pad_add_fusion.place_ref, bf16[2,1024,512]{2,1,0:T(8,128)(2,1)S(1)} %get-tuple-element.23.terms_ref, f32[32,1024]{1,0:T(8,128)S(1)} %shard_map.28.coef_ref, f32[32,512]{1,0:T(8,128)S(1)} %pad_maximum_fusion.5.design_ref, ...), custom_call_target="tpu_custom_call" | custom-call | tf_op jit(solution)/shard_map/pallas_call | solution.py:174
  98.9 4.3 %shard_map.31 = (f32[2,2,128,512]{3,2,1,0:T(8,128)S(1)}, bf16[2,2,128,512]{3,2,1,0:T(8,128)(2,1)S(1)}) custom-call(s32[3]{0:T(128)S(1)} %pad_add_fusion.place_ref, bf16[2,1024,512]{2,1,0:T(8,128)(2,1)S(1)} %get-tuple-element.23.terms_ref, f32[32,1024]{1,0:T(8,128)S(1)} %shard_map.28.coef_ref, f32[32,512]{1,0:T(8,128)S(1)} %pad_maximum_fusion.4.design_ref, ...), custom_call_target="tpu_custom_call" | custom-call | tf_op jit(solution)/shard_map/pallas_call | solution.py:174
  103.8 2.7 %shard_map.34 = (f32[2,128,512]{2,1,0:T(8,128)S(1)}, bf16[2,128,512]{2,1,0:T(8,128)(2,1)S(1)}, bf16[2,128,512]{2,1,0:T(8,128)(2,1)S(1)}, bf16[2,128,512]{2,1,0:T(8,128)(2,1)S(1)}) custom-call(s32[3]{0:T(128)S(1)} %pad_add_fusion.place_ref, f32[2,2,128,512]{3,2,1,0:T(8,128)S(1)} %get-tuple-element.22.own_ref, ...), custom_call_target="tpu_custom_call" | custom-call | tf_op jit(solution)/shard_map/pallas_call | solution.py:200
  110.0 2.7 %shard_map.32 = (f32[2,128,512]{2,1,0:T(8,128)S(1)}, bf16[2,128,512]{2,1,0:T(8,128)(2,1)S(1)}, bf16[2,128,512]{2,1,0:T(8,128)(2,1)S(1)}, bf16[2,128,512]{2,1,0:T(8,128)(2,1)S(1)}) custom-call(s32[3]{0:T(128)S(1)} %pad_add_fusion.place_ref, f32[2,2,128,512]{3,2,1,0:T(8,128)S(1)} %get-tuple-element.22.own_ref, ...), custom_call_target="tpu_custom_call" | custom-call | tf_op jit(solution)/shard_map/pallas_call | solution.py:200
  112.7 1.6 %collective-permute-start.11 = (bf16[2,128,512]{2,1,0:T(8,128)(2,1)S(1)}, bf16[2,128,512]{2,1,0:T(8,128)(2,1)S(1)}, u32[]{:S(2)}, u32[]{:S(2)}) collective-permute-start(bf16[2,128,512]{2,1,0:T(8,128)(2,1)S(1)} %get-tuple-element.30), channel_id=1, source_target_pairs={{0,8},{4,12},{8,0},{12,4},{16,24},{20,28},{24,16},{28,20},{1,9},{5... | collective-permute-start | bytes 786440 | tf_op jit(solution)/shard_map/ppermute | solution.py:287
  115.7 2.4 %collective-permute-start.13 = (bf16[2,128,512]{2,1,0:T(8,128)(2,1)S(1)}, bf16[2,128,512]{2,1,0:T(8,128)(2,1)S(1)}, u32[]{:S(2)}, u32[]{:S(2)}) collective-permute-start(bf16[2,128,512]{2,1,0:T(8,128)(2,1)S(1)} %get-tuple-element.32), channel_id=1, source_target_pairs={{0,24},{4,28},{8,16},{12,20},{16,8},{20,12},{24,0},{28,4},{1,25},{... | collective-permute-start | bytes 786440 | tf_op jit(solution)/shard_map/ppermute | solution.py:287
  118.1 4.0 %collective-permute-done.19.refs_6_ = bf16[2,128,512]{2,1,0:T(8,128)(2,1)S(1)} collective-permute-done((bf16[2,128,512]{2,1,0:T(8,128)(2,1)S(1)}, bf16[2,128,512]{2,1,0:T(8,128)(2,1)S(1)}, u32[]{:S(2)}, u32[]{:S(2)}) %collective-permute-start.19) | collective-permute-done | bytes 262176 | tf_op jit(solution)/shard_map/ppermute | solution.py:287
  122.3 4.7 %collective-permute-done.11.refs_1_ = bf16[2,128,512]{2,1,0:T(8,128)(2,1)S(1)} collective-permute-done((bf16[2,128,512]{2,1,0:T(8,128)(2,1)S(1)}, bf16[2,128,512]{2,1,0:T(8,128)(2,1)S(1)}, u32[]{:S(2)}, u32[]{:S(2)}) %collective-permute-start.11) | collective-permute-done | bytes 262176 | tf_op jit(solution)/shard_map/ppermute | solution.py:287
  126.9 5.9 %collective-permute-done.12.refs_2_ = bf16[2,128,512]{2,1,0:T(8,128)(2,1)S(1)} collective-permute-done((bf16[2,128,512]{2,1,0:T(8,128)(2,1)S(1)}, bf16[2,128,512]{2,1,0:T(8,128)(2,1)S(1)}, u32[]{:S(2)}, u32[]{:S(2)}) %collective-permute-start.12) | collective-permute-done | bytes 262176 | tf_op jit(solution)/shard_map/ppermute | solution.py:287
  132.8 2.2 %shard_map.35 = f32[256,512]{1,0:T(8,128)} custom-call(f32[2,128,512]{2,1,0:T(8,128)S(1)} %get-tuple-element.29.refs_0_, bf16[2,128,512]{2,1,0:T(8,128)(2,1)S(1)} %collective-permute-done.11.refs_1_, bf16[2,128,512]{2,1,0:T(8,128)(2,1)S(1)} %collective-permute-done.12.refs_2_, bf16[2,128,512]{2,1,0:T(8,128)(2,1)S(1)} %collective-permute-done.13.refs_3_, ...), custom_call_target="tpu_custom_call" | custom-call | tf_op jit(solution)/shard_map/pallas_call | solution.py:224
  (51 shorter events, 14.9 us)
Async XLA Ops:
  0.0 4.5 %copy-start = (f32[1024,512]{1,0:T(8,128)S(1)}, f32[1024,512]{1,0:T(8,128)}, u32[]{:S(2)}) copy-start(f32[1024,512]{1,0:T(8,128)} %own_ref.1) | copy-start | bytes 6291460
  0.0 4.5 %copy-start.3 = (f32[20,512]{1,0:T(8,128)S(1)}, f32[20,512]{1,0:T(8,128)}, u32[]{:S(2)}) copy-start(f32[20,512]{1,0:T(8,128)} %param.3) | copy-start | bytes 122884
  2.9 66.4 %collective-permute-start.15 = (bf16[1024,256]{1,0:T(8,128)(2,1)}, bf16[1024,256]{1,0:T(8,128)(2,1)S(1)}, u32[]{:S(2)}, u32[]{:S(2)}) collective-permute-start(bf16[1024,256]{1,0:T(8,128)(2,1)} %select_convert_fusion), channel_id=1, source_target_pairs={{0,3},{1,2},{2,1},{3,0},{4,7},{5,6},{6,5},{7,4},{8,11},{9,10},{10,... | collective-permute-start | bytes 1572872 | tf_op jit(solution)/shard_map/ppermute | solution.py:261
  3.4 69.9 %collective-permute-start.4 = (bf16[1024,256]{1,0:T(8,128)(2,1)}, bf16[1024,256]{1,0:T(8,128)(2,1)}, u32[]{:S(2)}, u32[]{:S(2)}) collective-permute-start(bf16[1024,256]{1,0:T(8,128)(2,1)} %select_convert_fusion), channel_id=1, source_target_pairs={{0,1},{1,0},{2,3},{3,2},{4,5},{5,4},{6,7},{7,6},{8,9},{9,8},{10,11... | collective-permute-start | bytes 1572872 | tf_op jit(solution)/shard_map/ppermute | solution.py:260
  6.3 40.4 %collective-permute-start.2 = (f32[24,1536]{1,0:T(8,128)S(1)}, f32[24,1536]{1,0:T(8,128)S(1)}, u32[]{:S(2)}, u32[]{:S(2)}) collective-permute-start(f32[24,1536]{1,0:T(8,128)S(1)} %pad_maximum_fusion.2.mine_ref), channel_id=1, source_target_pairs={{0,3},{1,2},{2,1},{3,0},{4,7},{5,6},{6,5},{7,4},{8,11},{9,10},{10,... | collective-permute-start | bytes 442376 | tf_op jit(solution)/shard_map/ppermute | solution.py:271
  10.4 65.2 %collective-permute-start.6 = (bf16[1024,256]{1,0:T(8,128)(2,1)}, bf16[1024,256]{1,0:T(8,128)(2,1)S(1)}, u32[]{:S(2)}, u32[]{:S(2)}) collective-permute-start(bf16[1024,256]{1,0:T(8,128)(2,1)} %select_convert_fusion.1), channel_id=1, source_target_pairs={{0,3},{1,2},{2,1},{3,0},{4,7},{5,6},{6,5},{7,4},{8,11},{9,10},{10,... | collective-permute-start | bytes 1572872 | tf_op jit(solution)/shard_map/ppermute | solution.py:261
  10.4 66.6 %collective-permute-start.3 = (bf16[1024,256]{1,0:T(8,128)(2,1)}, bf16[1024,256]{1,0:T(8,128)(2,1)}, u32[]{:S(2)}, u32[]{:S(2)}) collective-permute-start(bf16[1024,256]{1,0:T(8,128)(2,1)} %select_convert_fusion.1), channel_id=1, source_target_pairs={{0,1},{1,0},{2,3},{3,2},{4,5},{5,4},{6,7},{7,6},{8,9},{9,8},{10,11... | collective-permute-start | bytes 1572872 | tf_op jit(solution)/shard_map/ppermute | solution.py:260
  46.7 14.4 %collective-permute-start.1 = (f32[24,1536]{1,0:T(8,128)S(1)}, f32[24,1536]{1,0:T(8,128)S(1)}, u32[]{:S(2)}, u32[]{:S(2)}) collective-permute-start(f32[24,1536]{1,0:T(8,128)S(1)} %pad_maximum_fusion.2.mine_ref), channel_id=1, source_target_pairs={{0,2},{1,3},{2,0},{3,1},{4,6},{5,7},{6,4},{7,5},{8,10},{9,11},{10,... | collective-permute-start | bytes 442376 | tf_op jit(solution)/shard_map/ppermute | solution.py:271
  61.8 6.7 %collective-permute-start = (f32[24,1536]{1,0:T(8,128)S(1)}, f32[24,1536]{1,0:T(8,128)}, u32[]{:S(2)}, u32[]{:S(2)}) collective-permute-start(f32[24,1536]{1,0:T(8,128)S(1)} %pad_maximum_fusion.2.mine_ref), channel_id=1, source_target_pairs={{0,1},{1,0},{2,3},{3,2},{4,5},{5,4},{6,7},{7,6},{8,9},{9,8},{10,11... | collective-permute-start | bytes 442376 | tf_op jit(solution)/shard_map/ppermute | solution.py:271
  69.3 24.7 %collective-permute-start.16 = (bf16[1024,256]{1,0:T(8,128)(2,1)S(1)}, bf16[1024,256]{1,0:T(8,128)(2,1)S(1)}, u32[]{:S(2)}, u32[]{:S(2)}) collective-permute-start(bf16[1024,256]{1,0:T(8,128)(2,1)S(1)} %collective-permute-done.15.refs_2_), channel_id=1, source_target_pairs={{1,0},{2,3},{5,4},{6,7},{9,8},{10,11},{13,12},{14,15},{17,16},{18,... | collective-permute-start | bytes 1572872 | tf_op jit(solution)/shard_map/ppermute | solution.py:263
  73.2 21.3 %collective-permute-start.14 = (bf16[1024,256]{1,0:T(8,128)(2,1)}, bf16[1024,256]{1,0:T(8,128)(2,1)S(1)}, u32[]{:S(2)}, u32[]{:S(2)}) collective-permute-start(bf16[1024,256]{1,0:T(8,128)(2,1)} %collective-permute-done.4.refs_1_), channel_id=1, source_target_pairs={{1,2},{2,1},{5,6},{6,5},{9,10},{10,9},{13,14},{14,13},{17,18},{18,... | collective-permute-start | bytes 1572872 | tf_op jit(solution)/shard_map/ppermute | solution.py:262
  75.7 23.2 %collective-permute-start.7 = (bf16[1024,256]{1,0:T(8,128)(2,1)S(1)}, bf16[1024,256]{1,0:T(8,128)(2,1)S(1)}, u32[]{:S(2)}, u32[]{:S(2)}) collective-permute-start(bf16[1024,256]{1,0:T(8,128)(2,1)S(1)} %collective-permute-done.6.refs_2_), channel_id=1, source_target_pairs={{1,0},{2,3},{5,4},{6,7},{9,8},{10,11},{13,12},{14,15},{17,16},{18,... | collective-permute-start | bytes 1572872 | tf_op jit(solution)/shard_map/ppermute | solution.py:263
  77.0 21.9 %collective-permute-start.5 = (bf16[1024,256]{1,0:T(8,128)(2,1)}, bf16[1024,256]{1,0:T(8,128)(2,1)S(1)}, u32[]{:S(2)}, u32[]{:S(2)}) collective-permute-start(bf16[1024,256]{1,0:T(8,128)(2,1)} %collective-permute-done.3.refs_0_), channel_id=1, source_target_pairs={{1,2},{2,1},{5,6},{6,5},{9,10},{10,9},{13,14},{14,13},{17,18},{18,... | collective-permute-start | bytes 1572872 | tf_op jit(solution)/shard_map/ppermute | solution.py:262
  80.5 0.9 copy-start.2
  89.1 14.7 %collective-permute-start.8 = (bf16[2,2,128,512]{3,2,1,0:T(8,128)(2,1)S(1)}, bf16[2,2,128,512]{3,2,1,0:T(8,128)(2,1)S(1)}, u32[]{:S(2)}, u32[]{:S(2)}) collective-permute-start(bf16[2,2,128,512]{3,2,1,0:T(8,128)(2,1)S(1)} %get-tuple-element.26), channel_id=1, source_target_pairs={{0,4},{4,0},{8,12},{12,8},{16,20},{20,16},{24,28},{28,24},{1,5},{5... | collective-permute-start | bytes 1572872 | tf_op jit(solution)/shard_map/ppermute | solution.py:278
  94.0 9.7 %collective-permute-start.9 = (bf16[2,2,128,512]{3,2,1,0:T(8,128)(2,1)S(1)}, bf16[2,2,128,512]{3,2,1,0:T(8,128)(2,1)S(1)}, u32[]{:S(2)}, u32[]{:S(2)}) collective-permute-start(bf16[2,2,128,512]{3,2,1,0:T(8,128)(2,1)S(1)} %get-tuple-element.27), channel_id=1, source_target_pairs={{0,4},{4,0},{8,12},{12,8},{16,20},{20,16},{24,28},{28,24},{1,5},{5... | collective-permute-start | bytes 1572872 | tf_op jit(solution)/shard_map/ppermute | solution.py:278
  98.7 5.0 %collective-permute-start.17 = (bf16[2,2,128,512]{3,2,1,0:T(8,128)(2,1)S(1)}, bf16[2,2,128,512]{3,2,1,0:T(8,128)(2,1)S(1)}, u32[]{:S(2)}, u32[]{:S(2)}) collective-permute-start(bf16[2,2,128,512]{3,2,1,0:T(8,128)(2,1)S(1)} %get-tuple-element.34), channel_id=1, source_target_pairs={{0,4},{4,0},{8,12},{12,8},{16,20},{20,16},{24,28},{28,24},{1,5},{5... | collective-permute-start | bytes 1572872 | tf_op jit(solution)/shard_map/ppermute | solution.py:283
  103.2 6.8 %collective-permute-start.10 = (bf16[2,2,128,512]{3,2,1,0:T(8,128)(2,1)S(1)}, bf16[2,2,128,512]{3,2,1,0:T(8,128)(2,1)S(1)}, u32[]{:S(2)}, u32[]{:S(2)}) collective-permute-start(bf16[2,2,128,512]{3,2,1,0:T(8,128)(2,1)S(1)} %get-tuple-element.28), channel_id=1, source_target_pairs={{0,4},{4,0},{8,12},{12,8},{16,20},{20,16},{24,28},{28,24},{1,5},{5... | collective-permute-start | bytes 1572872 | tf_op jit(solution)/shard_map/ppermute | solution.py:283
  106.4 9.3 %collective-permute-start.18 = (bf16[2,128,512]{2,1,0:T(8,128)(2,1)S(1)}, bf16[2,128,512]{2,1,0:T(8,128)(2,1)S(1)}, u32[]{:S(2)}, u32[]{:S(2)}) collective-permute-start(bf16[2,128,512]{2,1,0:T(8,128)(2,1)S(1)} %get-tuple-element.36), channel_id=1, source_target_pairs={{0,8},{4,12},{8,0},{12,4},{16,24},{20,28},{24,16},{28,20},{1,9},{5... | collective-permute-start | bytes 786440 | tf_op jit(solution)/shard_map/ppermute | solution.py:287
  108.0 14.1 %collective-permute-start.19 = (bf16[2,128,512]{2,1,0:T(8,128)(2,1)S(1)}, bf16[2,128,512]{2,1,0:T(8,128)(2,1)S(1)}, u32[]{:S(2)}, u32[]{:S(2)}) collective-permute-start(bf16[2,128,512]{2,1,0:T(8,128)(2,1)S(1)} %get-tuple-element.37), channel_id=1, source_target_pairs={{0,16},{4,20},{8,24},{12,28},{16,0},{20,4},{24,8},{28,12},{1,17},{... | collective-permute-start | bytes 786440 | tf_op jit(solution)/shard_map/ppermute | solution.py:287
  109.5 12.8 %collective-permute-start.20 = (bf16[2,128,512]{2,1,0:T(8,128)(2,1)S(1)}, bf16[2,128,512]{2,1,0:T(8,128)(2,1)S(1)}, u32[]{:S(2)}, u32[]{:S(2)}) collective-permute-start(bf16[2,128,512]{2,1,0:T(8,128)(2,1)S(1)} %get-tuple-element.38), channel_id=1, source_target_pairs={{0,24},{4,28},{8,16},{12,20},{16,8},{20,12},{24,0},{28,4},{1,25},{... | collective-permute-start | bytes 786440 | tf_op jit(solution)/shard_map/ppermute | solution.py:287
  112.7 14.3 %collective-permute-start.11 = (bf16[2,128,512]{2,1,0:T(8,128)(2,1)S(1)}, bf16[2,128,512]{2,1,0:T(8,128)(2,1)S(1)}, u32[]{:S(2)}, u32[]{:S(2)}) collective-permute-start(bf16[2,128,512]{2,1,0:T(8,128)(2,1)S(1)} %get-tuple-element.30), channel_id=1, source_target_pairs={{0,8},{4,12},{8,0},{12,4},{16,24},{20,28},{24,16},{28,20},{1,9},{5... | collective-permute-start | bytes 786440 | tf_op jit(solution)/shard_map/ppermute | solution.py:287
  114.2 18.6 %collective-permute-start.12 = (bf16[2,128,512]{2,1,0:T(8,128)(2,1)S(1)}, bf16[2,128,512]{2,1,0:T(8,128)(2,1)S(1)}, u32[]{:S(2)}, u32[]{:S(2)}) collective-permute-start(bf16[2,128,512]{2,1,0:T(8,128)(2,1)S(1)} %get-tuple-element.31), channel_id=1, source_target_pairs={{0,16},{4,20},{8,24},{12,28},{16,0},{20,4},{24,8},{28,12},{1,17},{... | collective-permute-start | bytes 786440 | tf_op jit(solution)/shard_map/ppermute | solution.py:287
  115.7 17.1 %collective-permute-start.13 = (bf16[2,128,512]{2,1,0:T(8,128)(2,1)S(1)}, bf16[2,128,512]{2,1,0:T(8,128)(2,1)S(1)}, u32[]{:S(2)}, u32[]{:S(2)}) collective-permute-start(bf16[2,128,512]{2,1,0:T(8,128)(2,1)S(1)} %get-tuple-element.32), channel_id=1, source_target_pairs={{0,24},{4,28},{8,16},{12,20},{16,8},{20,12},{24,0},{28,4},{1,25},{... | collective-permute-start | bytes 786440 | tf_op jit(solution)/shard_map/ppermute | solution.py:287
  (1 other events, 0.7 us)

commit v4 on v3

--- a/solution.py
+++ b/solution.py
@@ -93,7 +93,7 @@
         in_specs=[vmem] * 4,
         out_specs=vmem,
         compiler_params=pltpu.CompilerParams(vmem_limit_bytes=VMEM_BYTES),
-        cost_estimate=FREE,
+        cost_estimate=pl.CostEstimate(flops=2 * 10**10, bytes_accessed=0, transcendentals=0),
     )(*theirs)
 
 
@@ -256,18 +256,21 @@
         a, b = p * quarter, p * quarter + half
         return jnp.concatenate([array[:, a:a + quarter], array[:, b:b + quarter]], axis=1)
 
-    coded = [encode(part(genotypes, p)) for p in range(2)]
-    near = [lax.ppermute(c, "samp", [(i, i ^ 1) for i in range(4)]) for c in coded]
-    three = [lax.ppermute(c, "samp", [(i, i ^ 3) for i in range(4)]) for c in coded]
-    far = [lax.ppermute(c, "samp", [(1, 2), (2, 1)]) for c in near]
-    out = [lax.ppermute(c, "samp", [(1, 0), (2, 3)]) for c in three]
-
     design = jnp.concatenate([jnp.ones((1, width), jnp.float32), pcs], axis=0)
     design = jnp.pad(design, ((0, -DESIGN_ROWS % 8), (0, 0)))
     dosage = jnp.where(genotypes >= 0.0, genotypes, 0.0)
     cross_part = lax.dot_general(design, dosage, (((1,), (1,)), ((), ())), precision=HIGH)
     snps = cross_part.shape[1]
     mine = jnp.concatenate([cross_part, design], axis=1)
+    middle = [(1, 2), (2, 1)]
+    coded = [encode(part(genotypes, p)) for p in range(2)]
+    coded = [after(c, mine) for c in coded]
+    near = [lax.ppermute(c, "samp", [(i, i ^ 1) for i in range(4)]) for c in coded]
+    across = [lax.ppermute(c, "samp", middle) for c in coded]
+    end = [lax.ppermute(c, "samp", [(0, 3), (3, 0)]) for c in coded]
+    far = [lax.ppermute(c, "samp", middle) for c in near]
+    out = [lax.ppermute(c, "samp", [(1, 0), (2, 3)]) for c in across]
+
     theirs = [mine] + [lax.ppermute(mine, "samp", [(i, i ^ j) for i in range(4)]) for j in range(1, 4)]
     coef = coefficients(theirs, snps)
     designs = [padded(t[:, snps:]) for t in theirs]
@@ -279,7 +282,7 @@
     parts = []
     for p in range(2):
         late_design = jnp.concatenate([part(designs[2], p), part(designs[3], p)], axis=1)
-        keep, give = block_sums(place, coef, late_design, terms=terms, coded=(far[p], out[p], three[p]), sources=((0, 1), (2,)))
+        keep, give = block_sums(place, coef, late_design, terms=terms, coded=(far[p], out[p], across[p], end[p]), sources=((0, 1), (2, 3)))
         got = lax.ppermute(give, "snp", other_core)
         mine, *sent = add_cores(place, p, keep_own, keep_near, keep, got_own, got_near, got)
         parts.append(mine)

time: 135 us -> 125 us (0.926)
  waiting for transfers between devices: 66 us -> 56.1 us
  local copies, waits for them, and re-layouts: 5.03 us -> 1.79 us
  matrix products: 1.78 us -> 3.4 us
    ppermute x3, waiting for transfers between devices: 51.2 us -> 3.66 us  [line_of_four(): lax.ppermute(mine, 'samp', [(i, i ^ j) for i in range(4)])]
    ppermute x2, waiting for transfers between devices: 0.01 us -> 22.4 us  [line_of_four(): lax.ppermute(c, 'samp', [(i, i ^ 1) for i in range(4)])]
    ppermute x6 -> x8, waiting for transfers between devices: 0.02 us -> 14.8 us  [the longest x2 7.9 us: line_of_four(): across = [lax.ppermute(c, 'samp', middle) for c in coded]]
    ppermute x2, starting transfers between devices: 2.91 us -> 6.04 us  [line_of_four(): lax.ppermute(c, 'samp', [(i, i ^ 1) for i in range(4)])]
    ppermute x3, starting transfers between devices: 6.5 us -> 3.55 us  [line_of_four(): lax.ppermute(mine, 'samp', [(i, i ^ j) for i in range(4)])]
    slice x4, local copies, waits for them, and re-layouts: 1.85 us -> 0.16 us  [part(): array[:, a:a + quarter]]
    dot_general x1, matrix products: 1.78 us -> 3.4 us  [line_of_four(): lax.dot_general(design, dosage, (((1,), (1,)), ((), ())), precision=HIGH)]
    unnamed x8 -> x4, local copies, waits for them, and re-layouts: 1.56 us -> 0.01 us
  transfers between devices with their start and end apart: 21 -> 23, of which waited for: 7 -> 11; matrix products, arithmetic and copies ran while one was open for 3% -> 3% of each run, Pallas kernels for 19% -> 21%
where the time goes in v4:
time: 125 us
  waiting for transfers between devices  56.1 us (45%)
  starting transfers between devices  32.1 us (26%)
  Pallas kernels  28.3 us (23%)
  matrix products  3.4 us (3%)
  other arithmetic  2.56 us (2%)
  local copies, waits for them, and re-layouts  1.79 us (1%)
    ppermute x2, waiting for transfers between devices, line_of_four(): lax.ppermute(c, 'samp', [(i, i ^ 1) for i in range(4)])  22.4 us
    pallas_call x4, Pallas kernels, block_sums(): pl.pallas_call(kernel, out_shape=out, in_specs=[pl.BlockSpec(memory_space...  16.8 us
    ppermute x6, waiting for transfers between devices, line_of_four(): lax.ppermute(sent[d - 1], 'snp', [(i, i ^ 2 * d) for i in range(8)])  15.2 us
    ppermute x6, starting transfers between devices, line_of_four(): lax.ppermute(sent[d - 1], 'snp', [(i, i ^ 2 * d) for i in range(8)])  8.85 us
    ppermute x2, waiting for transfers between devices, line_of_four(): across = [lax.ppermute(c, 'samp', middle) for c in coded]  7.9 us
    ppermute x2, waiting for transfers between devices, line_of_four(): far = [lax.ppermute(c, 'samp', middle) for c in near]  6.85 us
    ppermute x2, starting transfers between devices, line_of_four(): lax.ppermute(c, 'samp', [(i, i ^ 1) for i in range(4)])  6.04 us
    pallas_call x2, Pallas kernels, add_cores(): pl.pallas_call(add_kernel, grid=(1,), out_shape=(jax.ShapeDtypeStruct(sha...  5.51 us
  transfers between devices with their start and end apart: 23, of which 11 were waited for; matrix products, arithmetic and copies ran while one was open for 3% of the time, Pallas kernels for 21%

profile of v4, /device:TPU:16, one launch (start us, length us, event | category | flops | bytes accessed | tf_op | source)
XLA Modules:
  0.0 124.5 jit_solution(4671998711870907385)
XLA Ops:
  1.0 3.4 %fusion = f32[24,1024]{1,0:T(8,128)S(1)} fusion(f32[1024,512]{1,0:T(8,128)} %own_ref.1, f32[20,512]{1,0:T(8,128)} %param.3), kind=kOutput, calls=%fused_computation.1 | convolution fusion | flops 152068096 | bytes 2236416 | tf_op jit(solution)/shard_map/dot_general | solution.py:262
  9.6 2.5 %collective-permute-start.4 = (bf16[1024,256]{1,0:T(8,128)(2,1)}, bf16[1024,256]{1,0:T(8,128)(2,1)S(1)}, u32[]{:S(2)}, u32[]{:S(2)}) collective-permute-start(bf16[1024,256]{1,0:T(8,128)(2,1)} %get-tuple-element.27), channel_id=1, source_target_pairs={{0,1},{1,0},{2,3},{3,2},{4,5},{5,4},{6,7},{7,6},{8,9},{9,8},{10,11... | collective-permute-start | bytes 1572872 | tf_op jit(solution)/shard_map/ppermute | solution.py:268
  14.9 2.0 %collective-permute-done.1.b_ref = f32[24,1536]{1,0:T(8,128)} collective-permute-done((f32[24,1536]{1,0:T(8,128)S(1)}, f32[24,1536]{1,0:T(8,128)}, u32[]{:S(2)}, u32[]{:S(2)}) %collective-permute-start.1) | collective-permute-done | bytes 147488 | tf_op jit(solution)/shard_map/ppermute | solution.py:274
  16.9 3.6 %collective-permute-start.3 = (bf16[1024,256]{1,0:T(8,128)(2,1)}, bf16[1024,256]{1,0:T(8,128)(2,1)S(1)}, u32[]{:S(2)}, u32[]{:S(2)}) collective-permute-start(bf16[1024,256]{1,0:T(8,128)(2,1)} %get-tuple-element.26), channel_id=1, source_target_pairs={{0,1},{1,0},{2,3},{3,2},{4,5},{5,4},{6,7},{7,6},{8,9},{9,8},{10,11... | collective-permute-start | bytes 1572872 | tf_op jit(solution)/shard_map/ppermute | solution.py:268
  22.1 2.5 %collective-permute-start.6 = (bf16[1024,256]{1,0:T(8,128)(2,1)}, bf16[1024,256]{1,0:T(8,128)(2,1)S(1)}, u32[]{:S(2)}, u32[]{:S(2)}) collective-permute-start(bf16[1024,256]{1,0:T(8,128)(2,1)} %get-tuple-element.26), channel_id=1, source_target_pairs={{1,2},{2,1},{5,6},{6,5},{9,10},{10,9},{13,14},{14,13},{17,18},{18,... | collective-permute-start | bytes 1572872 | tf_op jit(solution)/shard_map/ppermute | solution.py:269
  24.7 3.8 %shard_map.28.coef_ref = f32[32,1024]{1,0:T(8,128)S(1)} custom-call(f32[24,1536]{1,0:T(8,128)S(1)} %pad_maximum_fusion.2.mine_ref, f32[24,1536]{1,0:T(8,128)S(1)} %collective-permute-done.a_ref, f32[24,1536]{1,0:T(8,128)} %collective-permute-done.1.b_ref, f32[24,1536]{1,0:T(8,128)} %collective-permute-done.2.c_ref), custom_call_target="tpu_custom_call" | custom-call | flops 20000000000 | tf_op jit(solution)/shard_map/pallas_call | solution.py:90
  30.1 9.1 %collective-permute-done.4.refs_1_ = bf16[1024,256]{1,0:T(8,128)(2,1)S(1)} collective-permute-done((bf16[1024,256]{1,0:T(8,128)(2,1)}, bf16[1024,256]{1,0:T(8,128)(2,1)S(1)}, u32[]{:S(2)}, u32[]{:S(2)}) %collective-permute-start.4) | collective-permute-done | bytes 524320 | tf_op jit(solution)/shard_map/ppermute | solution.py:268
  39.9 4.6 %collective-permute-done.16.refs_2_ = bf16[1024,256]{1,0:T(8,128)(2,1)S(1)} collective-permute-done((bf16[1024,256]{1,0:T(8,128)(2,1)}, bf16[1024,256]{1,0:T(8,128)(2,1)S(1)}, u32[]{:S(2)}, u32[]{:S(2)}) %collective-permute-start.16) | collective-permute-done | bytes 524320 | tf_op jit(solution)/shard_map/ppermute | solution.py:269
  44.5 2.5 %collective-permute-start.15 = (bf16[1024,256]{1,0:T(8,128)(2,1)S(1)}, bf16[1024,256]{1,0:T(8,128)(2,1)S(1)}, u32[]{:S(2)}, u32[]{:S(2)}) collective-permute-start(bf16[1024,256]{1,0:T(8,128)(2,1)S(1)} %collective-permute-done.4.refs_1_), channel_id=1, source_target_pairs={{1,2},{2,1},{5,6},{6,5},{9,10},{10,9},{13,14},{14,13},{17,18},{18,... | collective-permute-start | bytes 1572872 | tf_op jit(solution)/shard_map/ppermute | solution.py:271
  48.4 13.4 %collective-permute-done.3.refs_0_ = bf16[1024,256]{1,0:T(8,128)(2,1)S(1)} collective-permute-done((bf16[1024,256]{1,0:T(8,128)(2,1)}, bf16[1024,256]{1,0:T(8,128)(2,1)S(1)}, u32[]{:S(2)}, u32[]{:S(2)}) %collective-permute-start.3) | collective-permute-done | bytes 524320 | tf_op jit(solution)/shard_map/ppermute | solution.py:268
  61.8 1.9 %collective-permute-start.5 = (bf16[1024,256]{1,0:T(8,128)(2,1)S(1)}, bf16[1024,256]{1,0:T(8,128)(2,1)S(1)}, u32[]{:S(2)}, u32[]{:S(2)}) collective-permute-start(bf16[1024,256]{1,0:T(8,128)(2,1)S(1)} %collective-permute-done.3.refs_0_), channel_id=1, source_target_pairs={{1,2},{2,1},{5,6},{6,5},{9,10},{10,9},{13,14},{14,13},{17,18},{18,... | collective-permute-start | bytes 1572872 | tf_op jit(solution)/shard_map/ppermute | solution.py:271
  63.7 3.3 %collective-permute-done.6.refs_2_ = bf16[1024,256]{1,0:T(8,128)(2,1)S(1)} collective-permute-done((bf16[1024,256]{1,0:T(8,128)(2,1)}, bf16[1024,256]{1,0:T(8,128)(2,1)S(1)}, u32[]{:S(2)}, u32[]{:S(2)}) %collective-permute-start.6) | collective-permute-done | bytes 524320 | tf_op jit(solution)/shard_map/ppermute | solution.py:269
  68.3 3.9 %shard_map.29 = (bf16[2,1024,512]{2,1,0:T(8,128)(2,1)S(1)}, f32[2,2,128,512]{3,2,1,0:T(8,128)S(1)}, bf16[2,2,128,512]{3,2,1,0:T(8,128)(2,1)S(1)}) custom-call(s32[3]{0:T(128)S(1)} %pad_add_fusion.place_ref, f32[1024,512]{1,0:T(8,128)S(1)} %copy-done, f32[32,1024]{1,0:T(8,128)S(1)} %shard_map.28.coef_ref, f32[32,512]{1,0:T(8,128)S(1)} %pad.19.design_ref), custom_call_target="tpu_custom_call" | custom-call | tf_op jit(solution)/shard_map/pallas_call | solution.py:174
  72.3 4.2 %shard_map.30 = (f32[2,2,128,512]{3,2,1,0:T(8,128)S(1)}, bf16[2,2,128,512]{3,2,1,0:T(8,128)(2,1)S(1)}) custom-call(s32[3]{0:T(128)S(1)} %pad_add_fusion.place_ref, bf16[2,1024,512]{2,1,0:T(8,128)(2,1)S(1)} %get-tuple-element.25.terms_ref, f32[32,1024]{1,0:T(8,128)S(1)} %shard_map.28.coef_ref, f32[32,512]{1,0:T(8,128)S(1)} %pad_maximum_fusion.3.design_ref, ...), custom_call_target="tpu_custom_call" | custom-call | tf_op jit(solution)/shard_map/pallas_call | solution.py:174
  78.7 4.2 %shard_map.33 = (f32[2,2,128,512]{3,2,1,0:T(8,128)S(1)}, bf16[2,2,128,512]{3,2,1,0:T(8,128)(2,1)S(1)}) custom-call(s32[3]{0:T(128)S(1)} %pad_add_fusion.place_ref, bf16[2,1024,512]{2,1,0:T(8,128)(2,1)S(1)} %get-tuple-element.25.terms_ref, f32[32,1024]{1,0:T(8,128)S(1)} %shard_map.28.coef_ref, f32[32,512]{1,0:T(8,128)S(1)} %pad_maximum_fusion.5.design_ref, ...), custom_call_target="tpu_custom_call" | custom-call | tf_op jit(solution)/shard_map/pallas_call | solution.py:174
  83.1 5.1 %collective-permute-done.5.refs_0_ = bf16[1024,256]{1,0:T(8,128)(2,1)S(1)} collective-permute-done((bf16[1024,256]{1,0:T(8,128)(2,1)S(1)}, bf16[1024,256]{1,0:T(8,128)(2,1)S(1)}, u32[]{:S(2)}, u32[]{:S(2)}) %collective-permute-start.5) | collective-permute-done | bytes 524320 | tf_op jit(solution)/shard_map/ppermute | solution.py:271
  88.2 4.4 %shard_map.31 = (f32[2,2,128,512]{3,2,1,0:T(8,128)S(1)}, bf16[2,2,128,512]{3,2,1,0:T(8,128)(2,1)S(1)}) custom-call(s32[3]{0:T(128)S(1)} %pad_add_fusion.place_ref, bf16[2,1024,512]{2,1,0:T(8,128)(2,1)S(1)} %get-tuple-element.25.terms_ref, f32[32,1024]{1,0:T(8,128)S(1)} %shard_map.28.coef_ref, f32[32,512]{1,0:T(8,128)S(1)} %pad_maximum_fusion.4.design_ref, ...), custom_call_target="tpu_custom_call" | custom-call | tf_op jit(solution)/shard_map/pallas_call | solution.py:174
  92.7 2.8 %shard_map.34 = (f32[2,128,512]{2,1,0:T(8,128)S(1)}, bf16[2,128,512]{2,1,0:T(8,128)(2,1)S(1)}, bf16[2,128,512]{2,1,0:T(8,128)(2,1)S(1)}, bf16[2,128,512]{2,1,0:T(8,128)(2,1)S(1)}) custom-call(s32[3]{0:T(128)S(1)} %pad_add_fusion.place_ref, f32[2,2,128,512]{3,2,1,0:T(8,128)S(1)} %get-tuple-element.24.own_ref, ...), custom_call_target="tpu_custom_call" | custom-call | tf_op jit(solution)/shard_map/pallas_call | solution.py:200
  99.1 2.8 %shard_map.32 = (f32[2,128,512]{2,1,0:T(8,128)S(1)}, bf16[2,128,512]{2,1,0:T(8,128)(2,1)S(1)}, bf16[2,128,512]{2,1,0:T(8,128)(2,1)S(1)}, bf16[2,128,512]{2,1,0:T(8,128)(2,1)S(1)}) custom-call(s32[3]{0:T(128)S(1)} %pad_add_fusion.place_ref, f32[2,2,128,512]{3,2,1,0:T(8,128)S(1)} %get-tuple-element.24.own_ref, ...), custom_call_target="tpu_custom_call" | custom-call | tf_op jit(solution)/shard_map/pallas_call | solution.py:200
  104.9 2.2 %collective-permute-start.14 = (bf16[2,128,512]{2,1,0:T(8,128)(2,1)S(1)}, bf16[2,128,512]{2,1,0:T(8,128)(2,1)S(1)}, u32[]{:S(2)}, u32[]{:S(2)}) collective-permute-start(bf16[2,128,512]{2,1,0:T(8,128)(2,1)S(1)} %get-tuple-element.36), channel_id=1, source_target_pairs={{0,24},{4,28},{8,16},{12,20},{16,8},{20,12},{24,0},{28,4},{1,25},{... | collective-permute-start | bytes 786440 | tf_op jit(solution)/shard_map/ppermute | solution.py:290
  107.1 4.3 %collective-permute-done.21.refs_6_ = bf16[2,128,512]{2,1,0:T(8,128)(2,1)S(1)} collective-permute-done((bf16[2,128,512]{2,1,0:T(8,128)(2,1)S(1)}, bf16[2,128,512]{2,1,0:T(8,128)(2,1)S(1)}, u32[]{:S(2)}, u32[]{:S(2)}) %collective-permute-start.21) | collective-permute-done | bytes 262176 | tf_op jit(solution)/shard_map/ppermute | solution.py:290
  111.4 4.5 %collective-permute-done.12.refs_1_ = bf16[2,128,512]{2,1,0:T(8,128)(2,1)S(1)} collective-permute-done((bf16[2,128,512]{2,1,0:T(8,128)(2,1)S(1)}, bf16[2,128,512]{2,1,0:T(8,128)(2,1)S(1)}, u32[]{:S(2)}, u32[]{:S(2)}) %collective-permute-start.12) | collective-permute-done | bytes 262176 | tf_op jit(solution)/shard_map/ppermute | solution.py:290
  116.0 6.4 %collective-permute-done.13.refs_2_ = bf16[2,128,512]{2,1,0:T(8,128)(2,1)S(1)} collective-permute-done((bf16[2,128,512]{2,1,0:T(8,128)(2,1)S(1)}, bf16[2,128,512]{2,1,0:T(8,128)(2,1)S(1)}, u32[]{:S(2)}, u32[]{:S(2)}) %collective-permute-start.13) | collective-permute-done | bytes 262176 | tf_op jit(solution)/shard_map/ppermute | solution.py:290
  122.3 2.2 %shard_map.35 = f32[256,512]{1,0:T(8,128)} custom-call(f32[2,128,512]{2,1,0:T(8,128)S(1)} %get-tuple-element.33.refs_0_, bf16[2,128,512]{2,1,0:T(8,128)(2,1)S(1)} %collective-permute-done.12.refs_1_, bf16[2,128,512]{2,1,0:T(8,128)(2,1)S(1)} %collective-permute-done.13.refs_2_, bf16[2,128,512]{2,1,0:T(8,128)(2,1)S(1)} %collective-permute-done.14.refs_3_, ...), custom_call_target="tpu_custom_call" | custom-call | tf_op jit(solution)/shard_map/pallas_call | solution.py:224
  (50 shorter events, 24.7 us)
Async XLA Ops:
  4.4 9.7 %collective-permute-start = (f32[24,1536]{1,0:T(8,128)S(1)}, f32[24,1536]{1,0:T(8,128)S(1)}, u32[]{:S(2)}, u32[]{:S(2)}) collective-permute-start(f32[24,1536]{1,0:T(8,128)S(1)} %pad_maximum_fusion.2.mine_ref), channel_id=1, source_target_pairs={{0,1},{1,0},{2,3},{3,2},{4,5},{5,4},{6,7},{7,6},{8,9},{9,8},{10,11... | collective-permute-start | bytes 442376 | tf_op jit(solution)/shard_map/ppermute | solution.py:274
  6.0 10.8 %collective-permute-start.1 = (f32[24,1536]{1,0:T(8,128)S(1)}, f32[24,1536]{1,0:T(8,128)}, u32[]{:S(2)}, u32[]{:S(2)}) collective-permute-start(f32[24,1536]{1,0:T(8,128)S(1)} %pad_maximum_fusion.2.mine_ref), channel_id=1, source_target_pairs={{0,2},{1,3},{2,0},{3,1},{4,6},{5,7},{6,4},{7,5},{8,10},{9,11},{10,... | collective-permute-start | bytes 442376 | tf_op jit(solution)/shard_map/ppermute | solution.py:274
  6.4 15.8 %collective-permute-start.2 = (f32[24,1536]{1,0:T(8,128)S(1)}, f32[24,1536]{1,0:T(8,128)}, u32[]{:S(2)}, u32[]{:S(2)}) collective-permute-start(f32[24,1536]{1,0:T(8,128)S(1)} %pad_maximum_fusion.2.mine_ref), channel_id=1, source_target_pairs={{0,3},{1,2},{2,1},{3,0},{4,7},{5,6},{6,5},{7,4},{8,11},{9,10},{10,... | collective-permute-start | bytes 442376 | tf_op jit(solution)/shard_map/ppermute | solution.py:274
  9.6 29.6 %collective-permute-start.4 = (bf16[1024,256]{1,0:T(8,128)(2,1)}, bf16[1024,256]{1,0:T(8,128)(2,1)S(1)}, u32[]{:S(2)}, u32[]{:S(2)}) collective-permute-start(bf16[1024,256]{1,0:T(8,128)(2,1)} %get-tuple-element.27), channel_id=1, source_target_pairs={{0,1},{1,0},{2,3},{3,2},{4,5},{5,4},{6,7},{7,6},{8,9},{9,8},{10,11... | collective-permute-start | bytes 1572872 | tf_op jit(solution)/shard_map/ppermute | solution.py:268
  12.0 32.5 %collective-permute-start.16 = (bf16[1024,256]{1,0:T(8,128)(2,1)}, bf16[1024,256]{1,0:T(8,128)(2,1)S(1)}, u32[]{:S(2)}, u32[]{:S(2)}) collective-permute-start(bf16[1024,256]{1,0:T(8,128)(2,1)} %get-tuple-element.27), channel_id=1, source_target_pairs={{1,2},{2,1},{5,6},{6,5},{9,10},{10,9},{13,14},{14,13},{17,18},{18,... | collective-permute-start | bytes 1572872 | tf_op jit(solution)/shard_map/ppermute | solution.py:269
  14.1 25.1 %copy-start.1 = (bf16[1024,256]{1,0:T(8,128)(2,1)S(1)}, bf16[1024,256]{1,0:T(8,128)(2,1)}, u32[]{:S(2)}) copy-start(bf16[1024,256]{1,0:T(8,128)(2,1)} %get-tuple-element.26) | copy-start | bytes 1572868
  14.1 32.9 %collective-permute-start.18 = (bf16[1024,256]{1,0:T(8,128)(2,1)}, bf16[1024,256]{1,0:T(8,128)(2,1)S(1)}, u32[]{:S(2)}, u32[]{:S(2)}) collective-permute-start(bf16[1024,256]{1,0:T(8,128)(2,1)} %get-tuple-element.27), channel_id=1, source_target_pairs={{0,3},{3,0},{4,7},{7,4},{8,11},{11,8},{12,15},{15,12},{16,19},{19,... | collective-permute-start | bytes 1572872 | tf_op jit(solution)/shard_map/ppermute | solution.py:270
  16.9 44.9 %collective-permute-start.3 = (bf16[1024,256]{1,0:T(8,128)(2,1)}, bf16[1024,256]{1,0:T(8,128)(2,1)S(1)}, u32[]{:S(2)}, u32[]{:S(2)}) collective-permute-start(bf16[1024,256]{1,0:T(8,128)(2,1)} %get-tuple-element.26), channel_id=1, source_target_pairs={{0,1},{1,0},{2,3},{3,2},{4,5},{5,4},{6,7},{7,6},{8,9},{9,8},{10,11... | collective-permute-start | bytes 1572872 | tf_op jit(solution)/shard_map/ppermute | solution.py:268
  22.1 44.8 %collective-permute-start.6 = (bf16[1024,256]{1,0:T(8,128)(2,1)}, bf16[1024,256]{1,0:T(8,128)(2,1)S(1)}, u32[]{:S(2)}, u32[]{:S(2)}) collective-permute-start(bf16[1024,256]{1,0:T(8,128)(2,1)} %get-tuple-element.26), channel_id=1, source_target_pairs={{1,2},{2,1},{5,6},{6,5},{9,10},{10,9},{13,14},{14,13},{17,18},{18,... | collective-permute-start | bytes 1572872 | tf_op jit(solution)/shard_map/ppermute | solution.py:269
  39.2 43.8 %collective-permute-start.8 = (bf16[1024,256]{1,0:T(8,128)(2,1)S(1)}, bf16[1024,256]{1,0:T(8,128)(2,1)S(1)}, u32[]{:S(2)}, u32[]{:S(2)}) collective-permute-start(bf16[1024,256]{1,0:T(8,128)(2,1)S(1)} %copy-done.1), channel_id=1, source_target_pairs={{0,3},{3,0},{4,7},{7,4},{8,11},{11,8},{12,15},{15,12},{16,19},{19,... | collective-permute-start | bytes 1572872 | tf_op jit(solution)/shard_map/ppermute | solution.py:270
  44.5 33.7 %collective-permute-start.15 = (bf16[1024,256]{1,0:T(8,128)(2,1)S(1)}, bf16[1024,256]{1,0:T(8,128)(2,1)S(1)}, u32[]{:S(2)}, u32[]{:S(2)}) collective-permute-start(bf16[1024,256]{1,0:T(8,128)(2,1)S(1)} %collective-permute-done.4.refs_1_), channel_id=1, source_target_pairs={{1,2},{2,1},{5,6},{6,5},{9,10},{10,9},{13,14},{14,13},{17,18},{18,... | collective-permute-start | bytes 1572872 | tf_op jit(solution)/shard_map/ppermute | solution.py:271
  47.0 31.2 %collective-permute-start.17 = (bf16[1024,256]{1,0:T(8,128)(2,1)S(1)}, bf16[1024,256]{1,0:T(8,128)(2,1)S(1)}, u32[]{:S(2)}, u32[]{:S(2)}) collective-permute-start(bf16[1024,256]{1,0:T(8,128)(2,1)S(1)} %collective-permute-done.16.refs_2_), channel_id=1, source_target_pairs={{1,0},{2,3},{5,4},{6,7},{9,8},{10,11},{13,12},{14,15},{17,16},{18,... | collective-permute-start | bytes 1572872 | tf_op jit(solution)/shard_map/ppermute | solution.py:272
  61.8 26.4 %collective-permute-start.5 = (bf16[1024,256]{1,0:T(8,128)(2,1)S(1)}, bf16[1024,256]{1,0:T(8,128)(2,1)S(1)}, u32[]{:S(2)}, u32[]{:S(2)}) collective-permute-start(bf16[1024,256]{1,0:T(8,128)(2,1)S(1)} %collective-permute-done.3.refs_0_), channel_id=1, source_target_pairs={{1,2},{2,1},{5,6},{6,5},{9,10},{10,9},{13,14},{14,13},{17,18},{18,... | collective-permute-start | bytes 1572872 | tf_op jit(solution)/shard_map/ppermute | solution.py:271
  67.0 21.2 %collective-permute-start.7 = (bf16[1024,256]{1,0:T(8,128)(2,1)S(1)}, bf16[1024,256]{1,0:T(8,128)(2,1)S(1)}, u32[]{:S(2)}, u32[]{:S(2)}) collective-permute-start(bf16[1024,256]{1,0:T(8,128)(2,1)S(1)} %collective-permute-done.6.refs_2_), channel_id=1, source_target_pairs={{1,0},{2,3},{5,4},{6,7},{9,8},{10,11},{13,12},{14,15},{17,16},{18,... | collective-permute-start | bytes 1572872 | tf_op jit(solution)/shard_map/ppermute | solution.py:272
  78.2 14.5 %collective-permute-start.9 = (bf16[2,2,128,512]{3,2,1,0:T(8,128)(2,1)S(1)}, bf16[2,2,128,512]{3,2,1,0:T(8,128)(2,1)S(1)}, u32[]{:S(2)}, u32[]{:S(2)}) collective-permute-start(bf16[2,2,128,512]{3,2,1,0:T(8,128)(2,1)S(1)} %get-tuple-element.30), channel_id=1, source_target_pairs={{0,4},{4,0},{8,12},{12,8},{16,20},{20,16},{24,28},{28,24},{1,5},{5... | collective-permute-start | bytes 1572872 | tf_op jit(solution)/shard_map/ppermute | solution.py:281
  78.2 14.5 %collective-permute-start.10 = (bf16[2,2,128,512]{3,2,1,0:T(8,128)(2,1)S(1)}, bf16[2,2,128,512]{3,2,1,0:T(8,128)(2,1)S(1)}, u32[]{:S(2)}, u32[]{:S(2)}) collective-permute-start(bf16[2,2,128,512]{3,2,1,0:T(8,128)(2,1)S(1)} %get-tuple-element.31), channel_id=1, source_target_pairs={{0,4},{4,0},{8,12},{12,8},{16,20},{20,16},{24,28},{28,24},{1,5},{5... | collective-permute-start | bytes 1572872 | tf_op jit(solution)/shard_map/ppermute | solution.py:281
  83.0 9.8 %collective-permute-start.19 = (bf16[2,2,128,512]{3,2,1,0:T(8,128)(2,1)S(1)}, bf16[2,2,128,512]{3,2,1,0:T(8,128)(2,1)S(1)}, u32[]{:S(2)}, u32[]{:S(2)}) collective-permute-start(bf16[2,2,128,512]{3,2,1,0:T(8,128)(2,1)S(1)} %get-tuple-element.38), channel_id=1, source_target_pairs={{0,4},{4,0},{8,12},{12,8},{16,20},{20,16},{24,28},{28,24},{1,5},{5... | collective-permute-start | bytes 1572872 | tf_op jit(solution)/shard_map/ppermute | solution.py:286
  92.6 6.4 %collective-permute-start.11 = (bf16[2,2,128,512]{3,2,1,0:T(8,128)(2,1)S(1)}, bf16[2,2,128,512]{3,2,1,0:T(8,128)(2,1)S(1)}, u32[]{:S(2)}, u32[]{:S(2)}) collective-permute-start(bf16[2,2,128,512]{3,2,1,0:T(8,128)(2,1)S(1)} %get-tuple-element.32), channel_id=1, source_target_pairs={{0,4},{4,0},{8,12},{12,8},{16,20},{20,16},{24,28},{28,24},{1,5},{5... | collective-permute-start | bytes 1572872 | tf_op jit(solution)/shard_map/ppermute | solution.py:286
  95.5 9.4 %collective-permute-start.20 = (bf16[2,128,512]{2,1,0:T(8,128)(2,1)S(1)}, bf16[2,128,512]{2,1,0:T(8,128)(2,1)S(1)}, u32[]{:S(2)}, u32[]{:S(2)}) collective-permute-start(bf16[2,128,512]{2,1,0:T(8,128)(2,1)S(1)} %get-tuple-element.40), channel_id=1, source_target_pairs={{0,8},{4,12},{8,0},{12,4},{16,24},{20,28},{24,16},{28,20},{1,9},{5... | collective-permute-start | bytes 786440 | tf_op jit(solution)/shard_map/ppermute | solution.py:290
  97.1 14.4 %collective-permute-start.21 = (bf16[2,128,512]{2,1,0:T(8,128)(2,1)S(1)}, bf16[2,128,512]{2,1,0:T(8,128)(2,1)S(1)}, u32[]{:S(2)}, u32[]{:S(2)}) collective-permute-start(bf16[2,128,512]{2,1,0:T(8,128)(2,1)S(1)} %get-tuple-element.41), channel_id=1, source_target_pairs={{0,16},{4,20},{8,24},{12,28},{16,0},{20,4},{24,8},{28,12},{1,17},{... | collective-permute-start | bytes 786440 | tf_op jit(solution)/shard_map/ppermute | solution.py:290
  98.6 12.8 %collective-permute-start.22 = (bf16[2,128,512]{2,1,0:T(8,128)(2,1)S(1)}, bf16[2,128,512]{2,1,0:T(8,128)(2,1)S(1)}, u32[]{:S(2)}, u32[]{:S(2)}) collective-permute-start(bf16[2,128,512]{2,1,0:T(8,128)(2,1)S(1)} %get-tuple-element.42), channel_id=1, source_target_pairs={{0,24},{4,28},{8,16},{12,20},{16,8},{20,12},{24,0},{28,4},{1,25},{... | collective-permute-start | bytes 786440 | tf_op jit(solution)/shard_map/ppermute | solution.py:290
  101.8 14.1 %collective-permute-start.12 = (bf16[2,128,512]{2,1,0:T(8,128)(2,1)S(1)}, bf16[2,128,512]{2,1,0:T(8,128)(2,1)S(1)}, u32[]{:S(2)}, u32[]{:S(2)}) collective-permute-start(bf16[2,128,512]{2,1,0:T(8,128)(2,1)S(1)} %get-tuple-element.34), channel_id=1, source_target_pairs={{0,8},{4,12},{8,0},{12,4},{16,24},{20,28},{24,16},{28,20},{1,9},{5... | collective-permute-start | bytes 786440 | tf_op jit(solution)/shard_map/ppermute | solution.py:290
  103.4 18.9 %collective-permute-start.13 = (bf16[2,128,512]{2,1,0:T(8,128)(2,1)S(1)}, bf16[2,128,512]{2,1,0:T(8,128)(2,1)S(1)}, u32[]{:S(2)}, u32[]{:S(2)}) collective-permute-start(bf16[2,128,512]{2,1,0:T(8,128)(2,1)S(1)} %get-tuple-element.35), channel_id=1, source_target_pairs={{0,16},{4,20},{8,24},{12,28},{16,0},{20,4},{24,8},{28,12},{1,17},{... | collective-permute-start | bytes 786440 | tf_op jit(solution)/shard_map/ppermute | solution.py:290
  104.9 17.4 %collective-permute-start.14 = (bf16[2,128,512]{2,1,0:T(8,128)(2,1)S(1)}, bf16[2,128,512]{2,1,0:T(8,128)(2,1)S(1)}, u32[]{:S(2)}, u32[]{:S(2)}) collective-permute-start(bf16[2,128,512]{2,1,0:T(8,128)(2,1)S(1)} %get-tuple-element.36), channel_id=1, source_target_pairs={{0,24},{4,28},{8,16},{12,20},{16,8},{20,12},{24,0},{28,4},{1,25},{... | collective-permute-start | bytes 786440 | tf_op jit(solution)/shard_map/ppermute | solution.py:290
  (1 other events, 7.9 us)

commit v5 on v3

v5 whole, which is shorter than its diff:
```python
import functools

import jax
import jax.numpy as jnp
from jax import lax
from jax.experimental import pallas as pl
from jax.experimental.pallas import tpu as pltpu
from jax.sharding import PartitionSpec as P

HIGH = lax.Precision.HIGHEST
LINK = jnp.float16
OVER_ROWS = (((0,), (0,)), ((), ()))
RANGE = 120.0
PAD = 32
VMEM_BYTES = 24 * 2**20
FRONT_BYTES = 60 * 2**20
DESIGN_ROWS = 21
STEP = 256
FREE = pl.CostEstimate(flops=0, bytes_accessed=0, transcendentals=0)


def solve_coef(design, cross):
    gram = jnp.dot(design, design.T, precision=HIGH)
    factor = jnp.linalg.cholesky(gram)
    return jax.scipy.linalg.cho_solve((factor, True), cross)


def encode(genotypes):
    return jnp.where(genotypes >= 0.0, jnp.exp2(RANGE * genotypes - RANGE), 0.0).astype(jnp.bfloat16)


def decode(coded):
    value = coded.astype(jnp.float32)
    observed = value > 0.0
    return jnp.log2(jnp.where(observed, value, 1.0)) * (1.0 / RANGE) + 1.0, observed


def thirds(x):
    a = x.astype(jnp.bfloat16)
    rest = x - a.astype(jnp.float32)
    b = rest.astype(jnp.bfloat16)
    return a, b, (rest - b.astype(jnp.float32)).astype(jnp.bfloat16)


def left_stack(x):
    a, b, c = thirds(x)
    return jnp.concatenate([a, a, b, b, a, c], axis=0)


def right_stack(y):
    a, b, c = thirds(y)
    return jnp.concatenate([a, b, a, b, c, a], axis=0)


def resid_spread(dosage, observed, fitted):
    twice = jnp.clip(fitted, 0.04, 1.96)
    product = twice * (2.0 - twice)
    resid = jnp.where(observed, dosage - twice, 0.0)
    spread = jnp.where(observed, 0.5 * jnp.sqrt(product), 0.0)
    return resid.astype(jnp.bfloat16), spread.astype(jnp.bfloat16)


def product(left, right):
    return lax.dot_general(left, right, OVER_ROWS, preferred_element_type=jnp.float32)


def cross_kernel(genotypes_ref, pcs_ref, mine_ref):
    count, width = genotypes_ref.shape
    k = pcs_ref.shape[0]
    rows = mine_ref.shape[0]
    snps = mine_ref.shape[1] - width
    genotypes = genotypes_ref[...]
    blank = jnp.zeros((rows - k - 1, width), jnp.float32)
    design = jnp.concatenate([jnp.ones((1, width), jnp.float32), pcs_ref[...], blank], axis=0)
    d = [t.astype(jnp.float32) for t in thirds(design)]
    stacked = jnp.concatenate(d + d[:1], axis=0).astype(jnp.bfloat16)
    g = thirds(jnp.where(genotypes >= 0.0, genotypes, 0.0))
    lanes = (((1,), (1,)), ((), ()))
    first, second, third = [lax.dot_general(t, stacked, lanes, preferred_element_type=jnp.float32) for t in g]
    cross = (first[:, 2 * rows:3 * rows] + second[:, rows:2 * rows] + third[:, :rows]) + (first[:, rows:2 * rows] + second[:, :rows])
    cross = cross + first[:, :rows]
    step = pl.program_id(0)
    mine_ref[:, pl.ds(pl.multiple_of(step * count, count), count)] = cross.T

    @pl.when(step == 0)
    def _():
        mine_ref[:, snps:] = design


def cross_part(genotypes, pcs):
    snps, width = genotypes.shape
    rows = DESIGN_ROWS + -DESIGN_ROWS % 8
    return pl.pallas_call(
        cross_kernel,
        grid=(snps // STEP,),
        out_shape=jax.ShapeDtypeStruct((rows, snps + width), jnp.float32),
        in_specs=[pl.BlockSpec((STEP, width), lambda i: (i, 0)), pl.BlockSpec(pcs.shape, lambda i: (0, 0))],
        out_specs=pl.BlockSpec((rows, snps + width), lambda i: (0, 0)),
        compiler_params=pltpu.CompilerParams(vmem_limit_bytes=FRONT_BYTES),
        cost_estimate=FREE,
    )(genotypes, pcs)


def coef_kernel(cuts, mine_ref, a_ref, b_ref, c_ref, coef_ref, own_ref, near_ref, late_ref):
    rows, snps = mine_ref.shape[0], coef_ref.shape[1]
    across_lanes = (((1,), (1,)), ((), ()))
    cross = mine_ref[:, :snps] + a_ref[:, :snps] + b_ref[:, :snps] + c_ref[:, :snps]
    gram = jnp.zeros((rows, rows), jnp.float32)
    blank = jnp.zeros((PAD - rows, near_ref.shape[1]), jnp.float32)
    half = near_ref.shape[1] // 2
    for j, ref in enumerate((mine_ref, a_ref, b_ref, c_ref)):
        design = ref[:, snps:]
        gram = gram + lax.dot_general(design, design, across_lanes, precision=HIGH, preferred_element_type=jnp.float32)
        if j > 0:
            design = jnp.concatenate([design[:, at:at + n] for first, n in cuts for at in (first, first + half)], axis=1)
        stacked = right_stack(jnp.concatenate([design, blank], axis=0))
        if j < 2:
            (own_ref, near_ref)[j][...] = stacked
        else:
            late_ref[j - 2] = stacked
    row = lax.broadcasted_iota(jnp.int32, (rows, rows), 0)
    unit = (row == lax.broadcasted_iota(jnp.int32, (rows, rows), 1)).astype(jnp.float32)
    gram = gram + jnp.where(row >= DESIGN_ROWS, unit, 0.0)
    left, inverse = gram, unit
    for j in range(DESIGN_ROWS):
        pivot = 1.0 / left[j:j + 1, j:j + 1]
        factor = (left[:, j:j + 1] - unit[:, j:j + 1]) * pivot
        left, inverse = left - factor * left[j:j + 1, :], inverse - factor * inverse[j:j + 1, :]
    coef = jnp.dot(inverse, cross, precision=HIGH, preferred_element_type=jnp.float32)
    rest = cross - jnp.dot(gram, coef, precision=HIGH, preferred_element_type=jnp.float32)
    coef = coef + jnp.dot(inverse, rest, precision=HIGH, preferred_element_type=jnp.float32)
    coef_ref[...] = left_stack(jnp.concatenate([coef, jnp.zeros((PAD - rows, snps), jnp.float32)], axis=0))


def coefficients(theirs, snps, cuts):
    vmem = pl.BlockSpec(memory_space=pltpu.VMEM)
    width = theirs[0].shape[1] - snps
    shapes = [(6 * PAD, snps), (6 * PAD, width), (6 * PAD, width), (2, 6 * PAD, width)]
    return pl.pallas_call(
        functools.partial(coef_kernel, cuts),
        out_shape=tuple(jax.ShapeDtypeStruct(shape, jnp.bfloat16) for shape in shapes),
        in_specs=[vmem] * 4,
        out_specs=(vmem,) * 4,
        compiler_params=pltpu.CompilerParams(vmem_limit_bytes=VMEM_BYTES),
        cost_estimate=pl.CostEstimate(flops=10**10, bytes_accessed=0, transcendentals=0),
    )(*theirs)


def pack(sums):
    size = jnp.exp2(8.0 * jnp.log2(jnp.maximum(jnp.abs(sums), 1e-30)) + 20.0)
    return jnp.where(sums < 0.0, -size, size).astype(jnp.bfloat16)


def unpack(packed):
    value = packed.astype(jnp.float32)
    size = jnp.abs(value)
    sums = jnp.exp2(jnp.log2(jnp.where(size > 0.0, size, 1.0)) * 0.125 - 2.5)
    return jnp.where(size > 0.0, jnp.where(value < 0.0, -sums, sums), 0.0)


def own_kernel(place_ref, coef_ref, design_ref, own_ref, terms_ref, keep_ref, give_ref):
    half = keep_ref.shape[1]
    snps = coef_ref.shape[1]

    def terms(k, _):
        at = pl.ds(pl.multiple_of(k * STEP, STEP), STEP)
        dosage = own_ref[at, :]
        fitted = product(coef_ref[:, at], design_ref[...])
        terms_ref[0, at, :], terms_ref[1, at, :] = resid_spread(dosage, dosage >= 0.0, fitted)
        return 0

    lax.fori_loop(0, snps // STEP, terms, 0)
    first_core = place_ref[0] == 0
    for t in range(2):
        a, b = [product(terms_ref[t, :, h * half:(h + 1) * half], terms_ref[t]) for h in range(2)]
        keep_ref[t] = jnp.where(first_core, a, b)
        give_ref[t] = pack(jnp.where(first_core, b, a))


def block_kernel(groups, place_ref, coef_ref, design_ref, terms_ref, *refs):
    *coded, keep_ref, give_ref, rows_ref = refs
    snps = coef_ref.shape[1]

    def terms(k, _):
        at = pl.ds(pl.multiple_of(k * STEP, STEP), STEP)
        first = 0
        for choices, design, count, _ in groups:
            here = slice(first, first + 2 * count)
            values = [coded[i][at, c:c + 2 * count] for i, c in choices]
            value = values[0] if len(values) == 1 else jnp.where(place_ref[1] == 1, values[0], values[1])
            dosage, observed = decode(value)
            fitted = product(coef_ref[:, at], design_ref[design])
            rows_ref[0, at, here], rows_ref[1, at, here] = resid_spread(dosage, observed, fitted)
            first += 2 * count
        return 0

    lax.fori_loop(0, snps // STEP, terms, 0)
    first_core = place_ref[0] == 0
    first = 0
    for _, _, count, target in groups:
        for t in range(2):
            sums = product(rows_ref[t, :, first:first + 2 * count], terms_ref[t])
            a, b = sums[:count], sums[count:]
            keep_ref[target(t)] = jnp.where(first_core, a, b)
            give_ref[target(t)] = pack(jnp.where(first_core, b, a))
        first += 2 * count


def block_sums(place, coef, design, sums, own=None, terms=None, coded=(), groups=()):
    snps = coef.shape[1]
    vmem = pl.BlockSpec(memory_space=pltpu.VMEM)
    out = (jax.ShapeDtypeStruct(sums, jnp.float32), jax.ShapeDtypeStruct(sums, jnp.bfloat16))
    if own is not None:
        kernel, operands, scratch = own_kernel, (place, coef, design, own), []
        out = (jax.ShapeDtypeStruct((2,) + own.shape, jnp.bfloat16),) + out
    else:
        kernel, operands = functools.partial(block_kernel, groups), (place, coef, design, terms, *coded)
        scratch = [pltpu.VMEM((2, snps, sum(2 * group[2] for group in groups)), jnp.bfloat16)]
    return pl.pallas_call(
        kernel,
        out_shape=out,
        in_specs=[pl.BlockSpec(memory_space=pltpu.SMEM)] + [vmem] * (len(operands) - 1),
        out_specs=tuple(vmem for _ in out),
        scratch_shapes=scratch,
        compiler_params=pltpu.CompilerParams(vmem_limit_bytes=VMEM_BYTES),
        cost_estimate=FREE,
    )(*operands)


def add_kernel(first, place_ref, own_ref, near_ref, late_ref, got_own_ref, got_near_ref, got_late_ref, mine_ref, *refs):
    *sent, sums = refs
    here = slice(first, first + mine_ref.shape[1])
    sums[0] = own_ref[:, here] + unpack(got_own_ref[:, here])
    sums[1] = near_ref[:, here] + unpack(got_near_ref[:, here])
    for i in range(2):
        sums[2 + i] = late_ref[i] + unpack(got_late_ref[i])
    mine_ref[...] = sums[place_ref[2]]
    for d, ref in enumerate(sent, 1):
        ref[...] = pack(sums[jnp.bitwise_xor(place_ref[2], d)])


def add_cores(place, first, *operands):
    shape = operands[2].shape[1:]
    vmem = pl.BlockSpec(memory_space=pltpu.VMEM)
    return pl.pallas_call(
        functools.partial(add_kernel, first),
        out_shape=(jax.ShapeDtypeStruct(shape, jnp.float32),) + (jax.ShapeDtypeStruct(shape, jnp.bfloat16),) * 3,
        in_specs=[pl.BlockSpec(memory_space=pltpu.SMEM)] + [vmem] * len(operands),
        out_specs=(vmem,) * 4,
        scratch_shapes=[pltpu.VMEM((4,) + shape, jnp.float32)],
        compiler_params=pltpu.CompilerParams(vmem_limit_bytes=VMEM_BYTES),
        cost_estimate=FREE,
    )(place, *operands)


def divide_kernel(*refs):
    *parts, out_ref = refs
    first = 0
    for p in range(len(parts) // 4):
        mine, *got = parts[4 * p:4 * p + 4]
        count = mine.shape[1]
        sums = [mine[t] + unpack(got[0][t]) + unpack(got[1][t]) + unpack(got[2][t]) for t in range(2)]
        out_ref[first:first + count, :] = sums[0] / (4.0 * sums[1])
        first += count


def divide(parts):
    width = parts[0].shape[2]
    vmem = pl.BlockSpec(memory_space=pltpu.VMEM)
    return pl.pallas_call(
        divide_kernel,
        out_shape=jax.ShapeDtypeStruct((sum(m.shape[1] for m in parts[::4]), width), jnp.float32),
        in_specs=[vmem] * len(parts),
        out_specs=vmem,
        compiler_params=pltpu.CompilerParams(vmem_limit_bytes=VMEM_BYTES),
        cost_estimate=FREE,
    )(*parts)


def kinship(sums):
    return sums[0] / (4.0 * sums[1])


def after(value, *earlier):
    return lax.optimization_barrier((value, *earlier))[0]


def line_of_four(genotypes, pcs):
    width = genotypes.shape[1]
    half = width // 2
    s = lax.axis_index("snp")
    z = lax.axis_index("samp")
    chip = lax.div(s, 2)
    inner = jnp.logical_or(z == 1, z == 2)
    place = jnp.stack([lax.rem(s, 2), inner.astype(jnp.int32), chip ^ z])
    other_core = [(i, i ^ 1) for i in range(8)]
    cuts, pieces = ((0, half // 2), (half // 2, half // 4), (3 * half // 4, half // 4)), ((0,), (1, 2))
    mine = cross_part(genotypes, pcs)
    snps = genotypes.shape[0]
    theirs = [mine] + [lax.ppermute(mine, "samp", [(i, i ^ j) for i in range(4)]) for j in range(1, 4)]
    coef, design_own, design_near, design_late = coefficients(theirs, snps, cuts)

    coded = []
    for piece in pieces:
        columns = [genotypes[:, at:at + n] for p in piece for first, n in cuts[p:p + 1] for at in (first, first + half)]
        coded.append(encode(after(jnp.concatenate(columns, axis=1), mine)))
    near = [lax.ppermute(c, "samp", [(i, i ^ 1) for i in range(4)]) for c in coded]
    across = [lax.ppermute(c, "samp", [(1, 2), (2, 1)]) for c in coded]
    held, begin = {}, {}
    for i, piece in enumerate(pieces):
        at = 0
        for p in piece:
            held[p] = (i, at)
            at += 2 * cuts[p][1]
    start = 0
    for p, (_, count) in enumerate(cuts):
        begin[p] = start
        start += 2 * count

    sums = (2, half, width)
    terms, keep_own, give_own = block_sums(place, coef, design_own, sums, own=genotypes)
    groups = [
        (((held[p]),), (slice(None), slice(begin[p], begin[p] + 2 * n)), n, lambda t, first=first, n=n: (t, slice(first, first + n)))
        for p, (first, n) in enumerate(cuts)
    ]
    keep_near, give_near = block_sums(place, coef, design_near, sums, terms=terms, coded=near, groups=groups)
    got_own, got_near = [lax.ppermute(g, "snp", other_core) for g in (give_own, give_near)]
    totals, gates = [], [(), (), ()]
    for p, (first, count) in enumerate(cuts):
        i, at = held[p]
        cols = slice(at, at + 2 * count)
        ready = jnp.where(inner, near[i][:, cols], coded[i][:, cols])
        again = across[i][:, cols]
        if gates[p]:
            ready, again = [after(r, *gates[p]) for r in (ready, again)]
        far = lax.ppermute(ready, "samp", [(1, 2), (2, 1), (0, 3), (3, 0)])
        out = lax.ppermute(again, "samp", [(1, 0), (2, 3)])
        where = [(g, slice(None), slice(begin[p], begin[p] + 2 * count)) for g in range(2)]
        groups = [
            (choices, where[g], count, lambda t, g=g: (g, t)) for g, choices in enumerate((((0, 0), (1, 0)), ((2, at), (0, 0))))
        ]
        if p == 2:
            terms = after(terms, *totals[1:4])
        keep, give = block_sums(place, coef, design_late, (2, 2, count, width), terms=terms, coded=(far, out, across[i]), groups=groups)
        got = lax.ppermute(give, "snp", other_core)
        kept, *sent = add_cores(place, first, keep_own, keep_near, keep, got_own, got_near, got)
        if p == 0:
            gates[2] = (kept,)
        totals.append(kept)
        for d in range(1, 4):
            totals.append(lax.ppermute(sent[d - 1], "snp", [(i, i ^ (2 * d)) for i in range(8)]))
    return divide(totals)


def any_mesh(genotypes, pcs):
    width = genotypes.shape[1]
    design = jnp.concatenate([jnp.ones((1, width), jnp.float32), pcs], axis=0)
    observed = genotypes >= 0.0
    dosage = jnp.where(observed, genotypes, 0.0)
    cross_part = lax.dot_general(design, dosage, (((1,), (1,)), ((), ())), precision=HIGH)
    cross = lax.psum(cross_part, "samp")
    full = lax.all_gather(design, "samp", axis=1, tiled=True)
    fitted = lax.dot_general(solve_coef(full, cross), design, OVER_ROWS, precision=HIGH)
    own = resid_spread(dosage, observed, fitted)
    rows = lax.all_gather(jnp.stack(own), "samp", axis=2, tiled=True)
    sums = jnp.stack([product(rows[t], own[t]) for t in range(2)])
    return kinship(lax.psum_scatter(sums, "snp", scatter_dimension=1, tiled=True))


def solution(mesh):
    body = line_of_four if (mesh.shape["snp"], mesh.shape["samp"]) == (8, 4) else any_mesh
    in_specs = (P("snp", "samp"), P(None, "samp"))
    return jax.shard_map(body, mesh=mesh, in_specs=in_specs, out_specs=P("snp", "samp"), check_vma=False)
```

time: 135 us -> 122 us (0.904)
  waiting for transfers between devices: 66 us -> 51.7 us
  Pallas kernels: 28.5 us -> 34.7 us
  local copies, waits for them, and re-layouts: 5.03 us -> 1.75 us
  starting transfers between devices: 31.2 us -> 29.3 us
  matrix products: 1.78 us -> 0 us
  other arithmetic: 2.27 us -> 4.03 us
    ppermute x3, waiting for transfers between devices: 51.2 us -> 0.01 us  [line_of_four(): lax.ppermute(mine, 'samp', [(i, i ^ j) for i in range(4)])]
    ppermute x6 -> x8, waiting for transfers between devices: 0.02 us -> 21.9 us  [the longest x3 16.2 us: line_of_four(): far = lax.ppermute(ready, 'samp', [(1, 2), (2, 1), (0, 3), (3, 0)])]
    ppermute x2, waiting for transfers between devices: 0.01 us -> 20.2 us  [line_of_four(): lax.ppermute(c, 'samp', [(i, i ^ 1) for i in range(4)])]
    ppermute x6 -> x9, waiting for transfers between devices: 14.7 us -> 9.57 us  [line_of_four(): lax.ppermute(sent[d - 1], 'snp', [(i, i ^ 2 * d) for i in range(8)])]
    pallas_call x4 -> x6, Pallas kernels: 11.3 us -> 16.4 us  [the longest x3 5.61 us: add_cores(): pl.pallas_call(functools.partial(add_kernel, first), out_shape=(jax.Shape...]
    ppermute x3, starting transfers between devices: 6.5 us -> 3.49 us  [line_of_four(): lax.ppermute(mine, 'samp', [(i, i ^ j) for i in range(4)])]
    concatenate x4 -> x2, other arithmetic: 0.04 us -> 2.15 us  [line_of_four(): coded.append(encode(after(jnp.concatenate(columns, axis=1), mine)))]
    ppermute x6 -> x9, starting transfers between devices: 8.99 us -> 10.9 us  [line_of_four(): lax.ppermute(sent[d - 1], 'snp', [(i, i ^ 2 * d) for i in range(8)])]
  transfers between devices with their start and end apart: 21 -> 27, of which waited for: 7 -> 11; matrix products, arithmetic and copies ran while one was open for 3% -> 5% of each run, Pallas kernels for 19% -> 23%
where the time goes in v5:
time: 122 us
  waiting for transfers between devices  51.7 us (42%)
  Pallas kernels  34.7 us (28%)
  starting transfers between devices  29.3 us (24%)
  other arithmetic  4.03 us (3%)
  local copies, waits for them, and re-layouts  1.75 us (1%)
    ppermute x2, waiting for transfers between devices, line_of_four(): lax.ppermute(c, 'samp', [(i, i ^ 1) for i in range(4)])  20.2 us
    pallas_call x5, Pallas kernels, block_sums(): pl.pallas_call(kernel, out_shape=out, in_specs=[pl.BlockSpec(memory_space...  18.3 us
    ppermute x3, waiting for transfers between devices, line_of_four(): far = lax.ppermute(ready, 'samp', [(1, 2), (2, 1), (0, 3), (3, 0)])  16.2 us
    ppermute x9, starting transfers between devices, line_of_four(): lax.ppermute(sent[d - 1], 'snp', [(i, i ^ 2 * d) for i in range(8)])  10.9 us
    ppermute x9, waiting for transfers between devices, line_of_four(): lax.ppermute(sent[d - 1], 'snp', [(i, i ^ 2 * d) for i in range(8)])  9.57 us
    ppermute x3, waiting for transfers between devices, line_of_four(): out = lax.ppermute(again, 'samp', [(1, 0), (2, 3)])  5.7 us
    pallas_call x3, Pallas kernels, add_cores(): pl.pallas_call(functools.partial(add_kernel, first), out_shape=(jax.Shape...  5.61 us
    pallas_call x1, Pallas kernels, cross_part(): pl.pallas_call(cross_kernel, grid=(snps // STEP,), out_shape=jax.ShapeDty...  4.81 us
  transfers between devices with their start and end apart: 27, of which 11 were waited for; matrix products, arithmetic and copies ran while one was open for 5% of the time, Pallas kernels for 23%

profile of v5, /device:TPU:16, one launch (start us, length us, event | category | flops | bytes accessed | tf_op | source)
XLA Modules:
  0.0 121.7 jit_solution(6734235101302326140)
XLA Ops:
  0.0 4.8 %shard_map.28.mine_ref = f32[24,1536]{1,0:T(8,128)} custom-call(f32[1024,512]{1,0:T(8,128)} %own_ref.1, f32[20,512]{1,0:T(8,128)} %pcs_ref.1), custom_call_target="tpu_custom_call" | custom-call | tf_op jit(solution)/shard_map/pallas_call | solution.py:93
  9.6 2.5 %collective-permute-start.3 = (bf16[1024,256]{1,0:T(8,128)(2,1)}, bf16[1024,256]{1,0:T(8,128)(2,1)S(1)}, u32[]{:S(2)}, u32[]{:S(2)}) collective-permute-start(bf16[1024,256]{1,0:T(8,128)(2,1)} %select_convert_fusion.1), channel_id=1, source_target_pairs={{0,1},{1,0},{2,3},{3,2},{4,5},{5,4},{6,7},{7,6},{8,9},{9,8},{10,11... | collective-permute-start | bytes 1572872 | tf_op jit(solution)/shard_map/ppermute | solution.py:307
  12.1 1.9 %collective-permute-start.6 = (bf16[1024,256]{1,0:T(8,128)(2,1)}, bf16[1024,256]{1,0:T(8,128)(2,1)S(1)}, u32[]{:S(2)}, u32[]{:S(2)}) collective-permute-start(bf16[1024,256]{1,0:T(8,128)(2,1)} %select_convert_fusion.1), channel_id=1, source_target_pairs={{1,2},{2,1},{5,6},{6,5},{9,10},{10,9},{13,14},{14,13},{17,18},{18,... | collective-permute-start | bytes 1572872 | tf_op jit(solution)/shard_map/ppermute | solution.py:308
  14.0 1.6 %fusion = (f32[1024,64]{1,0:T(8,128)}, f32[1024,64]{1,0:T(8,128)}, f32[1024,64]{1,0:T(8,128)}, f32[1024,64]{1,0:T(8,128)}) fusion(f32[1024,512]{1,0:T(8,128)S(1)} %copy-done), kind=kLoop, calls=%fused_computation.8 | loop fusion | bytes 2097152 | tf_op jit(solution)/shard_map/slice | solution.py:305
  15.6 2.1 %pad_maximum_fusion.1 = f32[1024,256]{1,0:T(8,128)S(1)} fusion(f32[1024,64]{1,0:T(8,128)} %get-tuple-element.71, f32[1024,64]{1,0:T(8,128)} %get-tuple-element.72, f32[1024,64]{1,0:T(8,128)} %get-tuple-element.70, f32[1024,64]{1,0:T(8,128)} %get-tuple-element.69), kind=kLoop, calls=%fused_computation.1 | loop fusion | flops 786432 | bytes 2097152 | tf_op jit(solution)/shard_map/concatenate | solution.py:306
  18.1 10.1 %collective-permute-done.3.refs_0_ = bf16[1024,256]{1,0:T(8,128)(2,1)S(1)} collective-permute-done((bf16[1024,256]{1,0:T(8,128)(2,1)}, bf16[1024,256]{1,0:T(8,128)(2,1)S(1)}, u32[]{:S(2)}, u32[]{:S(2)}) %collective-permute-start.3) | collective-permute-done | bytes 524320 | tf_op jit(solution)/shard_map/ppermute | solution.py:307
  30.1 1.9 %collective-permute-start.15 = (bf16[1024,256]{1,0:T(8,128)(2,1)S(1)}, bf16[1024,256]{1,0:T(8,128)(2,1)S(1)}, u32[]{:S(2)}, u32[]{:S(2)}) collective-permute-start(bf16[1024,256]{1,0:T(8,128)(2,1)S(1)} %select_convert_fusion), channel_id=1, source_target_pairs={{1,2},{2,1},{5,6},{6,5},{9,10},{10,9},{13,14},{14,13},{17,18},{18,... | collective-permute-start | bytes 1572872 | tf_op jit(solution)/shard_map/ppermute | solution.py:308
  32.0 2.1 %collective-permute-start.5 = (bf16[1024,256]{1,0:T(8,128)(2,1)S(1)}, bf16[1024,256]{1,0:T(8,128)(2,1)S(1)}, u32[]{:S(2)}, u32[]{:S(2)}) collective-permute-start(bf16[1024,256]{1,0:T(8,128)(2,1)S(1)} %broadcast_select_fusion), channel_id=1, source_target_pairs={{1,2},{2,1},{0,3},{3,0},{5,6},{6,5},{4,7},{7,4},{9,10},{10,9},{8,1... | collective-permute-start | bytes 1572872 | tf_op jit(solution)/shard_map/ppermute | solution.py:336
  35.5 3.8 %shard_map.29 = (bf16[192,1024]{1,0:T(8,128)(2,1)S(1)}, bf16[192,512]{1,0:T(8,128)(2,1)S(1)}, bf16[192,512]{1,0:T(8,128)(2,1)S(1)}, bf16[2,192,512]{2,1,0:T(8,128)(2,1)S(1)}) custom-call(f32[24,1536]{1,0:T(8,128)S(1)} %copy-done.1, f32[24,1536]{1,0:T(8,128)S(1)} %collective-permute-done.a_ref, f32[24,1536]{1,0:T(8,128)S(1)} %collective-permute-done.1.b_ref, ...), custom_call_target="tpu_custom_call" | custom-call | flops 10000000000 | tf_op jit(solution)/shard_map/pallas_call | solution.py:139
  39.2 4.0 %shard_map.30 = (bf16[2,1024,512]{2,1,0:T(8,128)(2,1)S(1)}, f32[2,256,512]{2,1,0:T(8,128)S(1)}, bf16[2,256,512]{2,1,0:T(8,128)(2,1)S(1)}) custom-call(s32[3]{0:T(128)S(1)} %pad_add_fusion.place_ref, bf16[192,1024]{1,0:T(8,128)(2,1)S(1)} %get-tuple-element.37.coef_ref, bf16[192,512]{1,0:T(8,128)(2,1)S(1)} %get-tuple-element.38.design_ref, f32[1024,512]{1,0:T(8,128)S(1)} %copy-done), custom_call_target="tpu_custom_call" | custom-call | tf_op jit(solution)/shard_map/pallas_call | solution.py:219
  43.3 10.1 %collective-permute-done.4.refs_1_ = bf16[1024,256]{1,0:T(8,128)(2,1)S(1)} collective-permute-done((bf16[1024,256]{1,0:T(8,128)(2,1)S(1)}, bf16[1024,256]{1,0:T(8,128)(2,1)S(1)}, u32[]{:S(2)}, u32[]{:S(2)}) %collective-permute-start.4) | collective-permute-done | bytes 524320 | tf_op jit(solution)/shard_map/ppermute | solution.py:307
  53.4 4.3 %shard_map.31 = (f32[2,256,512]{2,1,0:T(8,128)S(1)}, bf16[2,256,512]{2,1,0:T(8,128)(2,1)S(1)}) custom-call(s32[3]{0:T(128)S(1)} %pad_add_fusion.place_ref, bf16[192,1024]{1,0:T(8,128)(2,1)S(1)} %get-tuple-element.37.coef_ref, bf16[192,512]{1,0:T(8,128)(2,1)S(1)} %get-tuple-element.40.design_ref, bf16[2,1024,512]{2,1,0:T(8,128)(2,1)S(1)} %get-tuple-element.60.terms_ref, ...), custom_call_target="tpu_custom_call" | custom-call | tf_op jit(solution)/shard_map/pallas_call | solution.py:219
  57.7 9.3 %collective-permute-done.5.refs_0_ = bf16[1024,256]{1,0:T(8,128)(2,1)S(1)} collective-permute-done((bf16[1024,256]{1,0:T(8,128)(2,1)S(1)}, bf16[1024,256]{1,0:T(8,128)(2,1)S(1)}, u32[]{:S(2)}, u32[]{:S(2)}) %collective-permute-start.5) | collective-permute-done | bytes 524320 | tf_op jit(solution)/shard_map/ppermute | solution.py:336
  67.0 4.2 %shard_map.32 = (f32[2,2,128,512]{3,2,1,0:T(8,128)S(1)}, bf16[2,2,128,512]{3,2,1,0:T(8,128)(2,1)S(1)}) custom-call(s32[3]{0:T(128)S(1)} %pad_add_fusion.place_ref, bf16[192,1024]{1,0:T(8,128)(2,1)S(1)} %get-tuple-element.37.coef_ref, bf16[2,192,512]{2,1,0:T(8,128)(2,1)S(1)} %get-tuple-element.45.design_ref, ...), custom_call_target="tpu_custom_call" | custom-call | tf_op jit(solution)/shard_map/pallas_call | solution.py:219
  73.3 2.8 %shard_map.33 = (f32[2,128,512]{2,1,0:T(8,128)S(1)}, bf16[2,128,512]{2,1,0:T(8,128)(2,1)S(1)}, bf16[2,128,512]{2,1,0:T(8,128)(2,1)S(1)}, bf16[2,128,512]{2,1,0:T(8,128)(2,1)S(1)}) custom-call(s32[3]{0:T(128)S(1)} %pad_add_fusion.place_ref, f32[2,256,512]{2,1,0:T(8,128)S(1)} %get-tuple-element.39.own_ref, f32[2,256,512]{2,1,0:T(8,128)S(1)} %get-tuple-element.44.near_ref, ...), custom_call_target="tpu_custom_call" | custom-call | tf_op jit(solution)/shard_map/pallas_call | solution.py:245
  79.7 4.5 %collective-permute-done.14.refs_0_ = bf16[1024,128]{1,0:T(8,128)(2,1)S(1)} collective-permute-done((bf16[1024,128]{1,0:T(8,128)(2,1)S(1)}, bf16[1024,128]{1,0:T(8,128)(2,1)S(1)}, u32[]{:S(2)}, u32[]{:S(2)}) %collective-permute-start.14) | collective-permute-done | bytes 262176 | tf_op jit(solution)/shard_map/ppermute | solution.py:336
  85.5 2.9 %shard_map.34 = (f32[2,2,64,512]{3,2,1,0:T(8,128)S(1)}, bf16[2,2,64,512]{3,2,1,0:T(8,128)(2,1)S(1)}) custom-call(s32[3]{0:T(128)S(1)} %pad_add_fusion.place_ref, bf16[192,1024]{1,0:T(8,128)(2,1)S(1)} %get-tuple-element.37.coef_ref, bf16[2,192,512]{2,1,0:T(8,128)(2,1)S(1)} %get-tuple-element.45.design_ref, ...), custom_call_target="tpu_custom_call" | custom-call | tf_op jit(solution)/shard_map/pallas_call | solution.py:219
  88.6 2.8 %collective-permute-done.12.refs_2_ = bf16[2,128,512]{2,1,0:T(8,128)(2,1)S(1)} collective-permute-done((bf16[2,128,512]{2,1,0:T(8,128)(2,1)S(1)}, bf16[2,128,512]{2,1,0:T(8,128)(2,1)S(1)}, u32[]{:S(2)}, u32[]{:S(2)}) %collective-permute-start.12) | collective-permute-done | bytes 262176 | tf_op jit(solution)/shard_map/ppermute | solution.py:351
  91.4 5.7 %collective-permute-done.22.refs_1_ = bf16[1024,128]{1,0:T(8,128)(2,1)S(1)} collective-permute-done((bf16[1024,128]{1,0:T(8,128)(2,1)S(1)}, bf16[1024,128]{1,0:T(8,128)(2,1)S(1)}, u32[]{:S(2)}, u32[]{:S(2)}) %collective-permute-start.22) | collective-permute-done | bytes 262176 | tf_op jit(solution)/shard_map/ppermute | solution.py:337
  97.1 2.3 %collective-permute-done.21.refs_0_ = bf16[1024,128]{1,0:T(8,128)(2,1)S(1)} collective-permute-done((bf16[1024,128]{1,0:T(8,128)(2,1)S(1)}, bf16[1024,128]{1,0:T(8,128)(2,1)S(1)}, u32[]{:S(2)}, u32[]{:S(2)}) %collective-permute-start.21) | collective-permute-done | bytes 262176 | tf_op jit(solution)/shard_map/ppermute | solution.py:336
  99.4 2.9 %shard_map.36 = (f32[2,2,64,512]{3,2,1,0:T(8,128)S(1)}, bf16[2,2,64,512]{3,2,1,0:T(8,128)(2,1)S(1)}) custom-call(s32[3]{0:T(128)S(1)} %pad_add_fusion.place_ref, bf16[192,1024]{1,0:T(8,128)(2,1)S(1)} %get-tuple-element.37.coef_ref, bf16[2,192,512]{2,1,0:T(8,128)(2,1)S(1)} %get-tuple-element.45.design_ref, ...), custom_call_target="tpu_custom_call" | custom-call | tf_op jit(solution)/shard_map/pallas_call | solution.py:219
  114.4 1.8 %collective-permute-done.24.refs_9_ = bf16[2,64,512]{2,1,0:T(8,128)(2,1)S(1)} collective-permute-done((bf16[2,64,512]{2,1,0:T(8,128)(2,1)S(1)}, bf16[2,64,512]{2,1,0:T(8,128)(2,1)S(1)}, u32[]{:S(2)}, u32[]{:S(2)}) %collective-permute-start.24) | collective-permute-done | bytes 131104 | tf_op jit(solution)/shard_map/ppermute | solution.py:351
  116.2 3.3 %collective-permute-done.25.refs_10_ = bf16[2,64,512]{2,1,0:T(8,128)(2,1)S(1)} collective-permute-done((bf16[2,64,512]{2,1,0:T(8,128)(2,1)S(1)}, bf16[2,64,512]{2,1,0:T(8,128)(2,1)S(1)}, u32[]{:S(2)}, u32[]{:S(2)}) %collective-permute-start.25) | collective-permute-done | bytes 131104 | tf_op jit(solution)/shard_map/ppermute | solution.py:351
  119.5 2.2 %shard_map.38 = f32[256,512]{1,0:T(8,128)} custom-call(f32[2,128,512]{2,1,0:T(8,128)S(1)} %get-tuple-element.50.refs_0_, bf16[2,128,512]{2,1,0:T(8,128)(2,1)S(1)} %collective-permute-done.11.refs_1_, bf16[2,128,512]{2,1,0:T(8,128)(2,1)S(1)} %collective-permute-done.12.refs_2_, bf16[2,128,512]{2,1,0:T(8,128)(2,1)S(1)} %collective-permute-done.13.refs_3_, ...), custom_call_target="tpu_custom_call" | custom-call | tf_op jit(solution)/shard_map/pallas_call | solution.py:270
  (59 shorter events, 27.5 us)
Async XLA Ops:
  4.8 25.3 %collective-permute-start = (f32[24,1536]{1,0:T(8,128)}, f32[24,1536]{1,0:T(8,128)S(1)}, u32[]{:S(2)}, u32[]{:S(2)}) collective-permute-start(f32[24,1536]{1,0:T(8,128)} %shard_map.28.mine_ref), channel_id=1, source_target_pairs={{0,1},{1,0},{2,3},{3,2},{4,5},{5,4},{6,7},{7,6},{8,9},{9,8},{10,11... | collective-permute-start | bytes 442376 | tf_op jit(solution)/shard_map/ppermute | solution.py:300
  6.4 25.6 %collective-permute-start.1 = (f32[24,1536]{1,0:T(8,128)}, f32[24,1536]{1,0:T(8,128)S(1)}, u32[]{:S(2)}, u32[]{:S(2)}) collective-permute-start(f32[24,1536]{1,0:T(8,128)} %shard_map.28.mine_ref), channel_id=1, source_target_pairs={{0,2},{1,3},{2,0},{3,1},{4,6},{5,7},{6,4},{7,5},{8,10},{9,11},{10,... | collective-permute-start | bytes 442376 | tf_op jit(solution)/shard_map/ppermute | solution.py:300
  6.7 28.7 %collective-permute-start.2 = (f32[24,1536]{1,0:T(8,128)}, f32[24,1536]{1,0:T(8,128)}, u32[]{:S(2)}, u32[]{:S(2)}) collective-permute-start(f32[24,1536]{1,0:T(8,128)} %shard_map.28.mine_ref), channel_id=1, source_target_pairs={{0,3},{1,2},{2,1},{3,0},{4,7},{5,6},{6,5},{7,4},{8,11},{9,10},{10,... | collective-permute-start | bytes 442376 | tf_op jit(solution)/shard_map/ppermute | solution.py:300
  9.6 18.6 %collective-permute-start.3 = (bf16[1024,256]{1,0:T(8,128)(2,1)}, bf16[1024,256]{1,0:T(8,128)(2,1)S(1)}, u32[]{:S(2)}, u32[]{:S(2)}) collective-permute-start(bf16[1024,256]{1,0:T(8,128)(2,1)} %select_convert_fusion.1), channel_id=1, source_target_pairs={{0,1},{1,0},{2,3},{3,2},{4,5},{5,4},{6,7},{7,6},{8,9},{9,8},{10,11... | collective-permute-start | bytes 1572872 | tf_op jit(solution)/shard_map/ppermute | solution.py:307
  12.1 22.0 %collective-permute-start.6 = (bf16[1024,256]{1,0:T(8,128)(2,1)}, bf16[1024,256]{1,0:T(8,128)(2,1)S(1)}, u32[]{:S(2)}, u32[]{:S(2)}) collective-permute-start(bf16[1024,256]{1,0:T(8,128)(2,1)} %select_convert_fusion.1), channel_id=1, source_target_pairs={{1,2},{2,1},{5,6},{6,5},{9,10},{10,9},{13,14},{14,13},{17,18},{18,... | collective-permute-start | bytes 1572872 | tf_op jit(solution)/shard_map/ppermute | solution.py:308
  28.2 25.1 %collective-permute-start.4 = (bf16[1024,256]{1,0:T(8,128)(2,1)S(1)}, bf16[1024,256]{1,0:T(8,128)(2,1)S(1)}, u32[]{:S(2)}, u32[]{:S(2)}) collective-permute-start(bf16[1024,256]{1,0:T(8,128)(2,1)S(1)} %select_convert_fusion), channel_id=1, source_target_pairs={{0,1},{1,0},{2,3},{3,2},{4,5},{5,4},{6,7},{7,6},{8,9},{9,8},{10,11... | collective-permute-start | bytes 1572872 | tf_op jit(solution)/shard_map/ppermute | solution.py:307
  30.1 41.7 %collective-permute-start.15 = (bf16[1024,256]{1,0:T(8,128)(2,1)S(1)}, bf16[1024,256]{1,0:T(8,128)(2,1)S(1)}, u32[]{:S(2)}, u32[]{:S(2)}) collective-permute-start(bf16[1024,256]{1,0:T(8,128)(2,1)S(1)} %select_convert_fusion), channel_id=1, source_target_pairs={{1,2},{2,1},{5,6},{6,5},{9,10},{10,9},{13,14},{14,13},{17,18},{18,... | collective-permute-start | bytes 1572872 | tf_op jit(solution)/shard_map/ppermute | solution.py:308
  32.0 35.0 %collective-permute-start.5 = (bf16[1024,256]{1,0:T(8,128)(2,1)S(1)}, bf16[1024,256]{1,0:T(8,128)(2,1)S(1)}, u32[]{:S(2)}, u32[]{:S(2)}) collective-permute-start(bf16[1024,256]{1,0:T(8,128)(2,1)S(1)} %broadcast_select_fusion), channel_id=1, source_target_pairs={{1,2},{2,1},{0,3},{3,0},{5,6},{6,5},{4,7},{7,4},{9,10},{10,9},{8,1... | collective-permute-start | bytes 1572872 | tf_op jit(solution)/shard_map/ppermute | solution.py:336
  34.1 32.9 %collective-permute-start.7 = (bf16[1024,256]{1,0:T(8,128)(2,1)S(1)}, bf16[1024,256]{1,0:T(8,128)(2,1)S(1)}, u32[]{:S(2)}, u32[]{:S(2)}) collective-permute-start(bf16[1024,256]{1,0:T(8,128)(2,1)S(1)} %collective-permute-done.6.refs_2_), channel_id=1, source_target_pairs={{1,0},{2,3},{5,4},{6,7},{9,8},{10,11},{13,12},{14,15},{17,16},{18,... | collective-permute-start | bytes 1572872 | tf_op jit(solution)/shard_map/ppermute | solution.py:337
  43.2 30.1 %collective-permute-start.8 = (bf16[2,256,512]{2,1,0:T(8,128)(2,1)S(1)}, bf16[2,256,512]{2,1,0:T(8,128)(2,1)S(1)}, u32[]{:S(2)}, u32[]{:S(2)}) collective-permute-start(bf16[2,256,512]{2,1,0:T(8,128)(2,1)S(1)} %get-tuple-element.47), channel_id=1, source_target_pairs={{0,4},{4,0},{8,12},{12,8},{16,20},{20,16},{24,28},{28,24},{1,5},{5... | collective-permute-start | bytes 1572872 | tf_op jit(solution)/shard_map/ppermute | solution.py:327
  57.6 15.7 %collective-permute-start.9 = (bf16[2,256,512]{2,1,0:T(8,128)(2,1)S(1)}, bf16[2,256,512]{2,1,0:T(8,128)(2,1)S(1)}, u32[]{:S(2)}, u32[]{:S(2)}) collective-permute-start(bf16[2,256,512]{2,1,0:T(8,128)(2,1)S(1)} %get-tuple-element.48), channel_id=1, source_target_pairs={{0,4},{4,0},{8,12},{12,8},{16,20},{20,16},{24,28},{28,24},{1,5},{5... | collective-permute-start | bytes 1572872 | tf_op jit(solution)/shard_map/ppermute | solution.py:327
  71.4 12.7 %collective-permute-start.14 = (bf16[1024,128]{1,0:T(8,128)(2,1)S(1)}, bf16[1024,128]{1,0:T(8,128)(2,1)S(1)}, u32[]{:S(2)}, u32[]{:S(2)}) collective-permute-start(bf16[1024,128]{1,0:T(8,128)(2,1)S(1)} %get-tuple-element.76), channel_id=1, source_target_pairs={{1,2},{2,1},{0,3},{3,0},{5,6},{6,5},{4,7},{7,4},{9,10},{10,9},{8,1... | collective-permute-start | bytes 786440 | tf_op jit(solution)/shard_map/ppermute | solution.py:336
  71.8 13.7 %collective-permute-start.16 = (bf16[1024,128]{1,0:T(8,128)(2,1)S(1)}, bf16[1024,128]{1,0:T(8,128)(2,1)S(1)}, u32[]{:S(2)}, u32[]{:S(2)}) collective-permute-start(bf16[1024,128]{1,0:T(8,128)(2,1)S(1)} %get-tuple-element.78), channel_id=1, source_target_pairs={{1,0},{2,3},{5,4},{6,7},{9,8},{10,11},{13,12},{14,15},{17,16},{18,... | collective-permute-start | bytes 786440 | tf_op jit(solution)/shard_map/ppermute | solution.py:337
  76.1 12.4 %collective-permute-start.11 = (bf16[2,128,512]{2,1,0:T(8,128)(2,1)S(1)}, bf16[2,128,512]{2,1,0:T(8,128)(2,1)S(1)}, u32[]{:S(2)}, u32[]{:S(2)}) collective-permute-start(bf16[2,128,512]{2,1,0:T(8,128)(2,1)S(1)} %get-tuple-element.51), channel_id=1, source_target_pairs={{0,8},{4,12},{8,0},{12,4},{16,24},{20,28},{24,16},{28,20},{1,9},{5... | collective-permute-start | bytes 786440 | tf_op jit(solution)/shard_map/ppermute | solution.py:351
  77.6 13.8 %collective-permute-start.12 = (bf16[2,128,512]{2,1,0:T(8,128)(2,1)S(1)}, bf16[2,128,512]{2,1,0:T(8,128)(2,1)S(1)}, u32[]{:S(2)}, u32[]{:S(2)}) collective-permute-start(bf16[2,128,512]{2,1,0:T(8,128)(2,1)S(1)} %get-tuple-element.52), channel_id=1, source_target_pairs={{0,16},{4,20},{8,24},{12,28},{16,0},{20,4},{24,8},{28,12},{1,17},{... | collective-permute-start | bytes 786440 | tf_op jit(solution)/shard_map/ppermute | solution.py:351
  79.2 12.2 %collective-permute-start.13 = (bf16[2,128,512]{2,1,0:T(8,128)(2,1)S(1)}, bf16[2,128,512]{2,1,0:T(8,128)(2,1)S(1)}, u32[]{:S(2)}, u32[]{:S(2)}) collective-permute-start(bf16[2,128,512]{2,1,0:T(8,128)(2,1)S(1)} %get-tuple-element.53), channel_id=1, source_target_pairs={{0,24},{4,28},{8,16},{12,20},{16,8},{20,12},{24,0},{28,4},{1,25},{... | collective-permute-start | bytes 786440 | tf_op jit(solution)/shard_map/ppermute | solution.py:351
  84.2 13.0 %collective-permute-start.22 = (bf16[1024,128]{1,0:T(8,128)(2,1)S(1)}, bf16[1024,128]{1,0:T(8,128)(2,1)S(1)}, u32[]{:S(2)}, u32[]{:S(2)}) collective-permute-start(bf16[1024,128]{1,0:T(8,128)(2,1)S(1)} %get-tuple-element.62), channel_id=1, source_target_pairs={{1,0},{2,3},{5,4},{6,7},{9,8},{10,11},{13,12},{14,15},{17,16},{18,... | collective-permute-start | bytes 786440 | tf_op jit(solution)/shard_map/ppermute | solution.py:337
  85.5 14.0 %collective-permute-start.21 = (bf16[1024,128]{1,0:T(8,128)(2,1)S(1)}, bf16[1024,128]{1,0:T(8,128)(2,1)S(1)}, u32[]{:S(2)}, u32[]{:S(2)}) collective-permute-start(bf16[1024,128]{1,0:T(8,128)(2,1)S(1)} %get-tuple-element.61), channel_id=1, source_target_pairs={{1,2},{2,1},{0,3},{3,0},{5,6},{6,5},{4,7},{7,4},{9,10},{10,9},{8,1... | collective-permute-start | bytes 786440 | tf_op jit(solution)/shard_map/ppermute | solution.py:336
  88.5 14.0 %collective-permute-start.17 = (bf16[2,2,64,512]{3,2,1,0:T(8,128)(2,1)S(1)}, bf16[2,2,64,512]{3,2,1,0:T(8,128)(2,1)S(1)}, u32[]{:S(2)}, u32[]{:S(2)}) collective-permute-start(bf16[2,2,64,512]{3,2,1,0:T(8,128)(2,1)S(1)} %get-tuple-element.55), channel_id=1, source_target_pairs={{0,4},{4,0},{8,12},{12,8},{16,20},{20,16},{24,28},{28,24},{1,5},{5... | collective-permute-start | bytes 786440 | tf_op jit(solution)/shard_map/ppermute | solution.py:345
  103.9 8.1 %collective-permute-start.18 = (bf16[2,64,512]{2,1,0:T(8,128)(2,1)S(1)}, bf16[2,64,512]{2,1,0:T(8,128)(2,1)S(1)}, u32[]{:S(2)}, u32[]{:S(2)}) collective-permute-start(bf16[2,64,512]{2,1,0:T(8,128)(2,1)S(1)} %get-tuple-element.57), channel_id=1, source_target_pairs={{0,8},{4,12},{8,0},{12,4},{16,24},{20,28},{24,16},{28,20},{1,9},{5... | collective-permute-start | bytes 393224 | tf_op jit(solution)/shard_map/ppermute | solution.py:351
  105.4 8.2 %collective-permute-start.19 = (bf16[2,64,512]{2,1,0:T(8,128)(2,1)S(1)}, bf16[2,64,512]{2,1,0:T(8,128)(2,1)S(1)}, u32[]{:S(2)}, u32[]{:S(2)}) collective-permute-start(bf16[2,64,512]{2,1,0:T(8,128)(2,1)S(1)} %get-tuple-element.58), channel_id=1, source_target_pairs={{0,16},{4,20},{8,24},{12,28},{16,0},{20,4},{24,8},{28,12},{1,17},{... | collective-permute-start | bytes 393224 | tf_op jit(solution)/shard_map/ppermute | solution.py:351
  107.0 7.4 %collective-permute-start.20 = (bf16[2,64,512]{2,1,0:T(8,128)(2,1)S(1)}, bf16[2,64,512]{2,1,0:T(8,128)(2,1)S(1)}, u32[]{:S(2)}, u32[]{:S(2)}) collective-permute-start(bf16[2,64,512]{2,1,0:T(8,128)(2,1)S(1)} %get-tuple-element.59), channel_id=1, source_target_pairs={{0,24},{4,28},{8,16},{12,20},{16,8},{20,12},{24,0},{28,4},{1,25},{... | collective-permute-start | bytes 393224 | tf_op jit(solution)/shard_map/ppermute | solution.py:351
  110.4 9.0 %collective-permute-start.25 = (bf16[2,64,512]{2,1,0:T(8,128)(2,1)S(1)}, bf16[2,64,512]{2,1,0:T(8,128)(2,1)S(1)}, u32[]{:S(2)}, u32[]{:S(2)}) collective-permute-start(bf16[2,64,512]{2,1,0:T(8,128)(2,1)S(1)} %get-tuple-element.67), channel_id=1, source_target_pairs={{0,16},{4,20},{8,24},{12,28},{16,0},{20,4},{24,8},{28,12},{1,17},{... | collective-permute-start | bytes 393224 | tf_op jit(solution)/shard_map/ppermute | solution.py:351
  112.0 7.5 %collective-permute-start.26 = (bf16[2,64,512]{2,1,0:T(8,128)(2,1)S(1)}, bf16[2,64,512]{2,1,0:T(8,128)(2,1)S(1)}, u32[]{:S(2)}, u32[]{:S(2)}) collective-permute-start(bf16[2,64,512]{2,1,0:T(8,128)(2,1)S(1)} %get-tuple-element.68), channel_id=1, source_target_pairs={{0,24},{4,28},{8,16},{12,20},{16,8},{20,12},{24,0},{28,4},{1,25},{... | collective-permute-start | bytes 393224 | tf_op jit(solution)/shard_map/ppermute | solution.py:351
  (7 other events, 55.8 us)

commit v6 on v5

--- a/solution.py
+++ b/solution.py
@@ -16,6 +16,7 @@
 FRONT_BYTES = 60 * 2**20
 DESIGN_ROWS = 21
 STEP = 256
+CROSS = 512
 FREE = pl.CostEstimate(flops=0, bytes_accessed=0, transcendentals=0)
 
 
@@ -92,27 +93,26 @@
     rows = DESIGN_ROWS + -DESIGN_ROWS % 8
     return pl.pallas_call(
         cross_kernel,
-        grid=(snps // STEP,),
+        grid=(snps // CROSS,),
         out_shape=jax.ShapeDtypeStruct((rows, snps + width), jnp.float32),
-        in_specs=[pl.BlockSpec((STEP, width), lambda i: (i, 0)), pl.BlockSpec(pcs.shape, lambda i: (0, 0))],
+        in_specs=[pl.BlockSpec((CROSS, width), lambda i: (i, 0)), pl.BlockSpec(pcs.shape, lambda i: (0, 0))],
         out_specs=pl.BlockSpec((rows, snps + width), lambda i: (0, 0)),
         compiler_params=pltpu.CompilerParams(vmem_limit_bytes=FRONT_BYTES),
         cost_estimate=FREE,
     )(genotypes, pcs)
 
 
-def coef_kernel(cuts, mine_ref, a_ref, b_ref, c_ref, coef_ref, own_ref, near_ref, late_ref):
-    rows, snps = mine_ref.shape[0], coef_ref.shape[1]
+def coef_kernel(cuts, pair_ref, got_ref, coef_ref, own_ref, near_ref, late_ref):
+    rows, (snps, width) = pair_ref.shape[0], (coef_ref.shape[1], near_ref.shape[1])
     across_lanes = (((1,), (1,)), ((), ()))
-    cross = mine_ref[:, :snps] + a_ref[:, :snps] + b_ref[:, :snps] + c_ref[:, :snps]
+    cross = pair_ref[:, :snps] + got_ref[:, :snps]
     gram = jnp.zeros((rows, rows), jnp.float32)
-    blank = jnp.zeros((PAD - rows, near_ref.shape[1]), jnp.float32)
-    half = near_ref.shape[1] // 2
-    for j, ref in enumerate((mine_ref, a_ref, b_ref, c_ref)):
-        design = ref[:, snps:]
+    blank = jnp.zeros((PAD - rows, width), jnp.float32)
+    for j, ref in enumerate((pair_ref, pair_ref, got_ref, got_ref)):
+        design = ref[:, snps + j % 2 * width:snps + (j % 2 + 1) * width]
         gram = gram + lax.dot_general(design, design, across_lanes, precision=HIGH, preferred_element_type=jnp.float32)
         if j > 0:
-            design = jnp.concatenate([design[:, at:at + n] for first, n in cuts for at in (first, first + half)], axis=1)
+            design = jnp.concatenate([design[:, at:at + n] for first, n in cuts for at in (first, first + width // 2)], axis=1)
         stacked = right_stack(jnp.concatenate([design, blank], axis=0))
         if j < 2:
             (own_ref, near_ref)[j][...] = stacked
@@ -132,18 +132,18 @@
     coef_ref[...] = left_stack(jnp.concatenate([coef, jnp.zeros((PAD - rows, snps), jnp.float32)], axis=0))
 
 
-def coefficients(theirs, snps, cuts):
+def coefficients(pair, got, snps, cuts):
     vmem = pl.BlockSpec(memory_space=pltpu.VMEM)
-    width = theirs[0].shape[1] - snps
+    width = (pair.shape[1] - snps) // 2
     shapes = [(6 * PAD, snps), (6 * PAD, width), (6 * PAD, width), (2, 6 * PAD, width)]
     return pl.pallas_call(
         functools.partial(coef_kernel, cuts),
         out_shape=tuple(jax.ShapeDtypeStruct(shape, jnp.bfloat16) for shape in shapes),
-        in_specs=[vmem] * 4,
+        in_specs=[vmem] * 2,
         out_specs=(vmem,) * 4,
         compiler_params=pltpu.CompilerParams(vmem_limit_bytes=VMEM_BYTES),
         cost_estimate=pl.CostEstimate(flops=10**10, bytes_accessed=0, transcendentals=0),
-    )(*theirs)
+    )(pair, got)
 
 
 def pack(sums):
@@ -297,13 +297,15 @@
     cuts, pieces = ((0, half // 2), (half // 2, half // 4), (3 * half // 4, half // 4)), ((0,), (1, 2))
     mine = cross_part(genotypes, pcs)
     snps = genotypes.shape[0]
-    theirs = [mine] + [lax.ppermute(mine, "samp", [(i, i ^ j) for i in range(4)]) for j in range(1, 4)]
-    coef, design_own, design_near, design_late = coefficients(theirs, snps, cuts)
+    other = lax.ppermute(mine, "samp", [(i, i ^ 1) for i in range(4)])
+    pair = jnp.concatenate([mine[:, :snps] + other[:, :snps], mine[:, snps:], other[:, snps:]], axis=1)
+    got = lax.ppermute(pair, "samp", [(i, i ^ 2) for i in range(4)])
+    coef, design_own, design_near, design_late = coefficients(pair, got, snps, cuts)
 
     coded = []
     for piece in pieces:
         columns = [genotypes[:, at:at + n] for p in piece for first, n in cuts[p:p + 1] for at in (first, first + half)]
-        coded.append(encode(after(jnp.concatenate(columns, axis=1), mine)))
+        coded.append(encode(after(jnp.concatenate(columns, axis=1), mine if not coded else pair)))
     near = [lax.ppermute(c, "samp", [(i, i ^ 1) for i in range(4)]) for c in coded]
     across = [lax.ppermute(c, "samp", [(1, 2), (2, 1)]) for c in coded]
     held, begin = {}, {}

time: 122 us -> 118 us (0.967)
  starting transfers between devices: 29.3 us -> 26.7 us
  Pallas kernels: 34.7 us -> 32.9 us
    ppermute x2, waiting for transfers between devices: 20.2 us -> 12.9 us  [line_of_four(): lax.ppermute(c, 'samp', [(i, i ^ 1) for i in range(4)])]
    ppermute x2, waiting for transfers between devices: 0.01 us -> 5.44 us  [line_of_four(): across = [lax.ppermute(c, 'samp', [(1, 2), (2, 1)]) for c in coded]]
    ppermute x9, waiting for transfers between devices: 9.57 us -> 11.9 us  [line_of_four(): lax.ppermute(sent[d - 1], 'snp', [(i, i ^ 2 * d) for i in range(8)])]
    ppermute x3, waiting for transfers between devices: 5.7 us -> 3.44 us  [line_of_four(): out = lax.ppermute(again, 'samp', [(1, 0), (2, 3)])]
    ppermute x3 -> x2, starting transfers between devices: 3.49 us -> 1.65 us  [the longest x1 1.58 us: line_of_four(): other = lax.ppermute(mine, 'samp', [(i, i ^ 1) for i in range(4)])]
  transfers between devices with their start and end apart: 27 -> 26, of which waited for: 11 -> 13; matrix products, arithmetic and copies ran while one was open for 5% -> 5% of each run, Pallas kernels for 23% -> 23%
where the time goes in v6:
time: 118 us; the launch traced here: 117 us
  waiting for transfers between devices  51.4 us (44%)
  Pallas kernels  32.9 us (28%)
  starting transfers between devices  26.7 us (23%)
  other arithmetic  4.06 us (3%)
  local copies, waits for them, and re-layouts  1.77 us (2%)
    pallas_call x5, Pallas kernels, block_sums(): pl.pallas_call(kernel, out_shape=out, in_specs=[pl.BlockSpec(memory_space...  18.3 us
    ppermute x3, waiting for transfers between devices, line_of_four(): far = lax.ppermute(ready, 'samp', [(1, 2), (2, 1), (0, 3), (3, 0)])  16.9 us
    ppermute x2, waiting for transfers between devices, line_of_four(): lax.ppermute(c, 'samp', [(i, i ^ 1) for i in range(4)])  12.9 us
    ppermute x9, waiting for transfers between devices, line_of_four(): lax.ppermute(sent[d - 1], 'snp', [(i, i ^ 2 * d) for i in range(8)])  11.9 us
    ppermute x9, starting transfers between devices, line_of_four(): lax.ppermute(sent[d - 1], 'snp', [(i, i ^ 2 * d) for i in range(8)])  10.9 us
    pallas_call x3, Pallas kernels, add_cores(): pl.pallas_call(functools.partial(add_kernel, first), out_shape=(jax.Shape...  5.56 us
    ppermute x2, waiting for transfers between devices, line_of_four(): across = [lax.ppermute(c, 'samp', [(1, 2), (2, 1)]) for c in coded]  5.44 us
    ppermute x2, starting transfers between devices, line_of_four(): across = [lax.ppermute(c, 'samp', [(1, 2), (2, 1)]) for c in coded]  4.69 us
  transfers between devices with their start and end apart: 26, of which 13 were waited for; matrix products, arithmetic and copies ran while one was open for 5% of the time, Pallas kernels for 23%

profile of v6, /device:TPU:16, one launch (start us, length us, event | category | flops | bytes accessed | tf_op | source)
XLA Modules:
  0.0 117.1 jit_solution(3715378971197399985)
XLA Ops:
  0.0 3.9 %shard_map.28 = f32[24,1536]{1,0:T(8,128)} custom-call(f32[1024,512]{1,0:T(8,128)} %own_ref.1, f32[20,512]{1,0:T(8,128)} %pcs_ref.1), custom_call_target="tpu_custom_call" | custom-call | tf_op jit(solution)/shard_map/pallas_call | solution.py:94
  7.3 2.3 %collective-permute-start.5 = (bf16[1024,256]{1,0:T(8,128)(2,1)}, bf16[1024,256]{1,0:T(8,128)(2,1)S(1)}, u32[]{:S(2)}, u32[]{:S(2)}) collective-permute-start(bf16[1024,256]{1,0:T(8,128)(2,1)} %select_convert_fusion.1), channel_id=1, source_target_pairs={{1,2},{2,1},{5,6},{6,5},{9,10},{10,9},{13,14},{14,13},{17,18},{18,... | collective-permute-start | bytes 1572872 | tf_op jit(solution)/shard_map/ppermute | solution.py:310
  9.6 1.6 %fusion = (f32[1024,64]{1,0:T(8,128)}, f32[1024,64]{1,0:T(8,128)}, f32[1024,64]{1,0:T(8,128)}, f32[1024,64]{1,0:T(8,128)}) fusion(f32[1024,512]{1,0:T(8,128)S(1)} %copy-done), kind=kLoop, calls=%fused_computation.10 | loop fusion | bytes 2097152 | tf_op jit(solution)/shard_map/slice | solution.py:307
  11.4 2.1 %pad_maximum_fusion.1 = f32[1024,256]{1,0:T(8,128)S(1)} fusion(f32[1024,64]{1,0:T(8,128)} %get-tuple-element.71, f32[1024,64]{1,0:T(8,128)} %get-tuple-element.72, f32[1024,64]{1,0:T(8,128)} %get-tuple-element.70, f32[1024,64]{1,0:T(8,128)} %get-tuple-element.69), kind=kLoop, calls=%fused_computation.1 | loop fusion | flops 786432 | bytes 2097152 | tf_op jit(solution)/shard_map/concatenate | solution.py:308
  13.9 3.1 %collective-permute-start.3 = (bf16[1024,256]{1,0:T(8,128)(2,1)S(1)}, bf16[1024,256]{1,0:T(8,128)(2,1)S(1)}, u32[]{:S(2)}, u32[]{:S(2)}) collective-permute-start(bf16[1024,256]{1,0:T(8,128)(2,1)S(1)} %select_convert_fusion), channel_id=1, source_target_pairs={{0,1},{1,0},{2,3},{3,2},{4,5},{5,4},{6,7},{7,6},{8,9},{9,8},{10,11... | collective-permute-start | bytes 1572872 | tf_op jit(solution)/shard_map/ppermute | solution.py:309
  17.0 2.3 %collective-permute-start.14 = (bf16[1024,256]{1,0:T(8,128)(2,1)S(1)}, bf16[1024,256]{1,0:T(8,128)(2,1)S(1)}, u32[]{:S(2)}, u32[]{:S(2)}) collective-permute-start(bf16[1024,256]{1,0:T(8,128)(2,1)S(1)} %select_convert_fusion), channel_id=1, source_target_pairs={{1,2},{2,1},{5,6},{6,5},{9,10},{10,9},{13,14},{14,13},{17,18},{18,... | collective-permute-start | bytes 1572872 | tf_op jit(solution)/shard_map/ppermute | solution.py:310
  19.3 2.6 %collective-permute-done.2.refs_0_ = bf16[1024,256]{1,0:T(8,128)(2,1)S(1)} collective-permute-done((bf16[1024,256]{1,0:T(8,128)(2,1)}, bf16[1024,256]{1,0:T(8,128)(2,1)S(1)}, u32[]{:S(2)}, u32[]{:S(2)}) %collective-permute-start.2) | collective-permute-done | bytes 524320 | tf_op jit(solution)/shard_map/ppermute | solution.py:309
  23.0 5.4 %collective-permute-done.5.refs_2_ = bf16[1024,256]{1,0:T(8,128)(2,1)S(1)} collective-permute-done((bf16[1024,256]{1,0:T(8,128)(2,1)}, bf16[1024,256]{1,0:T(8,128)(2,1)S(1)}, u32[]{:S(2)}, u32[]{:S(2)}) %collective-permute-start.5) | collective-permute-done | bytes 524320 | tf_op jit(solution)/shard_map/ppermute | solution.py:310
  30.6 2.9 %shard_map.29 = (bf16[192,1024]{1,0:T(8,128)(2,1)S(1)}, bf16[192,512]{1,0:T(8,128)(2,1)S(1)}, bf16[192,512]{1,0:T(8,128)(2,1)S(1)}, bf16[2,192,512]{2,1,0:T(8,128)(2,1)S(1)}) custom-call(f32[24,2048]{1,0:T(8,128)S(1)} %pad_maximum_fusion.2.pair_ref, f32[24,2048]{1,0:T(8,128)S(1)} %collective-permute-done.1.got_ref), custom_call_target="tpu_custom_call" | custom-call | flops 10000000000 | tf_op jit(solution)/shard_map/pallas_call | solution.py:139
  33.5 4.0 %shard_map.30 = (bf16[2,1024,512]{2,1,0:T(8,128)(2,1)S(1)}, f32[2,256,512]{2,1,0:T(8,128)S(1)}, bf16[2,256,512]{2,1,0:T(8,128)(2,1)S(1)}) custom-call(s32[3]{0:T(128)S(1)} %pad_add_fusion.place_ref, bf16[192,1024]{1,0:T(8,128)(2,1)S(1)} %get-tuple-element.37.coef_ref, bf16[192,512]{1,0:T(8,128)(2,1)S(1)} %get-tuple-element.38.design_ref, f32[1024,512]{1,0:T(8,128)S(1)} %copy-done), custom_call_target="tpu_custom_call" | custom-call | tf_op jit(solution)/shard_map/pallas_call | solution.py:219
  37.6 10.4 %collective-permute-done.3.refs_1_ = bf16[1024,256]{1,0:T(8,128)(2,1)S(1)} collective-permute-done((bf16[1024,256]{1,0:T(8,128)(2,1)S(1)}, bf16[1024,256]{1,0:T(8,128)(2,1)S(1)}, u32[]{:S(2)}, u32[]{:S(2)}) %collective-permute-start.3) | collective-permute-done | bytes 524320 | tf_op jit(solution)/shard_map/ppermute | solution.py:309
  47.9 4.3 %shard_map.31 = (f32[2,256,512]{2,1,0:T(8,128)S(1)}, bf16[2,256,512]{2,1,0:T(8,128)(2,1)S(1)}) custom-call(s32[3]{0:T(128)S(1)} %pad_add_fusion.place_ref, bf16[192,1024]{1,0:T(8,128)(2,1)S(1)} %get-tuple-element.37.coef_ref, bf16[192,512]{1,0:T(8,128)(2,1)S(1)} %get-tuple-element.40.design_ref, bf16[2,1024,512]{2,1,0:T(8,128)(2,1)S(1)} %get-tuple-element.60.terms_ref, ...), custom_call_target="tpu_custom_call" | custom-call | tf_op jit(solution)/shard_map/pallas_call | solution.py:219
  52.3 12.3 %collective-permute-done.4.refs_0_ = bf16[1024,256]{1,0:T(8,128)(2,1)S(1)} collective-permute-done((bf16[1024,256]{1,0:T(8,128)(2,1)S(1)}, bf16[1024,256]{1,0:T(8,128)(2,1)S(1)}, u32[]{:S(2)}, u32[]{:S(2)}) %collective-permute-start.4) | collective-permute-done | bytes 524320 | tf_op jit(solution)/shard_map/ppermute | solution.py:338
  64.6 4.2 %shard_map.32 = (f32[2,2,128,512]{3,2,1,0:T(8,128)S(1)}, bf16[2,2,128,512]{3,2,1,0:T(8,128)(2,1)S(1)}) custom-call(s32[3]{0:T(128)S(1)} %pad_add_fusion.place_ref, bf16[192,1024]{1,0:T(8,128)(2,1)S(1)} %get-tuple-element.37.coef_ref, bf16[2,192,512]{2,1,0:T(8,128)(2,1)S(1)} %get-tuple-element.45.design_ref, ...), custom_call_target="tpu_custom_call" | custom-call | tf_op jit(solution)/shard_map/pallas_call | solution.py:219
  71.1 2.7 %shard_map.33 = (f32[2,128,512]{2,1,0:T(8,128)S(1)}, bf16[2,128,512]{2,1,0:T(8,128)(2,1)S(1)}, bf16[2,128,512]{2,1,0:T(8,128)(2,1)S(1)}, bf16[2,128,512]{2,1,0:T(8,128)(2,1)S(1)}) custom-call(s32[3]{0:T(128)S(1)} %pad_add_fusion.place_ref, f32[2,256,512]{2,1,0:T(8,128)S(1)} %get-tuple-element.39.own_ref, f32[2,256,512]{2,1,0:T(8,128)S(1)} %get-tuple-element.44.near_ref, ...), custom_call_target="tpu_custom_call" | custom-call | tf_op jit(solution)/shard_map/pallas_call | solution.py:245
  77.3 2.2 %collective-permute-done.13.refs_0_ = bf16[1024,128]{1,0:T(8,128)(2,1)S(1)} collective-permute-done((bf16[1024,128]{1,0:T(8,128)(2,1)S(1)}, bf16[1024,128]{1,0:T(8,128)(2,1)S(1)}, u32[]{:S(2)}, u32[]{:S(2)}) %collective-permute-start.13) | collective-permute-done | bytes 262176 | tf_op jit(solution)/shard_map/ppermute | solution.py:338
  81.0 2.9 %shard_map.34 = (f32[2,2,64,512]{3,2,1,0:T(8,128)S(1)}, bf16[2,2,64,512]{3,2,1,0:T(8,128)(2,1)S(1)}) custom-call(s32[3]{0:T(128)S(1)} %pad_add_fusion.place_ref, bf16[192,1024]{1,0:T(8,128)(2,1)S(1)} %get-tuple-element.37.coef_ref, bf16[2,192,512]{2,1,0:T(8,128)(2,1)S(1)} %get-tuple-element.45.design_ref, ...), custom_call_target="tpu_custom_call" | custom-call | tf_op jit(solution)/shard_map/pallas_call | solution.py:219
  84.0 5.0 %collective-permute-done.11.refs_2_ = bf16[2,128,512]{2,1,0:T(8,128)(2,1)S(1)} collective-permute-done((bf16[2,128,512]{2,1,0:T(8,128)(2,1)S(1)}, bf16[2,128,512]{2,1,0:T(8,128)(2,1)S(1)}, u32[]{:S(2)}, u32[]{:S(2)}) %collective-permute-start.11) | collective-permute-done | bytes 262176 | tf_op jit(solution)/shard_map/ppermute | solution.py:353
  89.1 3.4 %collective-permute-done.21.refs_1_ = bf16[1024,128]{1,0:T(8,128)(2,1)S(1)} collective-permute-done((bf16[1024,128]{1,0:T(8,128)(2,1)S(1)}, bf16[1024,128]{1,0:T(8,128)(2,1)S(1)}, u32[]{:S(2)}, u32[]{:S(2)}) %collective-permute-start.21) | collective-permute-done | bytes 262176 | tf_op jit(solution)/shard_map/ppermute | solution.py:339
  92.5 2.3 %collective-permute-done.20.refs_0_ = bf16[1024,128]{1,0:T(8,128)(2,1)S(1)} collective-permute-done((bf16[1024,128]{1,0:T(8,128)(2,1)S(1)}, bf16[1024,128]{1,0:T(8,128)(2,1)S(1)}, u32[]{:S(2)}, u32[]{:S(2)}) %collective-permute-start.20) | collective-permute-done | bytes 262176 | tf_op jit(solution)/shard_map/ppermute | solution.py:338
  94.8 2.9 %shard_map.36 = (f32[2,2,64,512]{3,2,1,0:T(8,128)S(1)}, bf16[2,2,64,512]{3,2,1,0:T(8,128)(2,1)S(1)}) custom-call(s32[3]{0:T(128)S(1)} %pad_add_fusion.place_ref, bf16[192,1024]{1,0:T(8,128)(2,1)S(1)} %get-tuple-element.37.coef_ref, bf16[2,192,512]{2,1,0:T(8,128)(2,1)S(1)} %get-tuple-element.45.design_ref, ...), custom_call_target="tpu_custom_call" | custom-call | tf_op jit(solution)/shard_map/pallas_call | solution.py:219
  109.8 1.8 %collective-permute-done.23.refs_9_ = bf16[2,64,512]{2,1,0:T(8,128)(2,1)S(1)} collective-permute-done((bf16[2,64,512]{2,1,0:T(8,128)(2,1)S(1)}, bf16[2,64,512]{2,1,0:T(8,128)(2,1)S(1)}, u32[]{:S(2)}, u32[]{:S(2)}) %collective-permute-start.23) | collective-permute-done | bytes 131104 | tf_op jit(solution)/shard_map/ppermute | solution.py:353
  111.6 3.3 %collective-permute-done.24.refs_10_ = bf16[2,64,512]{2,1,0:T(8,128)(2,1)S(1)} collective-permute-done((bf16[2,64,512]{2,1,0:T(8,128)(2,1)S(1)}, bf16[2,64,512]{2,1,0:T(8,128)(2,1)S(1)}, u32[]{:S(2)}, u32[]{:S(2)}) %collective-permute-start.24) | collective-permute-done | bytes 131104 | tf_op jit(solution)/shard_map/ppermute | solution.py:353
  114.9 2.2 %shard_map.38 = f32[256,512]{1,0:T(8,128)} custom-call(f32[2,128,512]{2,1,0:T(8,128)S(1)} %get-tuple-element.50.refs_0_, bf16[2,128,512]{2,1,0:T(8,128)(2,1)S(1)} %collective-permute-done.10.refs_1_, bf16[2,128,512]{2,1,0:T(8,128)(2,1)S(1)} %collective-permute-done.11.refs_2_, bf16[2,128,512]{2,1,0:T(8,128)(2,1)S(1)} %collective-permute-done.12.refs_3_, ...), custom_call_target="tpu_custom_call" | custom-call | tf_op jit(solution)/shard_map/pallas_call | solution.py:270
  (61 shorter events, 26.4 us)
Async XLA Ops:
  3.9 9.5 %collective-permute-start = (f32[24,1536]{1,0:T(8,128)}, f32[24,1536]{1,0:T(8,128)S(1)}, u32[]{:S(2)}, u32[]{:S(2)}) collective-permute-start(f32[24,1536]{1,0:T(8,128)} %shard_map.28), channel_id=1, source_target_pairs={{0,1},{1,0},{2,3},{3,2},{4,5},{5,4},{6,7},{7,6},{8,9},{9,8},{10,11... | collective-permute-start | bytes 442376 | tf_op jit(solution)/shard_map/ppermute | solution.py:300
  6.8 15.1 %collective-permute-start.2 = (bf16[1024,256]{1,0:T(8,128)(2,1)}, bf16[1024,256]{1,0:T(8,128)(2,1)S(1)}, u32[]{:S(2)}, u32[]{:S(2)}) collective-permute-start(bf16[1024,256]{1,0:T(8,128)(2,1)} %select_convert_fusion.1), channel_id=1, source_target_pairs={{0,1},{1,0},{2,3},{3,2},{4,5},{5,4},{6,7},{7,6},{8,9},{9,8},{10,11... | collective-permute-start | bytes 1572872 | tf_op jit(solution)/shard_map/ppermute | solution.py:309
  7.3 21.2 %collective-permute-start.5 = (bf16[1024,256]{1,0:T(8,128)(2,1)}, bf16[1024,256]{1,0:T(8,128)(2,1)S(1)}, u32[]{:S(2)}, u32[]{:S(2)}) collective-permute-start(bf16[1024,256]{1,0:T(8,128)(2,1)} %select_convert_fusion.1), channel_id=1, source_target_pairs={{1,2},{2,1},{5,6},{6,5},{9,10},{10,9},{13,14},{14,13},{17,18},{18,... | collective-permute-start | bytes 1572872 | tf_op jit(solution)/shard_map/ppermute | solution.py:310
  13.5 17.1 %collective-permute-start.1 = (f32[24,2048]{1,0:T(8,128)S(1)}, f32[24,2048]{1,0:T(8,128)S(1)}, u32[]{:S(2)}, u32[]{:S(2)}) collective-permute-start(f32[24,2048]{1,0:T(8,128)S(1)} %pad_maximum_fusion.2.pair_ref), channel_id=1, source_target_pairs={{0,2},{1,3},{2,0},{3,1},{4,6},{5,7},{6,4},{7,5},{8,10},{9,11},{10,... | collective-permute-start | bytes 589832 | tf_op jit(solution)/shard_map/ppermute | solution.py:302
  13.9 34.0 %collective-permute-start.3 = (bf16[1024,256]{1,0:T(8,128)(2,1)S(1)}, bf16[1024,256]{1,0:T(8,128)(2,1)S(1)}, u32[]{:S(2)}, u32[]{:S(2)}) collective-permute-start(bf16[1024,256]{1,0:T(8,128)(2,1)S(1)} %select_convert_fusion), channel_id=1, source_target_pairs={{0,1},{1,0},{2,3},{3,2},{4,5},{5,4},{6,7},{7,6},{8,9},{9,8},{10,11... | collective-permute-start | bytes 1572872 | tf_op jit(solution)/shard_map/ppermute | solution.py:309
  17.0 52.5 %collective-permute-start.14 = (bf16[1024,256]{1,0:T(8,128)(2,1)S(1)}, bf16[1024,256]{1,0:T(8,128)(2,1)S(1)}, u32[]{:S(2)}, u32[]{:S(2)}) collective-permute-start(bf16[1024,256]{1,0:T(8,128)(2,1)S(1)} %select_convert_fusion), channel_id=1, source_target_pairs={{1,2},{2,1},{5,6},{6,5},{9,10},{10,9},{13,14},{14,13},{17,18},{18,... | collective-permute-start | bytes 1572872 | tf_op jit(solution)/shard_map/ppermute | solution.py:310
  22.2 42.4 %collective-permute-start.4 = (bf16[1024,256]{1,0:T(8,128)(2,1)S(1)}, bf16[1024,256]{1,0:T(8,128)(2,1)S(1)}, u32[]{:S(2)}, u32[]{:S(2)}) collective-permute-start(bf16[1024,256]{1,0:T(8,128)(2,1)S(1)} %broadcast_select_fusion), channel_id=1, source_target_pairs={{1,2},{2,1},{0,3},{3,0},{5,6},{6,5},{4,7},{7,4},{9,10},{10,9},{8,1... | collective-permute-start | bytes 1572872 | tf_op jit(solution)/shard_map/ppermute | solution.py:338
  28.4 36.2 %collective-permute-start.6 = (bf16[1024,256]{1,0:T(8,128)(2,1)S(1)}, bf16[1024,256]{1,0:T(8,128)(2,1)S(1)}, u32[]{:S(2)}, u32[]{:S(2)}) collective-permute-start(bf16[1024,256]{1,0:T(8,128)(2,1)S(1)} %collective-permute-done.5.refs_2_), channel_id=1, source_target_pairs={{1,0},{2,3},{5,4},{6,7},{9,8},{10,11},{13,12},{14,15},{17,16},{18,... | collective-permute-start | bytes 1572872 | tf_op jit(solution)/shard_map/ppermute | solution.py:339
  37.5 33.5 %collective-permute-start.7 = (bf16[2,256,512]{2,1,0:T(8,128)(2,1)S(1)}, bf16[2,256,512]{2,1,0:T(8,128)(2,1)S(1)}, u32[]{:S(2)}, u32[]{:S(2)}) collective-permute-start(bf16[2,256,512]{2,1,0:T(8,128)(2,1)S(1)} %get-tuple-element.47), channel_id=1, source_target_pairs={{0,4},{4,0},{8,12},{12,8},{16,20},{20,16},{24,28},{28,24},{1,5},{5... | collective-permute-start | bytes 1572872 | tf_op jit(solution)/shard_map/ppermute | solution.py:329
  52.2 18.8 %collective-permute-start.8 = (bf16[2,256,512]{2,1,0:T(8,128)(2,1)S(1)}, bf16[2,256,512]{2,1,0:T(8,128)(2,1)S(1)}, u32[]{:S(2)}, u32[]{:S(2)}) collective-permute-start(bf16[2,256,512]{2,1,0:T(8,128)(2,1)S(1)} %get-tuple-element.48), channel_id=1, source_target_pairs={{0,4},{4,0},{8,12},{12,8},{16,20},{20,16},{24,28},{28,24},{1,5},{5... | collective-permute-start | bytes 1572872 | tf_op jit(solution)/shard_map/ppermute | solution.py:329
  69.0 10.6 %collective-permute-start.13 = (bf16[1024,128]{1,0:T(8,128)(2,1)S(1)}, bf16[1024,128]{1,0:T(8,128)(2,1)S(1)}, u32[]{:S(2)}, u32[]{:S(2)}) collective-permute-start(bf16[1024,128]{1,0:T(8,128)(2,1)S(1)} %get-tuple-element.76), channel_id=1, source_target_pairs={{1,2},{2,1},{0,3},{3,0},{5,6},{6,5},{4,7},{7,4},{9,10},{10,9},{8,1... | collective-permute-start | bytes 786440 | tf_op jit(solution)/shard_map/ppermute | solution.py:338
  69.5 11.3 %collective-permute-start.15 = (bf16[1024,128]{1,0:T(8,128)(2,1)S(1)}, bf16[1024,128]{1,0:T(8,128)(2,1)S(1)}, u32[]{:S(2)}, u32[]{:S(2)}) collective-permute-start(bf16[1024,128]{1,0:T(8,128)(2,1)S(1)} %get-tuple-element.78), channel_id=1, source_target_pairs={{1,0},{2,3},{5,4},{6,7},{9,8},{10,11},{13,12},{14,15},{17,16},{18,... | collective-permute-start | bytes 786440 | tf_op jit(solution)/shard_map/ppermute | solution.py:339
  73.8 10.1 %collective-permute-start.10 = (bf16[2,128,512]{2,1,0:T(8,128)(2,1)S(1)}, bf16[2,128,512]{2,1,0:T(8,128)(2,1)S(1)}, u32[]{:S(2)}, u32[]{:S(2)}) collective-permute-start(bf16[2,128,512]{2,1,0:T(8,128)(2,1)S(1)} %get-tuple-element.51), channel_id=1, source_target_pairs={{0,8},{4,12},{8,0},{12,4},{16,24},{20,28},{24,16},{28,20},{1,9},{5... | collective-permute-start | bytes 786440 | tf_op jit(solution)/shard_map/ppermute | solution.py:353
  75.3 13.8 %collective-permute-start.11 = (bf16[2,128,512]{2,1,0:T(8,128)(2,1)S(1)}, bf16[2,128,512]{2,1,0:T(8,128)(2,1)S(1)}, u32[]{:S(2)}, u32[]{:S(2)}) collective-permute-start(bf16[2,128,512]{2,1,0:T(8,128)(2,1)S(1)} %get-tuple-element.52), channel_id=1, source_target_pairs={{0,16},{4,20},{8,24},{12,28},{16,0},{20,4},{24,8},{28,12},{1,17},{... | collective-permute-start | bytes 786440 | tf_op jit(solution)/shard_map/ppermute | solution.py:353
  76.9 12.2 %collective-permute-start.12 = (bf16[2,128,512]{2,1,0:T(8,128)(2,1)S(1)}, bf16[2,128,512]{2,1,0:T(8,128)(2,1)S(1)}, u32[]{:S(2)}, u32[]{:S(2)}) collective-permute-start(bf16[2,128,512]{2,1,0:T(8,128)(2,1)S(1)} %get-tuple-element.53), channel_id=1, source_target_pairs={{0,24},{4,28},{8,16},{12,20},{16,8},{20,12},{24,0},{28,4},{1,25},{... | collective-permute-start | bytes 786440 | tf_op jit(solution)/shard_map/ppermute | solution.py:353
  79.6 13.0 %collective-permute-start.21 = (bf16[1024,128]{1,0:T(8,128)(2,1)S(1)}, bf16[1024,128]{1,0:T(8,128)(2,1)S(1)}, u32[]{:S(2)}, u32[]{:S(2)}) collective-permute-start(bf16[1024,128]{1,0:T(8,128)(2,1)S(1)} %get-tuple-element.62), channel_id=1, source_target_pairs={{1,0},{2,3},{5,4},{6,7},{9,8},{10,11},{13,12},{14,15},{17,16},{18,... | collective-permute-start | bytes 786440 | tf_op jit(solution)/shard_map/ppermute | solution.py:339
  80.9 14.0 %collective-permute-start.20 = (bf16[1024,128]{1,0:T(8,128)(2,1)S(1)}, bf16[1024,128]{1,0:T(8,128)(2,1)S(1)}, u32[]{:S(2)}, u32[]{:S(2)}) collective-permute-start(bf16[1024,128]{1,0:T(8,128)(2,1)S(1)} %get-tuple-element.61), channel_id=1, source_target_pairs={{1,2},{2,1},{0,3},{3,0},{5,6},{6,5},{4,7},{7,4},{9,10},{10,9},{8,1... | collective-permute-start | bytes 786440 | tf_op jit(solution)/shard_map/ppermute | solution.py:338
  83.9 14.0 %collective-permute-start.16 = (bf16[2,2,64,512]{3,2,1,0:T(8,128)(2,1)S(1)}, bf16[2,2,64,512]{3,2,1,0:T(8,128)(2,1)S(1)}, u32[]{:S(2)}, u32[]{:S(2)}) collective-permute-start(bf16[2,2,64,512]{3,2,1,0:T(8,128)(2,1)S(1)} %get-tuple-element.55), channel_id=1, source_target_pairs={{0,4},{4,0},{8,12},{12,8},{16,20},{20,16},{24,28},{28,24},{1,5},{5... | collective-permute-start | bytes 786440 | tf_op jit(solution)/shard_map/ppermute | solution.py:347
  99.3 8.1 %collective-permute-start.17 = (bf16[2,64,512]{2,1,0:T(8,128)(2,1)S(1)}, bf16[2,64,512]{2,1,0:T(8,128)(2,1)S(1)}, u32[]{:S(2)}, u32[]{:S(2)}) collective-permute-start(bf16[2,64,512]{2,1,0:T(8,128)(2,1)S(1)} %get-tuple-element.57), channel_id=1, source_target_pairs={{0,8},{4,12},{8,0},{12,4},{16,24},{20,28},{24,16},{28,20},{1,9},{5... | collective-permute-start | bytes 393224 | tf_op jit(solution)/shard_map/ppermute | solution.py:353
  100.9 8.2 %collective-permute-start.18 = (bf16[2,64,512]{2,1,0:T(8,128)(2,1)S(1)}, bf16[2,64,512]{2,1,0:T(8,128)(2,1)S(1)}, u32[]{:S(2)}, u32[]{:S(2)}) collective-permute-start(bf16[2,64,512]{2,1,0:T(8,128)(2,1)S(1)} %get-tuple-element.58), channel_id=1, source_target_pairs={{0,16},{4,20},{8,24},{12,28},{16,0},{20,4},{24,8},{28,12},{1,17},{... | collective-permute-start | bytes 393224 | tf_op jit(solution)/shard_map/ppermute | solution.py:353
  102.4 7.4 %collective-permute-start.19 = (bf16[2,64,512]{2,1,0:T(8,128)(2,1)S(1)}, bf16[2,64,512]{2,1,0:T(8,128)(2,1)S(1)}, u32[]{:S(2)}, u32[]{:S(2)}) collective-permute-start(bf16[2,64,512]{2,1,0:T(8,128)(2,1)S(1)} %get-tuple-element.59), channel_id=1, source_target_pairs={{0,24},{4,28},{8,16},{12,20},{16,8},{20,12},{24,0},{28,4},{1,25},{... | collective-permute-start | bytes 393224 | tf_op jit(solution)/shard_map/ppermute | solution.py:353
  104.3 7.3 %collective-permute-start.23 = (bf16[2,64,512]{2,1,0:T(8,128)(2,1)S(1)}, bf16[2,64,512]{2,1,0:T(8,128)(2,1)S(1)}, u32[]{:S(2)}, u32[]{:S(2)}) collective-permute-start(bf16[2,64,512]{2,1,0:T(8,128)(2,1)S(1)} %get-tuple-element.66), channel_id=1, source_target_pairs={{0,8},{4,12},{8,0},{12,4},{16,24},{20,28},{24,16},{28,20},{1,9},{5... | collective-permute-start | bytes 393224 | tf_op jit(solution)/shard_map/ppermute | solution.py:353
  105.8 9.1 %collective-permute-start.24 = (bf16[2,64,512]{2,1,0:T(8,128)(2,1)S(1)}, bf16[2,64,512]{2,1,0:T(8,128)(2,1)S(1)}, u32[]{:S(2)}, u32[]{:S(2)}) collective-permute-start(bf16[2,64,512]{2,1,0:T(8,128)(2,1)S(1)} %get-tuple-element.67), channel_id=1, source_target_pairs={{0,16},{4,20},{8,24},{12,28},{16,0},{20,4},{24,8},{28,12},{1,17},{... | collective-permute-start | bytes 393224 | tf_op jit(solution)/shard_map/ppermute | solution.py:353
  107.3 7.6 %collective-permute-start.25 = (bf16[2,64,512]{2,1,0:T(8,128)(2,1)S(1)}, bf16[2,64,512]{2,1,0:T(8,128)(2,1)S(1)}, u32[]{:S(2)}, u32[]{:S(2)}) collective-permute-start(bf16[2,64,512]{2,1,0:T(8,128)(2,1)S(1)} %get-tuple-element.68), channel_id=1, source_target_pairs={{0,24},{4,28},{8,16},{12,20},{16,8},{20,12},{24,0},{28,4},{1,25},{... | collective-permute-start | bytes 393224 | tf_op jit(solution)/shard_map/ppermute | solution.py:353
  (6 other events, 26.2 us)

commit v7 on v6

--- a/solution.py
+++ b/solution.py
@@ -255,6 +255,7 @@
 
 def divide_kernel(*refs):
     *parts, out_ref = refs
+    parts = parts[len(parts) % 4:]
     first = 0
     for p in range(len(parts) // 4):
         mine, *got = parts[4 * p:4 * p + 4]
@@ -264,17 +265,18 @@
         first += count
 
 
-def divide(parts):
-    width = parts[0].shape[2]
-    vmem = pl.BlockSpec(memory_space=pltpu.VMEM)
+def divide(parts, rows, first, before=()):
+    count, width = sum(m.shape[1] for m in parts[::4]), parts[0].shape[2]
     return pl.pallas_call(
         divide_kernel,
-        out_shape=jax.ShapeDtypeStruct((sum(m.shape[1] for m in parts[::4]), width), jnp.float32),
-        in_specs=[vmem] * len(parts),
-        out_specs=vmem,
+        grid=(1,),
+        out_shape=jax.ShapeDtypeStruct((rows, width), jnp.float32),
+        in_specs=[pl.BlockSpec(memory_space=pl.ANY) for _ in before] + [pl.BlockSpec(x.shape, lambda i: (0, 0, 0)) for x in parts],
+        out_specs=pl.BlockSpec((count, width), lambda i: (first // count, 0)),
+        input_output_aliases={0: 0} if before else {},
         compiler_params=pltpu.CompilerParams(vmem_limit_bytes=VMEM_BYTES),
         cost_estimate=FREE,
-    )(*parts)
+    )(*before, *parts)
 
 
 def kinship(sums):
@@ -351,7 +353,8 @@
         totals.append(kept)
         for d in range(1, 4):
             totals.append(lax.ppermute(sent[d - 1], "snp", [(i, i ^ (2 * d)) for i in range(8)]))
-    return divide(totals)
+    most = divide(totals[:-4], half, 0)
+    return divide(totals[-4:], half, cuts[-1][0], (most,))
 
 
 def any_mesh(genotypes, pcs):

time: 118 us -> 116 us (0.983)
  waiting for transfers between devices: 51.4 us -> 49.6 us
    ppermute x9, waiting for transfers between devices: 11.9 us -> 10.1 us  [line_of_four(): lax.ppermute(sent[d - 1], 'snp', [(i, i ^ 2 * d) for i in range(8)])]
    pallas_call x1 -> x2, Pallas kernels: 2.19 us -> 2.82 us  [divide(): pl.pallas_call(divide_kernel, grid=(1,), out_shape=jax.ShapeDtypeStruct((...]
  transfers between devices with their start and end apart: 26 -> 26, of which waited for: 13 -> 13; matrix products, arithmetic and copies ran while one was open for 5% -> 5% of each run, Pallas kernels for 23% -> 25%
where the time goes in v7:
time: 116 us
  waiting for transfers between devices  49.6 us (43%)
  Pallas kernels  33.5 us (29%)
  starting transfers between devices  26.7 us (23%)
  other arithmetic  4.05 us (3%)
  local copies, waits for them, and re-layouts  1.77 us (2%)
    pallas_call x5, Pallas kernels, block_sums(): pl.pallas_call(kernel, out_shape=out, in_specs=[pl.BlockSpec(memory_space...  18.3 us
    ppermute x3, waiting for transfers between devices, line_of_four(): far = lax.ppermute(ready, 'samp', [(1, 2), (2, 1), (0, 3), (3, 0)])  16.8 us
    ppermute x2, waiting for transfers between devices, line_of_four(): lax.ppermute(c, 'samp', [(i, i ^ 1) for i in range(4)])  12.9 us
    ppermute x9, starting transfers between devices, line_of_four(): lax.ppermute(sent[d - 1], 'snp', [(i, i ^ 2 * d) for i in range(8)])  10.9 us
    ppermute x9, waiting for transfers between devices, line_of_four(): lax.ppermute(sent[d - 1], 'snp', [(i, i ^ 2 * d) for i in range(8)])  10.1 us
    pallas_call x3, Pallas kernels, add_cores(): pl.pallas_call(functools.partial(add_kernel, first), out_shape=(jax.Shape...  5.61 us
    ppermute x2, waiting for transfers between devices, line_of_four(): across = [lax.ppermute(c, 'samp', [(1, 2), (2, 1)]) for c in coded]  5.45 us
    ppermute x2, starting transfers between devices, line_of_four(): across = [lax.ppermute(c, 'samp', [(1, 2), (2, 1)]) for c in coded]  4.69 us
  transfers between devices with their start and end apart: 26, of which 13 were waited for; matrix products, arithmetic and copies ran while one was open for 5% of the time, Pallas kernels for 25%

profile of v7, /device:TPU:16, one launch (start us, length us, event | category | flops | bytes accessed | tf_op | source)
XLA Modules:
  0.0 115.9 jit_solution(4901943861735275639)
XLA Ops:
  0.0 3.9 %shard_map.28 = f32[24,1536]{1,0:T(8,128)} custom-call(f32[1024,512]{1,0:T(8,128)} %own_ref.1, f32[20,512]{1,0:T(8,128)} %pcs_ref.1), custom_call_target="tpu_custom_call" | custom-call | tf_op jit(solution)/shard_map/pallas_call | solution.py:94
  3.9 1.6 %collective-permute-start = (f32[24,1536]{1,0:T(8,128)}, f32[24,1536]{1,0:T(8,128)S(1)}, u32[]{:S(2)}, u32[]{:S(2)}) collective-permute-start(f32[24,1536]{1,0:T(8,128)} %shard_map.28), channel_id=1, source_target_pairs={{0,1},{1,0},{2,3},{3,2},{4,5},{5,4},{6,7},{7,6},{8,9},{9,8},{10,11... | collective-permute-start | bytes 442376 | tf_op jit(solution)/shard_map/ppermute | solution.py:302
  7.3 2.3 %collective-permute-start.5 = (bf16[1024,256]{1,0:T(8,128)(2,1)}, bf16[1024,256]{1,0:T(8,128)(2,1)S(1)}, u32[]{:S(2)}, u32[]{:S(2)}) collective-permute-start(bf16[1024,256]{1,0:T(8,128)(2,1)} %select_convert_fusion.1), channel_id=1, source_target_pairs={{1,2},{2,1},{5,6},{6,5},{9,10},{10,9},{13,14},{14,13},{17,18},{18,... | collective-permute-start | bytes 1572872 | tf_op jit(solution)/shard_map/ppermute | solution.py:312
  9.6 1.6 %fusion = (f32[1024,64]{1,0:T(8,128)}, f32[1024,64]{1,0:T(8,128)}, f32[1024,64]{1,0:T(8,128)}, f32[1024,64]{1,0:T(8,128)}) fusion(f32[1024,512]{1,0:T(8,128)S(1)} %copy-done), kind=kLoop, calls=%fused_computation.10 | loop fusion | bytes 2097152 | tf_op jit(solution)/shard_map/slice | solution.py:309
  11.4 2.1 %pad_maximum_fusion.1 = f32[1024,256]{1,0:T(8,128)S(1)} fusion(f32[1024,64]{1,0:T(8,128)} %get-tuple-element.71, f32[1024,64]{1,0:T(8,128)} %get-tuple-element.72, f32[1024,64]{1,0:T(8,128)} %get-tuple-element.70, f32[1024,64]{1,0:T(8,128)} %get-tuple-element.69), kind=kLoop, calls=%fused_computation.1 | loop fusion | flops 786432 | bytes 2097152 | tf_op jit(solution)/shard_map/concatenate | solution.py:310
  13.9 3.1 %collective-permute-start.3 = (bf16[1024,256]{1,0:T(8,128)(2,1)S(1)}, bf16[1024,256]{1,0:T(8,128)(2,1)S(1)}, u32[]{:S(2)}, u32[]{:S(2)}) collective-permute-start(bf16[1024,256]{1,0:T(8,128)(2,1)S(1)} %select_convert_fusion), channel_id=1, source_target_pairs={{0,1},{1,0},{2,3},{3,2},{4,5},{5,4},{6,7},{7,6},{8,9},{9,8},{10,11... | collective-permute-start | bytes 1572872 | tf_op jit(solution)/shard_map/ppermute | solution.py:311
  17.0 2.3 %collective-permute-start.14 = (bf16[1024,256]{1,0:T(8,128)(2,1)S(1)}, bf16[1024,256]{1,0:T(8,128)(2,1)S(1)}, u32[]{:S(2)}, u32[]{:S(2)}) collective-permute-start(bf16[1024,256]{1,0:T(8,128)(2,1)S(1)} %select_convert_fusion), channel_id=1, source_target_pairs={{1,2},{2,1},{5,6},{6,5},{9,10},{10,9},{13,14},{14,13},{17,18},{18,... | collective-permute-start | bytes 1572872 | tf_op jit(solution)/shard_map/ppermute | solution.py:312
  19.3 2.6 %collective-permute-done.2.refs_0_ = bf16[1024,256]{1,0:T(8,128)(2,1)S(1)} collective-permute-done((bf16[1024,256]{1,0:T(8,128)(2,1)}, bf16[1024,256]{1,0:T(8,128)(2,1)S(1)}, u32[]{:S(2)}, u32[]{:S(2)}) %collective-permute-start.2) | collective-permute-done | bytes 524320 | tf_op jit(solution)/shard_map/ppermute | solution.py:311
  23.0 5.4 %collective-permute-done.5.refs_2_ = bf16[1024,256]{1,0:T(8,128)(2,1)S(1)} collective-permute-done((bf16[1024,256]{1,0:T(8,128)(2,1)}, bf16[1024,256]{1,0:T(8,128)(2,1)S(1)}, u32[]{:S(2)}, u32[]{:S(2)}) %collective-permute-start.5) | collective-permute-done | bytes 524320 | tf_op jit(solution)/shard_map/ppermute | solution.py:312
  30.6 2.9 %shard_map.29 = (bf16[192,1024]{1,0:T(8,128)(2,1)S(1)}, bf16[192,512]{1,0:T(8,128)(2,1)S(1)}, bf16[192,512]{1,0:T(8,128)(2,1)S(1)}, bf16[2,192,512]{2,1,0:T(8,128)(2,1)S(1)}) custom-call(f32[24,2048]{1,0:T(8,128)S(1)} %pad_maximum_fusion.2.pair_ref, f32[24,2048]{1,0:T(8,128)S(1)} %collective-permute-done.1.got_ref), custom_call_target="tpu_custom_call" | custom-call | flops 10000000000 | tf_op jit(solution)/shard_map/pallas_call | solution.py:139
  33.5 4.0 %shard_map.30 = (bf16[2,1024,512]{2,1,0:T(8,128)(2,1)S(1)}, f32[2,256,512]{2,1,0:T(8,128)S(1)}, bf16[2,256,512]{2,1,0:T(8,128)(2,1)S(1)}) custom-call(s32[3]{0:T(128)S(1)} %pad_add_fusion.place_ref, bf16[192,1024]{1,0:T(8,128)(2,1)S(1)} %get-tuple-element.37.coef_ref, bf16[192,512]{1,0:T(8,128)(2,1)S(1)} %get-tuple-element.38.design_ref, f32[1024,512]{1,0:T(8,128)S(1)} %copy-done), custom_call_target="tpu_custom_call" | custom-call | tf_op jit(solution)/shard_map/pallas_call | solution.py:219
  37.6 10.4 %collective-permute-done.3.refs_1_ = bf16[1024,256]{1,0:T(8,128)(2,1)S(1)} collective-permute-done((bf16[1024,256]{1,0:T(8,128)(2,1)S(1)}, bf16[1024,256]{1,0:T(8,128)(2,1)S(1)}, u32[]{:S(2)}, u32[]{:S(2)}) %collective-permute-start.3) | collective-permute-done | bytes 524320 | tf_op jit(solution)/shard_map/ppermute | solution.py:311
  47.9 4.3 %shard_map.31 = (f32[2,256,512]{2,1,0:T(8,128)S(1)}, bf16[2,256,512]{2,1,0:T(8,128)(2,1)S(1)}) custom-call(s32[3]{0:T(128)S(1)} %pad_add_fusion.place_ref, bf16[192,1024]{1,0:T(8,128)(2,1)S(1)} %get-tuple-element.37.coef_ref, bf16[192,512]{1,0:T(8,128)(2,1)S(1)} %get-tuple-element.40.design_ref, bf16[2,1024,512]{2,1,0:T(8,128)(2,1)S(1)} %get-tuple-element.60.terms_ref, ...), custom_call_target="tpu_custom_call" | custom-call | tf_op jit(solution)/shard_map/pallas_call | solution.py:219
  52.3 12.3 %collective-permute-done.4.refs_0_ = bf16[1024,256]{1,0:T(8,128)(2,1)S(1)} collective-permute-done((bf16[1024,256]{1,0:T(8,128)(2,1)S(1)}, bf16[1024,256]{1,0:T(8,128)(2,1)S(1)}, u32[]{:S(2)}, u32[]{:S(2)}) %collective-permute-start.4) | collective-permute-done | bytes 524320 | tf_op jit(solution)/shard_map/ppermute | solution.py:340
  64.6 4.2 %shard_map.32 = (f32[2,2,128,512]{3,2,1,0:T(8,128)S(1)}, bf16[2,2,128,512]{3,2,1,0:T(8,128)(2,1)S(1)}) custom-call(s32[3]{0:T(128)S(1)} %pad_add_fusion.place_ref, bf16[192,1024]{1,0:T(8,128)(2,1)S(1)} %get-tuple-element.37.coef_ref, bf16[2,192,512]{2,1,0:T(8,128)(2,1)S(1)} %get-tuple-element.45.design_ref, ...), custom_call_target="tpu_custom_call" | custom-call | tf_op jit(solution)/shard_map/pallas_call | solution.py:219
  71.0 2.8 %shard_map.33 = (f32[2,128,512]{2,1,0:T(8,128)S(1)}, bf16[2,128,512]{2,1,0:T(8,128)(2,1)S(1)}, bf16[2,128,512]{2,1,0:T(8,128)(2,1)S(1)}, bf16[2,128,512]{2,1,0:T(8,128)(2,1)S(1)}) custom-call(s32[3]{0:T(128)S(1)} %pad_add_fusion.place_ref, f32[2,256,512]{2,1,0:T(8,128)S(1)} %get-tuple-element.39.own_ref, f32[2,256,512]{2,1,0:T(8,128)S(1)} %get-tuple-element.44.near_ref, ...), custom_call_target="tpu_custom_call" | custom-call | tf_op jit(solution)/shard_map/pallas_call | solution.py:245
  77.4 2.2 %collective-permute-done.13.refs_0_ = bf16[1024,128]{1,0:T(8,128)(2,1)S(1)} collective-permute-done((bf16[1024,128]{1,0:T(8,128)(2,1)S(1)}, bf16[1024,128]{1,0:T(8,128)(2,1)S(1)}, u32[]{:S(2)}, u32[]{:S(2)}) %collective-permute-start.13) | collective-permute-done | bytes 262176 | tf_op jit(solution)/shard_map/ppermute | solution.py:340
  81.0 2.9 %shard_map.34 = (f32[2,2,64,512]{3,2,1,0:T(8,128)S(1)}, bf16[2,2,64,512]{3,2,1,0:T(8,128)(2,1)S(1)}) custom-call(s32[3]{0:T(128)S(1)} %pad_add_fusion.place_ref, bf16[192,1024]{1,0:T(8,128)(2,1)S(1)} %get-tuple-element.37.coef_ref, bf16[2,192,512]{2,1,0:T(8,128)(2,1)S(1)} %get-tuple-element.45.design_ref, ...), custom_call_target="tpu_custom_call" | custom-call | tf_op jit(solution)/shard_map/pallas_call | solution.py:219
  84.0 5.1 %collective-permute-done.11.refs_2_ = bf16[2,128,512]{2,1,0:T(8,128)(2,1)S(1)} collective-permute-done((bf16[2,128,512]{2,1,0:T(8,128)(2,1)S(1)}, bf16[2,128,512]{2,1,0:T(8,128)(2,1)S(1)}, u32[]{:S(2)}, u32[]{:S(2)}) %collective-permute-start.11) | collective-permute-done | bytes 262176 | tf_op jit(solution)/shard_map/ppermute | solution.py:355
  89.1 3.4 %collective-permute-done.21.refs_1_ = bf16[1024,128]{1,0:T(8,128)(2,1)S(1)} collective-permute-done((bf16[1024,128]{1,0:T(8,128)(2,1)S(1)}, bf16[1024,128]{1,0:T(8,128)(2,1)S(1)}, u32[]{:S(2)}, u32[]{:S(2)}) %collective-permute-start.21) | collective-permute-done | bytes 262176 | tf_op jit(solution)/shard_map/ppermute | solution.py:341
  92.5 2.3 %collective-permute-done.20.refs_0_ = bf16[1024,128]{1,0:T(8,128)(2,1)S(1)} collective-permute-done((bf16[1024,128]{1,0:T(8,128)(2,1)S(1)}, bf16[1024,128]{1,0:T(8,128)(2,1)S(1)}, u32[]{:S(2)}, u32[]{:S(2)}) %collective-permute-start.20) | collective-permute-done | bytes 262176 | tf_op jit(solution)/shard_map/ppermute | solution.py:340
  94.8 2.9 %shard_map.37 = (f32[2,2,64,512]{3,2,1,0:T(8,128)S(1)}, bf16[2,2,64,512]{3,2,1,0:T(8,128)(2,1)S(1)}) custom-call(s32[3]{0:T(128)S(1)} %pad_add_fusion.place_ref, bf16[192,1024]{1,0:T(8,128)(2,1)S(1)} %get-tuple-element.37.coef_ref, bf16[2,192,512]{2,1,0:T(8,128)(2,1)S(1)} %get-tuple-element.45.design_ref, ...), custom_call_target="tpu_custom_call" | custom-call | tf_op jit(solution)/shard_map/pallas_call | solution.py:219
  109.8 1.8 %shard_map.36.refs_0_ = f32[256,512]{1,0:T(8,128)} custom-call(f32[2,128,512]{2,1,0:T(8,128)S(1)} %get-tuple-element.50.refs_0_, bf16[2,128,512]{2,1,0:T(8,128)(2,1)S(1)} %collective-permute-done.10.refs_1_, bf16[2,128,512]{2,1,0:T(8,128)(2,1)S(1)} %collective-permute-done.11.refs_2_, bf16[2,128,512]{2,1,0:T(8,128)(2,1)S(1)} %collective-permute-done.12.refs_3_, ...), custom_call_target="tpu_custom_call" | custom-call | tf_op jit(solution)/shard_map/pallas_call | solution.py:270
  111.6 3.3 %collective-permute-done.24.refs_3_ = bf16[2,64,512]{2,1,0:T(8,128)(2,1)S(1)} collective-permute-done((bf16[2,64,512]{2,1,0:T(8,128)(2,1)S(1)}, bf16[2,64,512]{2,1,0:T(8,128)(2,1)S(1)}, u32[]{:S(2)}, u32[]{:S(2)}) %collective-permute-start.24) | collective-permute-done | bytes 131104 | tf_op jit(solution)/shard_map/ppermute | solution.py:355
  (62 shorter events, 25.9 us)
Async XLA Ops:
  3.9 9.5 %collective-permute-start = (f32[24,1536]{1,0:T(8,128)}, f32[24,1536]{1,0:T(8,128)S(1)}, u32[]{:S(2)}, u32[]{:S(2)}) collective-permute-start(f32[24,1536]{1,0:T(8,128)} %shard_map.28), channel_id=1, source_target_pairs={{0,1},{1,0},{2,3},{3,2},{4,5},{5,4},{6,7},{7,6},{8,9},{9,8},{10,11... | collective-permute-start | bytes 442376 | tf_op jit(solution)/shard_map/ppermute | solution.py:302
  6.8 15.1 %collective-permute-start.2 = (bf16[1024,256]{1,0:T(8,128)(2,1)}, bf16[1024,256]{1,0:T(8,128)(2,1)S(1)}, u32[]{:S(2)}, u32[]{:S(2)}) collective-permute-start(bf16[1024,256]{1,0:T(8,128)(2,1)} %select_convert_fusion.1), channel_id=1, source_target_pairs={{0,1},{1,0},{2,3},{3,2},{4,5},{5,4},{6,7},{7,6},{8,9},{9,8},{10,11... | collective-permute-start | bytes 1572872 | tf_op jit(solution)/shard_map/ppermute | solution.py:311
  7.3 21.2 %collective-permute-start.5 = (bf16[1024,256]{1,0:T(8,128)(2,1)}, bf16[1024,256]{1,0:T(8,128)(2,1)S(1)}, u32[]{:S(2)}, u32[]{:S(2)}) collective-permute-start(bf16[1024,256]{1,0:T(8,128)(2,1)} %select_convert_fusion.1), channel_id=1, source_target_pairs={{1,2},{2,1},{5,6},{6,5},{9,10},{10,9},{13,14},{14,13},{17,18},{18,... | collective-permute-start | bytes 1572872 | tf_op jit(solution)/shard_map/ppermute | solution.py:312
  13.5 17.1 %collective-permute-start.1 = (f32[24,2048]{1,0:T(8,128)S(1)}, f32[24,2048]{1,0:T(8,128)S(1)}, u32[]{:S(2)}, u32[]{:S(2)}) collective-permute-start(f32[24,2048]{1,0:T(8,128)S(1)} %pad_maximum_fusion.2.pair_ref), channel_id=1, source_target_pairs={{0,2},{1,3},{2,0},{3,1},{4,6},{5,7},{6,4},{7,5},{8,10},{9,11},{10,... | collective-permute-start | bytes 589832 | tf_op jit(solution)/shard_map/ppermute | solution.py:304
  13.9 34.0 %collective-permute-start.3 = (bf16[1024,256]{1,0:T(8,128)(2,1)S(1)}, bf16[1024,256]{1,0:T(8,128)(2,1)S(1)}, u32[]{:S(2)}, u32[]{:S(2)}) collective-permute-start(bf16[1024,256]{1,0:T(8,128)(2,1)S(1)} %select_convert_fusion), channel_id=1, source_target_pairs={{0,1},{1,0},{2,3},{3,2},{4,5},{5,4},{6,7},{7,6},{8,9},{9,8},{10,11... | collective-permute-start | bytes 1572872 | tf_op jit(solution)/shard_map/ppermute | solution.py:311
  17.0 52.5 %collective-permute-start.14 = (bf16[1024,256]{1,0:T(8,128)(2,1)S(1)}, bf16[1024,256]{1,0:T(8,128)(2,1)S(1)}, u32[]{:S(2)}, u32[]{:S(2)}) collective-permute-start(bf16[1024,256]{1,0:T(8,128)(2,1)S(1)} %select_convert_fusion), channel_id=1, source_target_pairs={{1,2},{2,1},{5,6},{6,5},{9,10},{10,9},{13,14},{14,13},{17,18},{18,... | collective-permute-start | bytes 1572872 | tf_op jit(solution)/shard_map/ppermute | solution.py:312
  22.2 42.4 %collective-permute-start.4 = (bf16[1024,256]{1,0:T(8,128)(2,1)S(1)}, bf16[1024,256]{1,0:T(8,128)(2,1)S(1)}, u32[]{:S(2)}, u32[]{:S(2)}) collective-permute-start(bf16[1024,256]{1,0:T(8,128)(2,1)S(1)} %broadcast_select_fusion), channel_id=1, source_target_pairs={{1,2},{2,1},{0,3},{3,0},{5,6},{6,5},{4,7},{7,4},{9,10},{10,9},{8,1... | collective-permute-start | bytes 1572872 | tf_op jit(solution)/shard_map/ppermute | solution.py:340
  28.4 36.2 %collective-permute-start.6 = (bf16[1024,256]{1,0:T(8,128)(2,1)S(1)}, bf16[1024,256]{1,0:T(8,128)(2,1)S(1)}, u32[]{:S(2)}, u32[]{:S(2)}) collective-permute-start(bf16[1024,256]{1,0:T(8,128)(2,1)S(1)} %collective-permute-done.5.refs_2_), channel_id=1, source_target_pairs={{1,0},{2,3},{5,4},{6,7},{9,8},{10,11},{13,12},{14,15},{17,16},{18,... | collective-permute-start | bytes 1572872 | tf_op jit(solution)/shard_map/ppermute | solution.py:341
  37.5 33.5 %collective-permute-start.7 = (bf16[2,256,512]{2,1,0:T(8,128)(2,1)S(1)}, bf16[2,256,512]{2,1,0:T(8,128)(2,1)S(1)}, u32[]{:S(2)}, u32[]{:S(2)}) collective-permute-start(bf16[2,256,512]{2,1,0:T(8,128)(2,1)S(1)} %get-tuple-element.47), channel_id=1, source_target_pairs={{0,4},{4,0},{8,12},{12,8},{16,20},{20,16},{24,28},{28,24},{1,5},{5... | collective-permute-start | bytes 1572872 | tf_op jit(solution)/shard_map/ppermute | solution.py:331
  52.2 18.8 %collective-permute-start.8 = (bf16[2,256,512]{2,1,0:T(8,128)(2,1)S(1)}, bf16[2,256,512]{2,1,0:T(8,128)(2,1)S(1)}, u32[]{:S(2)}, u32[]{:S(2)}) collective-permute-start(bf16[2,256,512]{2,1,0:T(8,128)(2,1)S(1)} %get-tuple-element.48), channel_id=1, source_target_pairs={{0,4},{4,0},{8,12},{12,8},{16,20},{20,16},{24,28},{28,24},{1,5},{5... | collective-permute-start | bytes 1572872 | tf_op jit(solution)/shard_map/ppermute | solution.py:331
  69.0 10.6 %collective-permute-start.13 = (bf16[1024,128]{1,0:T(8,128)(2,1)S(1)}, bf16[1024,128]{1,0:T(8,128)(2,1)S(1)}, u32[]{:S(2)}, u32[]{:S(2)}) collective-permute-start(bf16[1024,128]{1,0:T(8,128)(2,1)S(1)} %get-tuple-element.76), channel_id=1, source_target_pairs={{1,2},{2,1},{0,3},{3,0},{5,6},{6,5},{4,7},{7,4},{9,10},{10,9},{8,1... | collective-permute-start | bytes 786440 | tf_op jit(solution)/shard_map/ppermute | solution.py:340
  69.5 11.3 %collective-permute-start.15 = (bf16[1024,128]{1,0:T(8,128)(2,1)S(1)}, bf16[1024,128]{1,0:T(8,128)(2,1)S(1)}, u32[]{:S(2)}, u32[]{:S(2)}) collective-permute-start(bf16[1024,128]{1,0:T(8,128)(2,1)S(1)} %get-tuple-element.78), channel_id=1, source_target_pairs={{1,0},{2,3},{5,4},{6,7},{9,8},{10,11},{13,12},{14,15},{17,16},{18,... | collective-permute-start | bytes 786440 | tf_op jit(solution)/shard_map/ppermute | solution.py:341
  73.8 10.1 %collective-permute-start.10 = (bf16[2,128,512]{2,1,0:T(8,128)(2,1)S(1)}, bf16[2,128,512]{2,1,0:T(8,128)(2,1)S(1)}, u32[]{:S(2)}, u32[]{:S(2)}) collective-permute-start(bf16[2,128,512]{2,1,0:T(8,128)(2,1)S(1)} %get-tuple-element.51), channel_id=1, source_target_pairs={{0,8},{4,12},{8,0},{12,4},{16,24},{20,28},{24,16},{28,20},{1,9},{5... | collective-permute-start | bytes 786440 | tf_op jit(solution)/shard_map/ppermute | solution.py:355
  75.4 13.8 %collective-permute-start.11 = (bf16[2,128,512]{2,1,0:T(8,128)(2,1)S(1)}, bf16[2,128,512]{2,1,0:T(8,128)(2,1)S(1)}, u32[]{:S(2)}, u32[]{:S(2)}) collective-permute-start(bf16[2,128,512]{2,1,0:T(8,128)(2,1)S(1)} %get-tuple-element.52), channel_id=1, source_target_pairs={{0,16},{4,20},{8,24},{12,28},{16,0},{20,4},{24,8},{28,12},{1,17},{... | collective-permute-start | bytes 786440 | tf_op jit(solution)/shard_map/ppermute | solution.py:355
  76.9 12.2 %collective-permute-start.12 = (bf16[2,128,512]{2,1,0:T(8,128)(2,1)S(1)}, bf16[2,128,512]{2,1,0:T(8,128)(2,1)S(1)}, u32[]{:S(2)}, u32[]{:S(2)}) collective-permute-start(bf16[2,128,512]{2,1,0:T(8,128)(2,1)S(1)} %get-tuple-element.53), channel_id=1, source_target_pairs={{0,24},{4,28},{8,16},{12,20},{16,8},{20,12},{24,0},{28,4},{1,25},{... | collective-permute-start | bytes 786440 | tf_op jit(solution)/shard_map/ppermute | solution.py:355
  79.6 13.0 %collective-permute-start.21 = (bf16[1024,128]{1,0:T(8,128)(2,1)S(1)}, bf16[1024,128]{1,0:T(8,128)(2,1)S(1)}, u32[]{:S(2)}, u32[]{:S(2)}) collective-permute-start(bf16[1024,128]{1,0:T(8,128)(2,1)S(1)} %get-tuple-element.62), channel_id=1, source_target_pairs={{1,0},{2,3},{5,4},{6,7},{9,8},{10,11},{13,12},{14,15},{17,16},{18,... | collective-permute-start | bytes 786440 | tf_op jit(solution)/shard_map/ppermute | solution.py:341
  80.9 14.0 %collective-permute-start.20 = (bf16[1024,128]{1,0:T(8,128)(2,1)S(1)}, bf16[1024,128]{1,0:T(8,128)(2,1)S(1)}, u32[]{:S(2)}, u32[]{:S(2)}) collective-permute-start(bf16[1024,128]{1,0:T(8,128)(2,1)S(1)} %get-tuple-element.61), channel_id=1, source_target_pairs={{1,2},{2,1},{0,3},{3,0},{5,6},{6,5},{4,7},{7,4},{9,10},{10,9},{8,1... | collective-permute-start | bytes 786440 | tf_op jit(solution)/shard_map/ppermute | solution.py:340
  83.9 14.0 %collective-permute-start.16 = (bf16[2,2,64,512]{3,2,1,0:T(8,128)(2,1)S(1)}, bf16[2,2,64,512]{3,2,1,0:T(8,128)(2,1)S(1)}, u32[]{:S(2)}, u32[]{:S(2)}) collective-permute-start(bf16[2,2,64,512]{3,2,1,0:T(8,128)(2,1)S(1)} %get-tuple-element.55), channel_id=1, source_target_pairs={{0,4},{4,0},{8,12},{12,8},{16,20},{20,16},{24,28},{28,24},{1,5},{5... | collective-permute-start | bytes 786440 | tf_op jit(solution)/shard_map/ppermute | solution.py:349
  99.3 8.1 %collective-permute-start.17 = (bf16[2,64,512]{2,1,0:T(8,128)(2,1)S(1)}, bf16[2,64,512]{2,1,0:T(8,128)(2,1)S(1)}, u32[]{:S(2)}, u32[]{:S(2)}) collective-permute-start(bf16[2,64,512]{2,1,0:T(8,128)(2,1)S(1)} %get-tuple-element.57), channel_id=1, source_target_pairs={{0,8},{4,12},{8,0},{12,4},{16,24},{20,28},{24,16},{28,20},{1,9},{5... | collective-permute-start | bytes 393224 | tf_op jit(solution)/shard_map/ppermute | solution.py:355
  100.9 8.2 %collective-permute-start.18 = (bf16[2,64,512]{2,1,0:T(8,128)(2,1)S(1)}, bf16[2,64,512]{2,1,0:T(8,128)(2,1)S(1)}, u32[]{:S(2)}, u32[]{:S(2)}) collective-permute-start(bf16[2,64,512]{2,1,0:T(8,128)(2,1)S(1)} %get-tuple-element.58), channel_id=1, source_target_pairs={{0,16},{4,20},{8,24},{12,28},{16,0},{20,4},{24,8},{28,12},{1,17},{... | collective-permute-start | bytes 393224 | tf_op jit(solution)/shard_map/ppermute | solution.py:355
  102.4 7.4 %collective-permute-start.19 = (bf16[2,64,512]{2,1,0:T(8,128)(2,1)S(1)}, bf16[2,64,512]{2,1,0:T(8,128)(2,1)S(1)}, u32[]{:S(2)}, u32[]{:S(2)}) collective-permute-start(bf16[2,64,512]{2,1,0:T(8,128)(2,1)S(1)} %get-tuple-element.59), channel_id=1, source_target_pairs={{0,24},{4,28},{8,16},{12,20},{16,8},{20,12},{24,0},{28,4},{1,25},{... | collective-permute-start | bytes 393224 | tf_op jit(solution)/shard_map/ppermute | solution.py:355
  104.3 7.3 %collective-permute-start.23 = (bf16[2,64,512]{2,1,0:T(8,128)(2,1)S(1)}, bf16[2,64,512]{2,1,0:T(8,128)(2,1)S(1)}, u32[]{:S(2)}, u32[]{:S(2)}) collective-permute-start(bf16[2,64,512]{2,1,0:T(8,128)(2,1)S(1)} %get-tuple-element.66), channel_id=1, source_target_pairs={{0,8},{4,12},{8,0},{12,4},{16,24},{20,28},{24,16},{28,20},{1,9},{5... | collective-permute-start | bytes 393224 | tf_op jit(solution)/shard_map/ppermute | solution.py:355
  105.8 9.0 %collective-permute-start.24 = (bf16[2,64,512]{2,1,0:T(8,128)(2,1)S(1)}, bf16[2,64,512]{2,1,0:T(8,128)(2,1)S(1)}, u32[]{:S(2)}, u32[]{:S(2)}) collective-permute-start(bf16[2,64,512]{2,1,0:T(8,128)(2,1)S(1)} %get-tuple-element.67), channel_id=1, source_target_pairs={{0,16},{4,20},{8,24},{12,28},{16,0},{20,4},{24,8},{28,12},{1,17},{... | collective-permute-start | bytes 393224 | tf_op jit(solution)/shard_map/ppermute | solution.py:355
  107.4 7.5 %collective-permute-start.25 = (bf16[2,64,512]{2,1,0:T(8,128)(2,1)S(1)}, bf16[2,64,512]{2,1,0:T(8,128)(2,1)S(1)}, u32[]{:S(2)}, u32[]{:S(2)}) collective-permute-start(bf16[2,64,512]{2,1,0:T(8,128)(2,1)S(1)} %get-tuple-element.68), channel_id=1, source_target_pairs={{0,24},{4,28},{8,16},{12,20},{16,8},{20,12},{24,0},{28,4},{1,25},{... | collective-permute-start | bytes 393224 | tf_op jit(solution)/shard_map/ppermute | solution.py:355
  (6 other events, 26.2 us)

commit v8 on v7

--- a/solution.py
+++ b/solution.py
@@ -15,7 +15,7 @@
 VMEM_BYTES = 24 * 2**20
 FRONT_BYTES = 60 * 2**20
 DESIGN_ROWS = 21
-STEP = 256
+STEP = 1024
 CROSS = 512
 FREE = pl.CostEstimate(flops=0, bytes_accessed=0, transcendentals=0)
 
@@ -75,10 +75,10 @@
     design = jnp.concatenate([jnp.ones((1, width), jnp.float32), pcs_ref[...], blank], axis=0)
     d = [t.astype(jnp.float32) for t in thirds(design)]
     stacked = jnp.concatenate(d + d[:1], axis=0).astype(jnp.bfloat16)
-    g = thirds(jnp.where(genotypes >= 0.0, genotypes, 0.0))
+    g = thirds(jnp.where(genotypes >= 0.0, genotypes, 0.0))[:2]
     lanes = (((1,), (1,)), ((), ()))
-    first, second, third = [lax.dot_general(t, stacked, lanes, preferred_element_type=jnp.float32) for t in g]
-    cross = (first[:, 2 * rows:3 * rows] + second[:, rows:2 * rows] + third[:, :rows]) + (first[:, rows:2 * rows] + second[:, :rows])
+    first, second = [lax.dot_general(t, stacked, lanes, preferred_element_type=jnp.float32) for t in g]
+    cross = (first[:, 2 * rows:3 * rows] + second[:, rows:2 * rows]) + (first[:, rows:2 * rows] + second[:, :rows])
     cross = cross + first[:, :rows]
     step = pl.program_id(0)
     mine_ref[:, pl.ds(pl.multiple_of(step * count, count), count)] = cross.T
@@ -373,6 +373,10 @@
 
 
 def solution(mesh):
-    body = line_of_four if (mesh.shape["snp"], mesh.shape["samp"]) == (8, 4) else any_mesh
+    def body(genotypes, pcs):
+        snps, width = genotypes.shape
+        fits = (mesh.shape["snp"], mesh.shape["samp"]) == (8, 4) and snps % STEP == 0 and width % 512 == 0
+        return (line_of_four if fits else any_mesh)(genotypes, pcs)
+
     in_specs = (P("snp", "samp"), P(None, "samp"))
     return jax.shard_map(body, mesh=mesh, in_specs=in_specs, out_specs=P("snp", "samp"), check_vma=False)

time: 116 us -> 115 us (level)
  Pallas kernels: 33.5 us -> 29.8 us
  waiting for transfers between devices: 49.6 us -> 51.7 us
    pallas_call x5, Pallas kernels: 18.3 us -> 14.9 us  [block_sums(): pl.pallas_call(kernel, out_shape=out, in_specs=[pl.BlockSpec(memory_space...]
  transfers between devices with their start and end apart: 26 -> 26, of which waited for: 13 -> 13; matrix products, arithmetic and copies ran while one was open for 5% -> 5% of each run, Pallas kernels for 25% -> 22%
where the time goes in v8:
time: 115 us; the launch traced here: 114 us
  waiting for transfers between devices  51.7 us (45%)
  Pallas kernels  29.8 us (26%)
  starting transfers between devices  26.9 us (23%)
  other arithmetic  4.05 us (4%)
  local copies, waits for them, and re-layouts  1.77 us (2%)
    ppermute x3, waiting for transfers between devices, line_of_four(): far = lax.ppermute(ready, 'samp', [(1, 2), (2, 1), (0, 3), (3, 0)])  17.9 us
    pallas_call x5, Pallas kernels, block_sums(): pl.pallas_call(kernel, out_shape=out, in_specs=[pl.BlockSpec(memory_space...  14.9 us
    ppermute x2, waiting for transfers between devices, line_of_four(): lax.ppermute(c, 'samp', [(i, i ^ 1) for i in range(4)])  13.6 us
    ppermute x9, starting transfers between devices, line_of_four(): lax.ppermute(sent[d - 1], 'snp', [(i, i ^ 2 * d) for i in range(8)])  10.9 us
    ppermute x9, waiting for transfers between devices, line_of_four(): lax.ppermute(sent[d - 1], 'snp', [(i, i ^ 2 * d) for i in range(8)])  10.4 us
    pallas_call x3, Pallas kernels, add_cores(): pl.pallas_call(functools.partial(add_kernel, first), out_shape=(jax.Shape...  5.61 us
    ppermute x2, waiting for transfers between devices, line_of_four(): across = [lax.ppermute(c, 'samp', [(1, 2), (2, 1)]) for c in coded]  5.45 us
    ppermute x2, starting transfers between devices, line_of_four(): across = [lax.ppermute(c, 'samp', [(1, 2), (2, 1)]) for c in coded]  4.68 us
  transfers between devices with their start and end apart: 26, of which 13 were waited for; matrix products, arithmetic and copies ran while one was open for 5% of the time, Pallas kernels for 22%

profile of v8, /device:TPU:16, one launch (start us, length us, event | category | flops | bytes accessed | tf_op | source)
XLA Modules:
  0.0 114.5 jit_solution(12417992930140884563)
XLA Ops:
  0.0 3.6 %shard_map.28 = f32[24,1536]{1,0:T(8,128)} custom-call(f32[1024,512]{1,0:T(8,128)} %own_ref.1, f32[20,512]{1,0:T(8,128)} %pcs_ref.1), custom_call_target="tpu_custom_call" | custom-call | tf_op jit(solution)/shard_map/pallas_call | solution.py:94
  3.6 1.6 %collective-permute-start = (f32[24,1536]{1,0:T(8,128)}, f32[24,1536]{1,0:T(8,128)S(1)}, u32[]{:S(2)}, u32[]{:S(2)}) collective-permute-start(f32[24,1536]{1,0:T(8,128)} %shard_map.28), channel_id=1, source_target_pairs={{0,1},{1,0},{2,3},{3,2},{4,5},{5,4},{6,7},{7,6},{8,9},{9,8},{10,11... | collective-permute-start | bytes 442376 | tf_op jit(solution)/shard_map/ppermute | solution.py:302
  6.9 2.3 %collective-permute-start.5 = (bf16[1024,256]{1,0:T(8,128)(2,1)}, bf16[1024,256]{1,0:T(8,128)(2,1)S(1)}, u32[]{:S(2)}, u32[]{:S(2)}) collective-permute-start(bf16[1024,256]{1,0:T(8,128)(2,1)} %select_convert_fusion.1), channel_id=1, source_target_pairs={{1,2},{2,1},{5,6},{6,5},{9,10},{10,9},{13,14},{14,13},{17,18},{18,... | collective-permute-start | bytes 1572872 | tf_op jit(solution)/shard_map/ppermute | solution.py:312
  9.3 1.6 %fusion = (f32[1024,64]{1,0:T(8,128)}, f32[1024,64]{1,0:T(8,128)}, f32[1024,64]{1,0:T(8,128)}, f32[1024,64]{1,0:T(8,128)}) fusion(f32[1024,512]{1,0:T(8,128)S(1)} %copy-done), kind=kLoop, calls=%fused_computation.10 | loop fusion | bytes 2097152 | tf_op jit(solution)/shard_map/slice | solution.py:309
  11.0 2.1 %pad_maximum_fusion.1 = f32[1024,256]{1,0:T(8,128)S(1)} fusion(f32[1024,64]{1,0:T(8,128)} %get-tuple-element.71, f32[1024,64]{1,0:T(8,128)} %get-tuple-element.72, f32[1024,64]{1,0:T(8,128)} %get-tuple-element.70, f32[1024,64]{1,0:T(8,128)} %get-tuple-element.69), kind=kLoop, calls=%fused_computation.1 | loop fusion | flops 786432 | bytes 2097152 | tf_op jit(solution)/shard_map/concatenate | solution.py:310
  13.5 3.1 %collective-permute-start.3 = (bf16[1024,256]{1,0:T(8,128)(2,1)S(1)}, bf16[1024,256]{1,0:T(8,128)(2,1)S(1)}, u32[]{:S(2)}, u32[]{:S(2)}) collective-permute-start(bf16[1024,256]{1,0:T(8,128)(2,1)S(1)} %select_convert_fusion), channel_id=1, source_target_pairs={{0,1},{1,0},{2,3},{3,2},{4,5},{5,4},{6,7},{7,6},{8,9},{9,8},{10,11... | collective-permute-start | bytes 1572872 | tf_op jit(solution)/shard_map/ppermute | solution.py:311
  16.6 2.3 %collective-permute-start.14 = (bf16[1024,256]{1,0:T(8,128)(2,1)S(1)}, bf16[1024,256]{1,0:T(8,128)(2,1)S(1)}, u32[]{:S(2)}, u32[]{:S(2)}) collective-permute-start(bf16[1024,256]{1,0:T(8,128)(2,1)S(1)} %select_convert_fusion), channel_id=1, source_target_pairs={{1,2},{2,1},{5,6},{6,5},{9,10},{10,9},{13,14},{14,13},{17,18},{18,... | collective-permute-start | bytes 1572872 | tf_op jit(solution)/shard_map/ppermute | solution.py:312
  19.0 2.6 %collective-permute-done.2.refs_0_ = bf16[1024,256]{1,0:T(8,128)(2,1)S(1)} collective-permute-done((bf16[1024,256]{1,0:T(8,128)(2,1)}, bf16[1024,256]{1,0:T(8,128)(2,1)S(1)}, u32[]{:S(2)}, u32[]{:S(2)}) %collective-permute-start.2) | collective-permute-done | bytes 524320 | tf_op jit(solution)/shard_map/ppermute | solution.py:311
  22.7 5.5 %collective-permute-done.5.refs_2_ = bf16[1024,256]{1,0:T(8,128)(2,1)S(1)} collective-permute-done((bf16[1024,256]{1,0:T(8,128)(2,1)}, bf16[1024,256]{1,0:T(8,128)(2,1)S(1)}, u32[]{:S(2)}, u32[]{:S(2)}) %collective-permute-start.5) | collective-permute-done | bytes 524320 | tf_op jit(solution)/shard_map/ppermute | solution.py:312
  30.3 2.9 %shard_map.29 = (bf16[192,1024]{1,0:T(8,128)(2,1)S(1)}, bf16[192,512]{1,0:T(8,128)(2,1)S(1)}, bf16[192,512]{1,0:T(8,128)(2,1)S(1)}, bf16[2,192,512]{2,1,0:T(8,128)(2,1)S(1)}) custom-call(f32[24,2048]{1,0:T(8,128)S(1)} %pad_maximum_fusion.2.pair_ref, f32[24,2048]{1,0:T(8,128)S(1)} %collective-permute-done.1.got_ref), custom_call_target="tpu_custom_call" | custom-call | flops 10000000000 | tf_op jit(solution)/shard_map/pallas_call | solution.py:139
  33.2 3.3 %shard_map.30 = (bf16[2,1024,512]{2,1,0:T(8,128)(2,1)S(1)}, f32[2,256,512]{2,1,0:T(8,128)S(1)}, bf16[2,256,512]{2,1,0:T(8,128)(2,1)S(1)}) custom-call(s32[3]{0:T(128)S(1)} %pad_add_fusion.place_ref, bf16[192,1024]{1,0:T(8,128)(2,1)S(1)} %get-tuple-element.37.coef_ref, bf16[192,512]{1,0:T(8,128)(2,1)S(1)} %get-tuple-element.38.design_ref, f32[1024,512]{1,0:T(8,128)S(1)} %copy-done), custom_call_target="tpu_custom_call" | custom-call | tf_op jit(solution)/shard_map/pallas_call | solution.py:219
  36.5 11.1 %collective-permute-done.3.refs_1_ = bf16[1024,256]{1,0:T(8,128)(2,1)S(1)} collective-permute-done((bf16[1024,256]{1,0:T(8,128)(2,1)S(1)}, bf16[1024,256]{1,0:T(8,128)(2,1)S(1)}, u32[]{:S(2)}, u32[]{:S(2)}) %collective-permute-start.3) | collective-permute-done | bytes 524320 | tf_op jit(solution)/shard_map/ppermute | solution.py:311
  47.6 3.6 %shard_map.31 = (f32[2,256,512]{2,1,0:T(8,128)S(1)}, bf16[2,256,512]{2,1,0:T(8,128)(2,1)S(1)}) custom-call(s32[3]{0:T(128)S(1)} %pad_add_fusion.place_ref, bf16[192,1024]{1,0:T(8,128)(2,1)S(1)} %get-tuple-element.37.coef_ref, bf16[192,512]{1,0:T(8,128)(2,1)S(1)} %get-tuple-element.40.design_ref, bf16[2,1024,512]{2,1,0:T(8,128)(2,1)S(1)} %get-tuple-element.60.terms_ref, ...), custom_call_target="tpu_custom_call" | custom-call | tf_op jit(solution)/shard_map/pallas_call | solution.py:219
  51.2 13.0 %collective-permute-done.4.refs_0_ = bf16[1024,256]{1,0:T(8,128)(2,1)S(1)} collective-permute-done((bf16[1024,256]{1,0:T(8,128)(2,1)S(1)}, bf16[1024,256]{1,0:T(8,128)(2,1)S(1)}, u32[]{:S(2)}, u32[]{:S(2)}) %collective-permute-start.4) | collective-permute-done | bytes 524320 | tf_op jit(solution)/shard_map/ppermute | solution.py:340
  64.3 3.6 %shard_map.32 = (f32[2,2,128,512]{3,2,1,0:T(8,128)S(1)}, bf16[2,2,128,512]{3,2,1,0:T(8,128)(2,1)S(1)}) custom-call(s32[3]{0:T(128)S(1)} %pad_add_fusion.place_ref, bf16[192,1024]{1,0:T(8,128)(2,1)S(1)} %get-tuple-element.37.coef_ref, bf16[2,192,512]{2,1,0:T(8,128)(2,1)S(1)} %get-tuple-element.45.design_ref, ...), custom_call_target="tpu_custom_call" | custom-call | tf_op jit(solution)/shard_map/pallas_call | solution.py:219
  69.9 2.8 %shard_map.33 = (f32[2,128,512]{2,1,0:T(8,128)S(1)}, bf16[2,128,512]{2,1,0:T(8,128)(2,1)S(1)}, bf16[2,128,512]{2,1,0:T(8,128)(2,1)S(1)}, bf16[2,128,512]{2,1,0:T(8,128)(2,1)S(1)}) custom-call(s32[3]{0:T(128)S(1)} %pad_add_fusion.place_ref, f32[2,256,512]{2,1,0:T(8,128)S(1)} %get-tuple-element.39.own_ref, f32[2,256,512]{2,1,0:T(8,128)S(1)} %get-tuple-element.44.near_ref, ...), custom_call_target="tpu_custom_call" | custom-call | tf_op jit(solution)/shard_map/pallas_call | solution.py:245
  76.3 2.4 %collective-permute-done.13.refs_0_ = bf16[1024,128]{1,0:T(8,128)(2,1)S(1)} collective-permute-done((bf16[1024,128]{1,0:T(8,128)(2,1)S(1)}, bf16[1024,128]{1,0:T(8,128)(2,1)S(1)}, u32[]{:S(2)}, u32[]{:S(2)}) %collective-permute-start.13) | collective-permute-done | bytes 262176 | tf_op jit(solution)/shard_map/ppermute | solution.py:340
  80.2 2.2 %shard_map.34 = (f32[2,2,64,512]{3,2,1,0:T(8,128)S(1)}, bf16[2,2,64,512]{3,2,1,0:T(8,128)(2,1)S(1)}) custom-call(s32[3]{0:T(128)S(1)} %pad_add_fusion.place_ref, bf16[192,1024]{1,0:T(8,128)(2,1)S(1)} %get-tuple-element.37.coef_ref, bf16[2,192,512]{2,1,0:T(8,128)(2,1)S(1)} %get-tuple-element.45.design_ref, ...), custom_call_target="tpu_custom_call" | custom-call | tf_op jit(solution)/shard_map/pallas_call | solution.py:219
  82.6 5.4 %collective-permute-done.11.refs_2_ = bf16[2,128,512]{2,1,0:T(8,128)(2,1)S(1)} collective-permute-done((bf16[2,128,512]{2,1,0:T(8,128)(2,1)S(1)}, bf16[2,128,512]{2,1,0:T(8,128)(2,1)S(1)}, u32[]{:S(2)}, u32[]{:S(2)}) %collective-permute-start.11) | collective-permute-done | bytes 262176 | tf_op jit(solution)/shard_map/ppermute | solution.py:355
  88.0 3.6 %collective-permute-done.21.refs_1_ = bf16[1024,128]{1,0:T(8,128)(2,1)S(1)} collective-permute-done((bf16[1024,128]{1,0:T(8,128)(2,1)S(1)}, bf16[1024,128]{1,0:T(8,128)(2,1)S(1)}, u32[]{:S(2)}, u32[]{:S(2)}) %collective-permute-start.21) | collective-permute-done | bytes 262176 | tf_op jit(solution)/shard_map/ppermute | solution.py:341
  91.6 2.5 %collective-permute-done.20.refs_0_ = bf16[1024,128]{1,0:T(8,128)(2,1)S(1)} collective-permute-done((bf16[1024,128]{1,0:T(8,128)(2,1)S(1)}, bf16[1024,128]{1,0:T(8,128)(2,1)S(1)}, u32[]{:S(2)}, u32[]{:S(2)}) %collective-permute-start.20) | collective-permute-done | bytes 262176 | tf_op jit(solution)/shard_map/ppermute | solution.py:340
  94.1 2.2 %shard_map.37 = (f32[2,2,64,512]{3,2,1,0:T(8,128)S(1)}, bf16[2,2,64,512]{3,2,1,0:T(8,128)(2,1)S(1)}) custom-call(s32[3]{0:T(128)S(1)} %pad_add_fusion.place_ref, bf16[192,1024]{1,0:T(8,128)(2,1)S(1)} %get-tuple-element.37.coef_ref, bf16[2,192,512]{2,1,0:T(8,128)(2,1)S(1)} %get-tuple-element.45.design_ref, ...), custom_call_target="tpu_custom_call" | custom-call | tf_op jit(solution)/shard_map/pallas_call | solution.py:219
  108.3 1.8 %shard_map.36.refs_0_ = f32[256,512]{1,0:T(8,128)} custom-call(f32[2,128,512]{2,1,0:T(8,128)S(1)} %get-tuple-element.50.refs_0_, bf16[2,128,512]{2,1,0:T(8,128)(2,1)S(1)} %collective-permute-done.10.refs_1_, bf16[2,128,512]{2,1,0:T(8,128)(2,1)S(1)} %collective-permute-done.11.refs_2_, bf16[2,128,512]{2,1,0:T(8,128)(2,1)S(1)} %collective-permute-done.12.refs_3_, ...), custom_call_target="tpu_custom_call" | custom-call | tf_op jit(solution)/shard_map/pallas_call | solution.py:270
  110.1 3.3 %collective-permute-done.24.refs_3_ = bf16[2,64,512]{2,1,0:T(8,128)(2,1)S(1)} collective-permute-done((bf16[2,64,512]{2,1,0:T(8,128)(2,1)S(1)}, bf16[2,64,512]{2,1,0:T(8,128)(2,1)S(1)}, u32[]{:S(2)}, u32[]{:S(2)}) %collective-permute-start.24) | collective-permute-done | bytes 131104 | tf_op jit(solution)/shard_map/ppermute | solution.py:355
  (62 shorter events, 25.9 us)
Async XLA Ops:
  3.6 9.5 %collective-permute-start = (f32[24,1536]{1,0:T(8,128)}, f32[24,1536]{1,0:T(8,128)S(1)}, u32[]{:S(2)}, u32[]{:S(2)}) collective-permute-start(f32[24,1536]{1,0:T(8,128)} %shard_map.28), channel_id=1, source_target_pairs={{0,1},{1,0},{2,3},{3,2},{4,5},{5,4},{6,7},{7,6},{8,9},{9,8},{10,11... | collective-permute-start | bytes 442376 | tf_op jit(solution)/shard_map/ppermute | solution.py:302
  6.5 15.1 %collective-permute-start.2 = (bf16[1024,256]{1,0:T(8,128)(2,1)}, bf16[1024,256]{1,0:T(8,128)(2,1)S(1)}, u32[]{:S(2)}, u32[]{:S(2)}) collective-permute-start(bf16[1024,256]{1,0:T(8,128)(2,1)} %select_convert_fusion.1), channel_id=1, source_target_pairs={{0,1},{1,0},{2,3},{3,2},{4,5},{5,4},{6,7},{7,6},{8,9},{9,8},{10,11... | collective-permute-start | bytes 1572872 | tf_op jit(solution)/shard_map/ppermute | solution.py:311
  6.9 21.2 %collective-permute-start.5 = (bf16[1024,256]{1,0:T(8,128)(2,1)}, bf16[1024,256]{1,0:T(8,128)(2,1)S(1)}, u32[]{:S(2)}, u32[]{:S(2)}) collective-permute-start(bf16[1024,256]{1,0:T(8,128)(2,1)} %select_convert_fusion.1), channel_id=1, source_target_pairs={{1,2},{2,1},{5,6},{6,5},{9,10},{10,9},{13,14},{14,13},{17,18},{18,... | collective-permute-start | bytes 1572872 | tf_op jit(solution)/shard_map/ppermute | solution.py:312
  13.2 17.1 %collective-permute-start.1 = (f32[24,2048]{1,0:T(8,128)S(1)}, f32[24,2048]{1,0:T(8,128)S(1)}, u32[]{:S(2)}, u32[]{:S(2)}) collective-permute-start(f32[24,2048]{1,0:T(8,128)S(1)} %pad_maximum_fusion.2.pair_ref), channel_id=1, source_target_pairs={{0,2},{1,3},{2,0},{3,1},{4,6},{5,7},{6,4},{7,5},{8,10},{9,11},{10,... | collective-permute-start | bytes 589832 | tf_op jit(solution)/shard_map/ppermute | solution.py:304
  13.5 34.0 %collective-permute-start.3 = (bf16[1024,256]{1,0:T(8,128)(2,1)S(1)}, bf16[1024,256]{1,0:T(8,128)(2,1)S(1)}, u32[]{:S(2)}, u32[]{:S(2)}) collective-permute-start(bf16[1024,256]{1,0:T(8,128)(2,1)S(1)} %select_convert_fusion), channel_id=1, source_target_pairs={{0,1},{1,0},{2,3},{3,2},{4,5},{5,4},{6,7},{7,6},{8,9},{9,8},{10,11... | collective-permute-start | bytes 1572872 | tf_op jit(solution)/shard_map/ppermute | solution.py:311
  16.6 51.9 %collective-permute-start.14 = (bf16[1024,256]{1,0:T(8,128)(2,1)S(1)}, bf16[1024,256]{1,0:T(8,128)(2,1)S(1)}, u32[]{:S(2)}, u32[]{:S(2)}) collective-permute-start(bf16[1024,256]{1,0:T(8,128)(2,1)S(1)} %select_convert_fusion), channel_id=1, source_target_pairs={{1,2},{2,1},{5,6},{6,5},{9,10},{10,9},{13,14},{14,13},{17,18},{18,... | collective-permute-start | bytes 1572872 | tf_op jit(solution)/shard_map/ppermute | solution.py:312
  21.9 42.4 %collective-permute-start.4 = (bf16[1024,256]{1,0:T(8,128)(2,1)S(1)}, bf16[1024,256]{1,0:T(8,128)(2,1)S(1)}, u32[]{:S(2)}, u32[]{:S(2)}) collective-permute-start(bf16[1024,256]{1,0:T(8,128)(2,1)S(1)} %broadcast_select_fusion), channel_id=1, source_target_pairs={{1,2},{2,1},{0,3},{3,0},{5,6},{6,5},{4,7},{7,4},{9,10},{10,9},{8,1... | collective-permute-start | bytes 1572872 | tf_op jit(solution)/shard_map/ppermute | solution.py:340
  28.1 36.1 %collective-permute-start.6 = (bf16[1024,256]{1,0:T(8,128)(2,1)S(1)}, bf16[1024,256]{1,0:T(8,128)(2,1)S(1)}, u32[]{:S(2)}, u32[]{:S(2)}) collective-permute-start(bf16[1024,256]{1,0:T(8,128)(2,1)S(1)} %collective-permute-done.5.refs_2_), channel_id=1, source_target_pairs={{1,0},{2,3},{5,4},{6,7},{9,8},{10,11},{13,12},{14,15},{17,16},{18,... | collective-permute-start | bytes 1572872 | tf_op jit(solution)/shard_map/ppermute | solution.py:341
  36.4 33.5 %collective-permute-start.7 = (bf16[2,256,512]{2,1,0:T(8,128)(2,1)S(1)}, bf16[2,256,512]{2,1,0:T(8,128)(2,1)S(1)}, u32[]{:S(2)}, u32[]{:S(2)}) collective-permute-start(bf16[2,256,512]{2,1,0:T(8,128)(2,1)S(1)} %get-tuple-element.47), channel_id=1, source_target_pairs={{0,4},{4,0},{8,12},{12,8},{16,20},{20,16},{24,28},{28,24},{1,5},{5... | collective-permute-start | bytes 1572872 | tf_op jit(solution)/shard_map/ppermute | solution.py:331
  51.2 18.8 %collective-permute-start.8 = (bf16[2,256,512]{2,1,0:T(8,128)(2,1)S(1)}, bf16[2,256,512]{2,1,0:T(8,128)(2,1)S(1)}, u32[]{:S(2)}, u32[]{:S(2)}) collective-permute-start(bf16[2,256,512]{2,1,0:T(8,128)(2,1)S(1)} %get-tuple-element.48), channel_id=1, source_target_pairs={{0,4},{4,0},{8,12},{12,8},{16,20},{20,16},{24,28},{28,24},{1,5},{5... | collective-permute-start | bytes 1572872 | tf_op jit(solution)/shard_map/ppermute | solution.py:331
  68.0 10.6 %collective-permute-start.13 = (bf16[1024,128]{1,0:T(8,128)(2,1)S(1)}, bf16[1024,128]{1,0:T(8,128)(2,1)S(1)}, u32[]{:S(2)}, u32[]{:S(2)}) collective-permute-start(bf16[1024,128]{1,0:T(8,128)(2,1)S(1)} %get-tuple-element.76), channel_id=1, source_target_pairs={{1,2},{2,1},{0,3},{3,0},{5,6},{6,5},{4,7},{7,4},{9,10},{10,9},{8,1... | collective-permute-start | bytes 786440 | tf_op jit(solution)/shard_map/ppermute | solution.py:340
  68.6 11.6 %collective-permute-start.15 = (bf16[1024,128]{1,0:T(8,128)(2,1)S(1)}, bf16[1024,128]{1,0:T(8,128)(2,1)S(1)}, u32[]{:S(2)}, u32[]{:S(2)}) collective-permute-start(bf16[1024,128]{1,0:T(8,128)(2,1)S(1)} %get-tuple-element.78), channel_id=1, source_target_pairs={{1,0},{2,3},{5,4},{6,7},{9,8},{10,11},{13,12},{14,15},{17,16},{18,... | collective-permute-start | bytes 786440 | tf_op jit(solution)/shard_map/ppermute | solution.py:341
  72.7 9.8 %collective-permute-start.10 = (bf16[2,128,512]{2,1,0:T(8,128)(2,1)S(1)}, bf16[2,128,512]{2,1,0:T(8,128)(2,1)S(1)}, u32[]{:S(2)}, u32[]{:S(2)}) collective-permute-start(bf16[2,128,512]{2,1,0:T(8,128)(2,1)S(1)} %get-tuple-element.51), channel_id=1, source_target_pairs={{0,8},{4,12},{8,0},{12,4},{16,24},{20,28},{24,16},{28,20},{1,9},{5... | collective-permute-start | bytes 786440 | tf_op jit(solution)/shard_map/ppermute | solution.py:355
  74.3 13.8 %collective-permute-start.11 = (bf16[2,128,512]{2,1,0:T(8,128)(2,1)S(1)}, bf16[2,128,512]{2,1,0:T(8,128)(2,1)S(1)}, u32[]{:S(2)}, u32[]{:S(2)}) collective-permute-start(bf16[2,128,512]{2,1,0:T(8,128)(2,1)S(1)} %get-tuple-element.52), channel_id=1, source_target_pairs={{0,16},{4,20},{8,24},{12,28},{16,0},{20,4},{24,8},{28,12},{1,17},{... | collective-permute-start | bytes 786440 | tf_op jit(solution)/shard_map/ppermute | solution.py:355
  75.8 12.2 %collective-permute-start.12 = (bf16[2,128,512]{2,1,0:T(8,128)(2,1)S(1)}, bf16[2,128,512]{2,1,0:T(8,128)(2,1)S(1)}, u32[]{:S(2)}, u32[]{:S(2)}) collective-permute-start(bf16[2,128,512]{2,1,0:T(8,128)(2,1)S(1)} %get-tuple-element.53), channel_id=1, source_target_pairs={{0,24},{4,28},{8,16},{12,20},{16,8},{20,12},{24,0},{28,4},{1,25},{... | collective-permute-start | bytes 786440 | tf_op jit(solution)/shard_map/ppermute | solution.py:355
  78.6 13.0 %collective-permute-start.21 = (bf16[1024,128]{1,0:T(8,128)(2,1)S(1)}, bf16[1024,128]{1,0:T(8,128)(2,1)S(1)}, u32[]{:S(2)}, u32[]{:S(2)}) collective-permute-start(bf16[1024,128]{1,0:T(8,128)(2,1)S(1)} %get-tuple-element.62), channel_id=1, source_target_pairs={{1,0},{2,3},{5,4},{6,7},{9,8},{10,11},{13,12},{14,15},{17,16},{18,... | collective-permute-start | bytes 786440 | tf_op jit(solution)/shard_map/ppermute | solution.py:341
  80.2 14.0 %collective-permute-start.20 = (bf16[1024,128]{1,0:T(8,128)(2,1)S(1)}, bf16[1024,128]{1,0:T(8,128)(2,1)S(1)}, u32[]{:S(2)}, u32[]{:S(2)}) collective-permute-start(bf16[1024,128]{1,0:T(8,128)(2,1)S(1)} %get-tuple-element.61), channel_id=1, source_target_pairs={{1,2},{2,1},{0,3},{3,0},{5,6},{6,5},{4,7},{7,4},{9,10},{10,9},{8,1... | collective-permute-start | bytes 786440 | tf_op jit(solution)/shard_map/ppermute | solution.py:340
  82.5 14.0 %collective-permute-start.16 = (bf16[2,2,64,512]{3,2,1,0:T(8,128)(2,1)S(1)}, bf16[2,2,64,512]{3,2,1,0:T(8,128)(2,1)S(1)}, u32[]{:S(2)}, u32[]{:S(2)}) collective-permute-start(bf16[2,2,64,512]{3,2,1,0:T(8,128)(2,1)S(1)} %get-tuple-element.55), channel_id=1, source_target_pairs={{0,4},{4,0},{8,12},{12,8},{16,20},{20,16},{24,28},{28,24},{1,5},{5... | collective-permute-start | bytes 786440 | tf_op jit(solution)/shard_map/ppermute | solution.py:349
  97.9 8.1 %collective-permute-start.17 = (bf16[2,64,512]{2,1,0:T(8,128)(2,1)S(1)}, bf16[2,64,512]{2,1,0:T(8,128)(2,1)S(1)}, u32[]{:S(2)}, u32[]{:S(2)}) collective-permute-start(bf16[2,64,512]{2,1,0:T(8,128)(2,1)S(1)} %get-tuple-element.57), channel_id=1, source_target_pairs={{0,8},{4,12},{8,0},{12,4},{16,24},{20,28},{24,16},{28,20},{1,9},{5... | collective-permute-start | bytes 393224 | tf_op jit(solution)/shard_map/ppermute | solution.py:355
  99.4 8.2 %collective-permute-start.18 = (bf16[2,64,512]{2,1,0:T(8,128)(2,1)S(1)}, bf16[2,64,512]{2,1,0:T(8,128)(2,1)S(1)}, u32[]{:S(2)}, u32[]{:S(2)}) collective-permute-start(bf16[2,64,512]{2,1,0:T(8,128)(2,1)S(1)} %get-tuple-element.58), channel_id=1, source_target_pairs={{0,16},{4,20},{8,24},{12,28},{16,0},{20,4},{24,8},{28,12},{1,17},{... | collective-permute-start | bytes 393224 | tf_op jit(solution)/shard_map/ppermute | solution.py:355
  101.0 7.3 %collective-permute-start.19 = (bf16[2,64,512]{2,1,0:T(8,128)(2,1)S(1)}, bf16[2,64,512]{2,1,0:T(8,128)(2,1)S(1)}, u32[]{:S(2)}, u32[]{:S(2)}) collective-permute-start(bf16[2,64,512]{2,1,0:T(8,128)(2,1)S(1)} %get-tuple-element.59), channel_id=1, source_target_pairs={{0,24},{4,28},{8,16},{12,20},{16,8},{20,12},{24,0},{28,4},{1,25},{... | collective-permute-start | bytes 393224 | tf_op jit(solution)/shard_map/ppermute | solution.py:355
  102.9 7.3 %collective-permute-start.23 = (bf16[2,64,512]{2,1,0:T(8,128)(2,1)S(1)}, bf16[2,64,512]{2,1,0:T(8,128)(2,1)S(1)}, u32[]{:S(2)}, u32[]{:S(2)}) collective-permute-start(bf16[2,64,512]{2,1,0:T(8,128)(2,1)S(1)} %get-tuple-element.66), channel_id=1, source_target_pairs={{0,8},{4,12},{8,0},{12,4},{16,24},{20,28},{24,16},{28,20},{1,9},{5... | collective-permute-start | bytes 393224 | tf_op jit(solution)/shard_map/ppermute | solution.py:355
  104.4 9.0 %collective-permute-start.24 = (bf16[2,64,512]{2,1,0:T(8,128)(2,1)S(1)}, bf16[2,64,512]{2,1,0:T(8,128)(2,1)S(1)}, u32[]{:S(2)}, u32[]{:S(2)}) collective-permute-start(bf16[2,64,512]{2,1,0:T(8,128)(2,1)S(1)} %get-tuple-element.67), channel_id=1, source_target_pairs={{0,16},{4,20},{8,24},{12,28},{16,0},{20,4},{24,8},{28,12},{1,17},{... | collective-permute-start | bytes 393224 | tf_op jit(solution)/shard_map/ppermute | solution.py:355
  106.0 7.5 %collective-permute-start.25 = (bf16[2,64,512]{2,1,0:T(8,128)(2,1)S(1)}, bf16[2,64,512]{2,1,0:T(8,128)(2,1)S(1)}, u32[]{:S(2)}, u32[]{:S(2)}) collective-permute-start(bf16[2,64,512]{2,1,0:T(8,128)(2,1)S(1)} %get-tuple-element.68), channel_id=1, source_target_pairs={{0,24},{4,28},{8,16},{12,20},{16,8},{20,12},{24,0},{28,4},{1,25},{... | collective-permute-start | bytes 393224 | tf_op jit(solution)/shard_map/ppermute | solution.py:355
  (6 other events, 25.7 us)

commit v9 on v8

--- a/solution.py
+++ b/solution.py
@@ -65,12 +65,13 @@
     return lax.dot_general(left, right, OVER_ROWS, preferred_element_type=jnp.float32)
 
 
-def cross_kernel(genotypes_ref, pcs_ref, mine_ref):
+def cross_kernel(columns, genotypes_ref, pcs_ref, mine_ref, coded_ref):
     count, width = genotypes_ref.shape
     k = pcs_ref.shape[0]
     rows = mine_ref.shape[0]
     snps = mine_ref.shape[1] - width
     genotypes = genotypes_ref[...]
+    coded_ref[...] = encode(jnp.concatenate([genotypes[:, at:at + n] for at, n in columns], axis=1))
     blank = jnp.zeros((rows - k - 1, width), jnp.float32)
     design = jnp.concatenate([jnp.ones((1, width), jnp.float32), pcs_ref[...], blank], axis=0)
     d = [t.astype(jnp.float32) for t in thirds(design)]
@@ -88,15 +89,16 @@
         mine_ref[:, snps:] = design
 
 
-def cross_part(genotypes, pcs):
+def cross_part(genotypes, pcs, columns):
     snps, width = genotypes.shape
+    size = sum(n for _, n in columns)
     rows = DESIGN_ROWS + -DESIGN_ROWS % 8
     return pl.pallas_call(
-        cross_kernel,
+        functools.partial(cross_kernel, columns),
         grid=(snps // CROSS,),
-        out_shape=jax.ShapeDtypeStruct((rows, snps + width), jnp.float32),
+        out_shape=(jax.ShapeDtypeStruct((rows, snps + width), jnp.float32), jax.ShapeDtypeStruct((snps, size), jnp.bfloat16)),
         in_specs=[pl.BlockSpec((CROSS, width), lambda i: (i, 0)), pl.BlockSpec(pcs.shape, lambda i: (0, 0))],
-        out_specs=pl.BlockSpec((rows, snps + width), lambda i: (0, 0)),
+        out_specs=(pl.BlockSpec((rows, snps + width), lambda i: (0, 0)), pl.BlockSpec((CROSS, size), lambda i: (i, 0))),
         compiler_params=pltpu.CompilerParams(vmem_limit_bytes=FRONT_BYTES),
         cost_estimate=FREE,
     )(genotypes, pcs)
@@ -142,7 +144,7 @@
         in_specs=[vmem] * 2,
         out_specs=(vmem,) * 4,
         compiler_params=pltpu.CompilerParams(vmem_limit_bytes=VMEM_BYTES),
-        cost_estimate=pl.CostEstimate(flops=10**10, bytes_accessed=0, transcendentals=0),
+        cost_estimate=pl.CostEstimate(flops=10**11, bytes_accessed=0, transcendentals=0),
     )(pair, got)
 
 
@@ -297,17 +299,16 @@
     place = jnp.stack([lax.rem(s, 2), inner.astype(jnp.int32), chip ^ z])
     other_core = [(i, i ^ 1) for i in range(8)]
     cuts, pieces = ((0, half // 2), (half // 2, half // 4), (3 * half // 4, half // 4)), ((0,), (1, 2))
-    mine = cross_part(genotypes, pcs)
+    columns = [[(at, n) for p in piece for first, n in cuts[p:p + 1] for at in (first, first + half)] for piece in pieces]
+    mine, ahead = cross_part(genotypes, pcs, columns[0])
     snps = genotypes.shape[0]
     other = lax.ppermute(mine, "samp", [(i, i ^ 1) for i in range(4)])
     pair = jnp.concatenate([mine[:, :snps] + other[:, :snps], mine[:, snps:], other[:, snps:]], axis=1)
     got = lax.ppermute(pair, "samp", [(i, i ^ 2) for i in range(4)])
     coef, design_own, design_near, design_late = coefficients(pair, got, snps, cuts)
 
-    coded = []
-    for piece in pieces:
-        columns = [genotypes[:, at:at + n] for p in piece for first, n in cuts[p:p + 1] for at in (first, first + half)]
-        coded.append(encode(after(jnp.concatenate(columns, axis=1), mine if not coded else pair)))
+    rest = [jnp.concatenate([genotypes[:, at:at + n] for at, n in c], axis=1) for c in columns[1:]]
+    coded = [after(ahead, mine)] + [encode(after(r, pair)) for r in rest]
     near = [lax.ppermute(c, "samp", [(i, i ^ 1) for i in range(4)]) for c in coded]
     across = [lax.ppermute(c, "samp", [(1, 2), (2, 1)]) for c in coded]
     held, begin = {}, {}
@@ -351,7 +352,7 @@
         if p == 0:
             gates[2] = (kept,)
         totals.append(kept)
-        for d in range(1, 4):
+        for d in (3, 1, 2):
             totals.append(lax.ppermute(sent[d - 1], "snp", [(i, i ^ (2 * d)) for i in range(8)]))
     most = divide(totals[:-4], half, 0)
     return divide(totals[-4:], half, cuts[-1][0], (most,))

time: 115 us -> 115 us (level)
  waiting for transfers between devices: 51.7 us -> 53.3 us
  other arithmetic: 4.05 us -> 2.55 us
    ppermute x2, waiting for transfers between devices: 13.6 us -> 16.5 us  [line_of_four(): lax.ppermute(c, 'samp', [(i, i ^ 1) for i in range(4)])]
    ppermute x9, waiting for transfers between devices: 10.4 us -> 8.69 us  [line_of_four(): lax.ppermute(sent[d - 1], 'snp', [(i, i ^ 2 * d) for i in range(8)])]
    ppermute x3, waiting for transfers between devices: 3.57 us -> 5.09 us  [line_of_four(): out = lax.ppermute(again, 'samp', [(1, 0), (2, 3)])]
  transfers between devices with their start and end apart: 26 -> 26, of which waited for: 13 -> 12; matrix products, arithmetic and copies ran while one was open for 5% -> 4% of each run, Pallas kernels for 22% -> 22%
where the time goes in v9:
time: 115 us
  waiting for transfers between devices  53.3 us (46%)
  Pallas kernels  30.1 us (26%)
  starting transfers between devices  26.6 us (23%)
  other arithmetic  2.55 us (2%)
  local copies, waits for them, and re-layouts  1.7 us (1%)
    ppermute x3, waiting for transfers between devices, line_of_four(): far = lax.ppermute(ready, 'samp', [(1, 2), (2, 1), (0, 3), (3, 0)])  17.9 us
    ppermute x2, waiting for transfers between devices, line_of_four(): lax.ppermute(c, 'samp', [(i, i ^ 1) for i in range(4)])  16.5 us
    pallas_call x5, Pallas kernels, block_sums(): pl.pallas_call(kernel, out_shape=out, in_specs=[pl.BlockSpec(memory_space...  14.9 us
    ppermute x9, starting transfers between devices, line_of_four(): lax.ppermute(sent[d - 1], 'snp', [(i, i ^ 2 * d) for i in range(8)])  10.9 us
    ppermute x9, waiting for transfers between devices, line_of_four(): lax.ppermute(sent[d - 1], 'snp', [(i, i ^ 2 * d) for i in range(8)])  8.69 us
    pallas_call x3, Pallas kernels, add_cores(): pl.pallas_call(functools.partial(add_kernel, first), out_shape=(jax.Shape...  5.61 us
    ppermute x3, waiting for transfers between devices, line_of_four(): out = lax.ppermute(again, 'samp', [(1, 0), (2, 3)])  5.09 us
    ppermute x2, starting transfers between devices, line_of_four(): across = [lax.ppermute(c, 'samp', [(1, 2), (2, 1)]) for c in coded]  4.69 us
  transfers between devices with their start and end apart: 26, of which 12 were waited for; matrix products, arithmetic and copies ran while one was open for 4% of the time, Pallas kernels for 22%

profile of v9, /device:TPU:16, one launch (start us, length us, event | category | flops | bytes accessed | tf_op | source)
XLA Modules:
  0.0 114.6 jit_solution(9454872445505501557)
XLA Ops:
  0.0 3.8 %shard_map.28 = (f32[24,1536]{1,0:T(8,128)}, bf16[1024,256]{1,0:T(8,128)(2,1)}) custom-call(f32[1024,512]{1,0:T(8,128)} %own_ref.1, f32[20,512]{1,0:T(8,128)} %pcs_ref.1), custom_call_target="tpu_custom_call" | custom-call | tf_op jit(solution)/shard_map/pallas_call | solution.py:96
  5.9 2.3 %collective-permute-start.5 = (bf16[1024,256]{1,0:T(8,128)(2,1)}, bf16[1024,256]{1,0:T(8,128)(2,1)S(1)}, u32[]{:S(2)}, u32[]{:S(2)}) collective-permute-start(bf16[1024,256]{1,0:T(8,128)(2,1)} %get-tuple-element.46), channel_id=1, source_target_pairs={{1,2},{2,1},{5,6},{6,5},{9,10},{10,9},{13,14},{14,13},{17,18},{18,... | collective-permute-start | bytes 1572872 | tf_op jit(solution)/shard_map/ppermute | solution.py:313
  10.0 2.0 %pad_maximum_fusion = f32[1024,256]{1,0:T(8,128)S(1)} fusion(f32[1024,64]{1,0:T(8,128)} %get-tuple-element.75, f32[1024,64]{1,0:T(8,128)} %get-tuple-element.76, f32[1024,64]{1,0:T(8,128)} %get-tuple-element.74, f32[1024,64]{1,0:T(8,128)} %get-tuple-element.73), kind=kLoop, calls=%fused_computation | loop fusion | flops 786432 | bytes 2097152 | tf_op jit(solution)/shard_map/concatenate | solution.py:310
  12.5 3.1 %collective-permute-start.3 = (bf16[1024,256]{1,0:T(8,128)(2,1)S(1)}, bf16[1024,256]{1,0:T(8,128)(2,1)S(1)}, u32[]{:S(2)}, u32[]{:S(2)}) collective-permute-start(bf16[1024,256]{1,0:T(8,128)(2,1)S(1)} %select_convert_fusion), channel_id=1, source_target_pairs={{0,1},{1,0},{2,3},{3,2},{4,5},{5,4},{6,7},{7,6},{8,9},{9,8},{10,11... | collective-permute-start | bytes 1572872 | tf_op jit(solution)/shard_map/ppermute | solution.py:312
  15.6 2.3 %collective-permute-start.14 = (bf16[1024,256]{1,0:T(8,128)(2,1)S(1)}, bf16[1024,256]{1,0:T(8,128)(2,1)S(1)}, u32[]{:S(2)}, u32[]{:S(2)}) collective-permute-start(bf16[1024,256]{1,0:T(8,128)(2,1)S(1)} %select_convert_fusion), channel_id=1, source_target_pairs={{1,2},{2,1},{5,6},{6,5},{9,10},{10,9},{13,14},{14,13},{17,18},{18,... | collective-permute-start | bytes 1572872 | tf_op jit(solution)/shard_map/ppermute | solution.py:313
  17.9 4.1 %collective-permute-done.2.refs_0_ = bf16[1024,256]{1,0:T(8,128)(2,1)S(1)} collective-permute-done((bf16[1024,256]{1,0:T(8,128)(2,1)}, bf16[1024,256]{1,0:T(8,128)(2,1)S(1)}, u32[]{:S(2)}, u32[]{:S(2)}) %collective-permute-start.2) | collective-permute-done | bytes 524320 | tf_op jit(solution)/shard_map/ppermute | solution.py:312
  22.6 4.4 %collective-permute-done.5.refs_2_ = bf16[1024,256]{1,0:T(8,128)(2,1)S(1)} collective-permute-done((bf16[1024,256]{1,0:T(8,128)(2,1)}, bf16[1024,256]{1,0:T(8,128)(2,1)S(1)}, u32[]{:S(2)}, u32[]{:S(2)}) %collective-permute-start.5) | collective-permute-done | bytes 524320 | tf_op jit(solution)/shard_map/ppermute | solution.py:313
  29.2 2.9 %shard_map.29 = (bf16[192,1024]{1,0:T(8,128)(2,1)S(1)}, bf16[192,512]{1,0:T(8,128)(2,1)S(1)}, bf16[192,512]{1,0:T(8,128)(2,1)S(1)}, bf16[2,192,512]{2,1,0:T(8,128)(2,1)S(1)}) custom-call(f32[24,2048]{1,0:T(8,128)S(1)} %pad_maximum_fusion.1.pair_ref, f32[24,2048]{1,0:T(8,128)S(1)} %collective-permute-done.1.got_ref), custom_call_target="tpu_custom_call" | custom-call | flops 99999997952 | tf_op jit(solution)/shard_map/pallas_call | solution.py:141
  32.1 3.3 %shard_map.30 = (bf16[2,1024,512]{2,1,0:T(8,128)(2,1)S(1)}, f32[2,256,512]{2,1,0:T(8,128)S(1)}, bf16[2,256,512]{2,1,0:T(8,128)(2,1)S(1)}) custom-call(s32[3]{0:T(128)S(1)} %pad_add_fusion.place_ref, bf16[192,1024]{1,0:T(8,128)(2,1)S(1)} %get-tuple-element.40.coef_ref, bf16[192,512]{1,0:T(8,128)(2,1)S(1)} %get-tuple-element.41.design_ref, f32[1024,512]{1,0:T(8,128)S(1)} %copy-done), custom_call_target="tpu_custom_call" | custom-call | tf_op jit(solution)/shard_map/pallas_call | solution.py:221
  35.5 12.4 %collective-permute-done.3.refs_1_ = bf16[1024,256]{1,0:T(8,128)(2,1)S(1)} collective-permute-done((bf16[1024,256]{1,0:T(8,128)(2,1)S(1)}, bf16[1024,256]{1,0:T(8,128)(2,1)S(1)}, u32[]{:S(2)}, u32[]{:S(2)}) %collective-permute-start.3) | collective-permute-done | bytes 524320 | tf_op jit(solution)/shard_map/ppermute | solution.py:312
  47.8 3.6 %shard_map.31 = (f32[2,256,512]{2,1,0:T(8,128)S(1)}, bf16[2,256,512]{2,1,0:T(8,128)(2,1)S(1)}) custom-call(s32[3]{0:T(128)S(1)} %pad_add_fusion.place_ref, bf16[192,1024]{1,0:T(8,128)(2,1)S(1)} %get-tuple-element.40.coef_ref, bf16[192,512]{1,0:T(8,128)(2,1)S(1)} %get-tuple-element.43.design_ref, bf16[2,1024,512]{2,1,0:T(8,128)(2,1)S(1)} %get-tuple-element.64.terms_ref, ...), custom_call_target="tpu_custom_call" | custom-call | tf_op jit(solution)/shard_map/pallas_call | solution.py:221
  51.5 11.7 %collective-permute-done.4.refs_0_ = bf16[1024,256]{1,0:T(8,128)(2,1)S(1)} collective-permute-done((bf16[1024,256]{1,0:T(8,128)(2,1)S(1)}, bf16[1024,256]{1,0:T(8,128)(2,1)S(1)}, u32[]{:S(2)}, u32[]{:S(2)}) %collective-permute-start.4) | collective-permute-done | bytes 524320 | tf_op jit(solution)/shard_map/ppermute | solution.py:341
  63.2 3.6 %shard_map.32 = (f32[2,2,128,512]{3,2,1,0:T(8,128)S(1)}, bf16[2,2,128,512]{3,2,1,0:T(8,128)(2,1)S(1)}) custom-call(s32[3]{0:T(128)S(1)} %pad_add_fusion.place_ref, bf16[192,1024]{1,0:T(8,128)(2,1)S(1)} %get-tuple-element.40.coef_ref, bf16[2,192,512]{2,1,0:T(8,128)(2,1)S(1)} %get-tuple-element.49.design_ref, ...), custom_call_target="tpu_custom_call" | custom-call | tf_op jit(solution)/shard_map/pallas_call | solution.py:221
  68.9 2.8 %shard_map.33 = (f32[2,128,512]{2,1,0:T(8,128)S(1)}, bf16[2,128,512]{2,1,0:T(8,128)(2,1)S(1)}, bf16[2,128,512]{2,1,0:T(8,128)(2,1)S(1)}, bf16[2,128,512]{2,1,0:T(8,128)(2,1)S(1)}) custom-call(s32[3]{0:T(128)S(1)} %pad_add_fusion.place_ref, f32[2,256,512]{2,1,0:T(8,128)S(1)} %get-tuple-element.42.own_ref, f32[2,256,512]{2,1,0:T(8,128)S(1)} %get-tuple-element.48.near_ref, ...), custom_call_target="tpu_custom_call" | custom-call | tf_op jit(solution)/shard_map/pallas_call | solution.py:247
  71.6 2.5 %collective-permute-start.10 = (bf16[2,128,512]{2,1,0:T(8,128)(2,1)S(1)}, bf16[2,128,512]{2,1,0:T(8,128)(2,1)S(1)}, u32[]{:S(2)}, u32[]{:S(2)}) collective-permute-start(bf16[2,128,512]{2,1,0:T(8,128)(2,1)S(1)} %get-tuple-element.55), channel_id=1, source_target_pairs={{0,24},{4,28},{8,16},{12,20},{16,8},{20,12},{24,0},{28,4},{1,25},{... | collective-permute-start | bytes 786440 | tf_op jit(solution)/shard_map/ppermute | solution.py:356
  75.2 3.7 %collective-permute-done.13.refs_0_ = bf16[1024,128]{1,0:T(8,128)(2,1)S(1)} collective-permute-done((bf16[1024,128]{1,0:T(8,128)(2,1)S(1)}, bf16[1024,128]{1,0:T(8,128)(2,1)S(1)}, u32[]{:S(2)}, u32[]{:S(2)}) %collective-permute-start.13) | collective-permute-done | bytes 262176 | tf_op jit(solution)/shard_map/ppermute | solution.py:341
  80.5 2.2 %shard_map.34 = (f32[2,2,64,512]{3,2,1,0:T(8,128)S(1)}, bf16[2,2,64,512]{3,2,1,0:T(8,128)(2,1)S(1)}) custom-call(s32[3]{0:T(128)S(1)} %pad_add_fusion.place_ref, bf16[192,1024]{1,0:T(8,128)(2,1)S(1)} %get-tuple-element.40.coef_ref, bf16[2,192,512]{2,1,0:T(8,128)(2,1)S(1)} %get-tuple-element.49.design_ref, ...), custom_call_target="tpu_custom_call" | custom-call | tf_op jit(solution)/shard_map/pallas_call | solution.py:221
  82.9 3.9 %collective-permute-done.11.refs_2_ = bf16[2,128,512]{2,1,0:T(8,128)(2,1)S(1)} collective-permute-done((bf16[2,128,512]{2,1,0:T(8,128)(2,1)S(1)}, bf16[2,128,512]{2,1,0:T(8,128)(2,1)S(1)}, u32[]{:S(2)}, u32[]{:S(2)}) %collective-permute-start.11) | collective-permute-done | bytes 262176 | tf_op jit(solution)/shard_map/ppermute | solution.py:356
  86.7 5.1 %collective-permute-done.21.refs_1_ = bf16[1024,128]{1,0:T(8,128)(2,1)S(1)} collective-permute-done((bf16[1024,128]{1,0:T(8,128)(2,1)S(1)}, bf16[1024,128]{1,0:T(8,128)(2,1)S(1)}, u32[]{:S(2)}, u32[]{:S(2)}) %collective-permute-start.21) | collective-permute-done | bytes 262176 | tf_op jit(solution)/shard_map/ppermute | solution.py:342
  91.8 2.5 %collective-permute-done.20.refs_0_ = bf16[1024,128]{1,0:T(8,128)(2,1)S(1)} collective-permute-done((bf16[1024,128]{1,0:T(8,128)(2,1)S(1)}, bf16[1024,128]{1,0:T(8,128)(2,1)S(1)}, u32[]{:S(2)}, u32[]{:S(2)}) %collective-permute-start.20) | collective-permute-done | bytes 262176 | tf_op jit(solution)/shard_map/ppermute | solution.py:341
  94.4 2.2 %shard_map.37 = (f32[2,2,64,512]{3,2,1,0:T(8,128)S(1)}, bf16[2,2,64,512]{3,2,1,0:T(8,128)(2,1)S(1)}) custom-call(s32[3]{0:T(128)S(1)} %pad_add_fusion.place_ref, bf16[192,1024]{1,0:T(8,128)(2,1)S(1)} %get-tuple-element.40.coef_ref, bf16[2,192,512]{2,1,0:T(8,128)(2,1)S(1)} %get-tuple-element.49.design_ref, ...), custom_call_target="tpu_custom_call" | custom-call | tf_op jit(solution)/shard_map/pallas_call | solution.py:221
  98.1 2.5 %collective-permute-start.17 = (bf16[2,64,512]{2,1,0:T(8,128)(2,1)S(1)}, bf16[2,64,512]{2,1,0:T(8,128)(2,1)S(1)}, u32[]{:S(2)}, u32[]{:S(2)}) collective-permute-start(bf16[2,64,512]{2,1,0:T(8,128)(2,1)S(1)} %get-tuple-element.61), channel_id=1, source_target_pairs={{0,24},{4,28},{8,16},{12,20},{16,8},{20,12},{24,0},{28,4},{1,25},{... | collective-permute-start | bytes 393224 | tf_op jit(solution)/shard_map/ppermute | solution.py:356
  103.1 2.5 %collective-permute-start.23 = (bf16[2,64,512]{2,1,0:T(8,128)(2,1)S(1)}, bf16[2,64,512]{2,1,0:T(8,128)(2,1)S(1)}, u32[]{:S(2)}, u32[]{:S(2)}) collective-permute-start(bf16[2,64,512]{2,1,0:T(8,128)(2,1)S(1)} %get-tuple-element.70), channel_id=1, source_target_pairs={{0,24},{4,28},{8,16},{12,20},{16,8},{20,12},{24,0},{28,4},{1,25},{... | collective-permute-start | bytes 393224 | tf_op jit(solution)/shard_map/ppermute | solution.py:356
  111.0 2.5 %collective-permute-done.24.refs_3_ = bf16[2,64,512]{2,1,0:T(8,128)(2,1)S(1)} collective-permute-done((bf16[2,64,512]{2,1,0:T(8,128)(2,1)S(1)}, bf16[2,64,512]{2,1,0:T(8,128)(2,1)S(1)}, u32[]{:S(2)}, u32[]{:S(2)}) %collective-permute-start.24) | collective-permute-done | bytes 131104 | tf_op jit(solution)/shard_map/ppermute | solution.py:356
  (57 shorter events, 22.2 us)
Async XLA Ops:
  3.8 8.2 %collective-permute-start = (f32[24,1536]{1,0:T(8,128)}, f32[24,1536]{1,0:T(8,128)S(1)}, u32[]{:S(2)}, u32[]{:S(2)}) collective-permute-start(f32[24,1536]{1,0:T(8,128)} %get-tuple-element.39), channel_id=1, source_target_pairs={{0,1},{1,0},{2,3},{3,2},{4,5},{5,4},{6,7},{7,6},{8,9},{9,8},{10,11... | collective-permute-start | bytes 442376 | tf_op jit(solution)/shard_map/ppermute | solution.py:305
  5.4 16.6 %collective-permute-start.2 = (bf16[1024,256]{1,0:T(8,128)(2,1)}, bf16[1024,256]{1,0:T(8,128)(2,1)S(1)}, u32[]{:S(2)}, u32[]{:S(2)}) collective-permute-start(bf16[1024,256]{1,0:T(8,128)(2,1)} %get-tuple-element.46), channel_id=1, source_target_pairs={{0,1},{1,0},{2,3},{3,2},{4,5},{5,4},{6,7},{7,6},{8,9},{9,8},{10,11... | collective-permute-start | bytes 1572872 | tf_op jit(solution)/shard_map/ppermute | solution.py:312
  5.9 21.2 %collective-permute-start.5 = (bf16[1024,256]{1,0:T(8,128)(2,1)}, bf16[1024,256]{1,0:T(8,128)(2,1)S(1)}, u32[]{:S(2)}, u32[]{:S(2)}) collective-permute-start(bf16[1024,256]{1,0:T(8,128)(2,1)} %get-tuple-element.46), channel_id=1, source_target_pairs={{1,2},{2,1},{5,6},{6,5},{9,10},{10,9},{13,14},{14,13},{17,18},{18,... | collective-permute-start | bytes 1572872 | tf_op jit(solution)/shard_map/ppermute | solution.py:313
  12.1 17.1 %collective-permute-start.1 = (f32[24,2048]{1,0:T(8,128)S(1)}, f32[24,2048]{1,0:T(8,128)S(1)}, u32[]{:S(2)}, u32[]{:S(2)}) collective-permute-start(f32[24,2048]{1,0:T(8,128)S(1)} %pad_maximum_fusion.1.pair_ref), channel_id=1, source_target_pairs={{0,2},{1,3},{2,0},{3,1},{4,6},{5,7},{6,4},{7,5},{8,10},{9,11},{10,... | collective-permute-start | bytes 589832 | tf_op jit(solution)/shard_map/ppermute | solution.py:307
  12.5 35.3 %collective-permute-start.3 = (bf16[1024,256]{1,0:T(8,128)(2,1)S(1)}, bf16[1024,256]{1,0:T(8,128)(2,1)S(1)}, u32[]{:S(2)}, u32[]{:S(2)}) collective-permute-start(bf16[1024,256]{1,0:T(8,128)(2,1)S(1)} %select_convert_fusion), channel_id=1, source_target_pairs={{0,1},{1,0},{2,3},{3,2},{4,5},{5,4},{6,7},{7,6},{8,9},{9,8},{10,11... | collective-permute-start | bytes 1572872 | tf_op jit(solution)/shard_map/ppermute | solution.py:312
  15.6 51.9 %collective-permute-start.14 = (bf16[1024,256]{1,0:T(8,128)(2,1)S(1)}, bf16[1024,256]{1,0:T(8,128)(2,1)S(1)}, u32[]{:S(2)}, u32[]{:S(2)}) collective-permute-start(bf16[1024,256]{1,0:T(8,128)(2,1)S(1)} %select_convert_fusion), channel_id=1, source_target_pairs={{1,2},{2,1},{5,6},{6,5},{9,10},{10,9},{13,14},{14,13},{17,18},{18,... | collective-permute-start | bytes 1572872 | tf_op jit(solution)/shard_map/ppermute | solution.py:313
  22.1 41.1 %collective-permute-start.4 = (bf16[1024,256]{1,0:T(8,128)(2,1)S(1)}, bf16[1024,256]{1,0:T(8,128)(2,1)S(1)}, u32[]{:S(2)}, u32[]{:S(2)}) collective-permute-start(bf16[1024,256]{1,0:T(8,128)(2,1)S(1)} %broadcast_select_fusion), channel_id=1, source_target_pairs={{1,2},{2,1},{0,3},{3,0},{5,6},{6,5},{4,7},{7,4},{9,10},{10,9},{8,1... | collective-permute-start | bytes 1572872 | tf_op jit(solution)/shard_map/ppermute | solution.py:341
  27.0 36.2 %collective-permute-start.6 = (bf16[1024,256]{1,0:T(8,128)(2,1)S(1)}, bf16[1024,256]{1,0:T(8,128)(2,1)S(1)}, u32[]{:S(2)}, u32[]{:S(2)}) collective-permute-start(bf16[1024,256]{1,0:T(8,128)(2,1)S(1)} %collective-permute-done.5.refs_2_), channel_id=1, source_target_pairs={{1,0},{2,3},{5,4},{6,7},{9,8},{10,11},{13,12},{14,15},{17,16},{18,... | collective-permute-start | bytes 1572872 | tf_op jit(solution)/shard_map/ppermute | solution.py:342
  35.4 33.5 %collective-permute-start.7 = (bf16[2,256,512]{2,1,0:T(8,128)(2,1)S(1)}, bf16[2,256,512]{2,1,0:T(8,128)(2,1)S(1)}, u32[]{:S(2)}, u32[]{:S(2)}) collective-permute-start(bf16[2,256,512]{2,1,0:T(8,128)(2,1)S(1)} %get-tuple-element.51), channel_id=1, source_target_pairs={{0,4},{4,0},{8,12},{12,8},{16,20},{20,16},{24,28},{28,24},{1,5},{5... | collective-permute-start | bytes 1572872 | tf_op jit(solution)/shard_map/ppermute | solution.py:332
  51.4 17.5 %collective-permute-start.8 = (bf16[2,256,512]{2,1,0:T(8,128)(2,1)S(1)}, bf16[2,256,512]{2,1,0:T(8,128)(2,1)S(1)}, u32[]{:S(2)}, u32[]{:S(2)}) collective-permute-start(bf16[2,256,512]{2,1,0:T(8,128)(2,1)S(1)} %get-tuple-element.52), channel_id=1, source_target_pairs={{0,4},{4,0},{8,12},{12,8},{16,20},{20,16},{24,28},{28,24},{1,5},{5... | collective-permute-start | bytes 1572872 | tf_op jit(solution)/shard_map/ppermute | solution.py:332
  67.0 11.9 %collective-permute-start.13 = (bf16[1024,128]{1,0:T(8,128)(2,1)S(1)}, bf16[1024,128]{1,0:T(8,128)(2,1)S(1)}, u32[]{:S(2)}, u32[]{:S(2)}) collective-permute-start(bf16[1024,128]{1,0:T(8,128)(2,1)S(1)} %get-tuple-element.78), channel_id=1, source_target_pairs={{1,2},{2,1},{0,3},{3,0},{5,6},{6,5},{4,7},{7,4},{9,10},{10,9},{8,1... | collective-permute-start | bytes 786440 | tf_op jit(solution)/shard_map/ppermute | solution.py:341
  67.5 12.9 %collective-permute-start.15 = (bf16[1024,128]{1,0:T(8,128)(2,1)S(1)}, bf16[1024,128]{1,0:T(8,128)(2,1)S(1)}, u32[]{:S(2)}, u32[]{:S(2)}) collective-permute-start(bf16[1024,128]{1,0:T(8,128)(2,1)S(1)} %get-tuple-element.80), channel_id=1, source_target_pairs={{1,0},{2,3},{5,4},{6,7},{9,8},{10,11},{13,12},{14,15},{17,16},{18,... | collective-permute-start | bytes 786440 | tf_op jit(solution)/shard_map/ppermute | solution.py:342
  71.6 11.1 %collective-permute-start.10 = (bf16[2,128,512]{2,1,0:T(8,128)(2,1)S(1)}, bf16[2,128,512]{2,1,0:T(8,128)(2,1)S(1)}, u32[]{:S(2)}, u32[]{:S(2)}) collective-permute-start(bf16[2,128,512]{2,1,0:T(8,128)(2,1)S(1)} %get-tuple-element.55), channel_id=1, source_target_pairs={{0,24},{4,28},{8,16},{12,20},{16,8},{20,12},{24,0},{28,4},{1,25},{... | collective-permute-start | bytes 786440 | tf_op jit(solution)/shard_map/ppermute | solution.py:356
  74.1 12.6 %collective-permute-start.11 = (bf16[2,128,512]{2,1,0:T(8,128)(2,1)S(1)}, bf16[2,128,512]{2,1,0:T(8,128)(2,1)S(1)}, u32[]{:S(2)}, u32[]{:S(2)}) collective-permute-start(bf16[2,128,512]{2,1,0:T(8,128)(2,1)S(1)} %get-tuple-element.56), channel_id=1, source_target_pairs={{0,8},{4,12},{8,0},{12,4},{16,24},{20,28},{24,16},{28,20},{1,9},{5... | collective-permute-start | bytes 786440 | tf_op jit(solution)/shard_map/ppermute | solution.py:356
  74.7 12.1 %collective-permute-start.12 = (bf16[2,128,512]{2,1,0:T(8,128)(2,1)S(1)}, bf16[2,128,512]{2,1,0:T(8,128)(2,1)S(1)}, u32[]{:S(2)}, u32[]{:S(2)}) collective-permute-start(bf16[2,128,512]{2,1,0:T(8,128)(2,1)S(1)} %get-tuple-element.57), channel_id=1, source_target_pairs={{0,16},{4,20},{8,24},{12,28},{16,0},{20,4},{24,8},{28,12},{1,17},{... | collective-permute-start | bytes 786440 | tf_op jit(solution)/shard_map/ppermute | solution.py:356
  78.9 13.0 %collective-permute-start.21 = (bf16[1024,128]{1,0:T(8,128)(2,1)S(1)}, bf16[1024,128]{1,0:T(8,128)(2,1)S(1)}, u32[]{:S(2)}, u32[]{:S(2)}) collective-permute-start(bf16[1024,128]{1,0:T(8,128)(2,1)S(1)} %get-tuple-element.66), channel_id=1, source_target_pairs={{1,0},{2,3},{5,4},{6,7},{9,8},{10,11},{13,12},{14,15},{17,16},{18,... | collective-permute-start | bytes 786440 | tf_op jit(solution)/shard_map/ppermute | solution.py:342
  80.4 14.0 %collective-permute-start.20 = (bf16[1024,128]{1,0:T(8,128)(2,1)S(1)}, bf16[1024,128]{1,0:T(8,128)(2,1)S(1)}, u32[]{:S(2)}, u32[]{:S(2)}) collective-permute-start(bf16[1024,128]{1,0:T(8,128)(2,1)S(1)} %get-tuple-element.65), channel_id=1, source_target_pairs={{1,2},{2,1},{0,3},{3,0},{5,6},{6,5},{4,7},{7,4},{9,10},{10,9},{8,1... | collective-permute-start | bytes 786440 | tf_op jit(solution)/shard_map/ppermute | solution.py:341
  82.7 14.0 %collective-permute-start.16 = (bf16[2,2,64,512]{3,2,1,0:T(8,128)(2,1)S(1)}, bf16[2,2,64,512]{3,2,1,0:T(8,128)(2,1)S(1)}, u32[]{:S(2)}, u32[]{:S(2)}) collective-permute-start(bf16[2,2,64,512]{3,2,1,0:T(8,128)(2,1)S(1)} %get-tuple-element.59), channel_id=1, source_target_pairs={{0,4},{4,0},{8,12},{12,8},{16,20},{20,16},{24,28},{28,24},{1,5},{5... | collective-permute-start | bytes 786440 | tf_op jit(solution)/shard_map/ppermute | solution.py:350
  98.1 8.0 %collective-permute-start.17 = (bf16[2,64,512]{2,1,0:T(8,128)(2,1)S(1)}, bf16[2,64,512]{2,1,0:T(8,128)(2,1)S(1)}, u32[]{:S(2)}, u32[]{:S(2)}) collective-permute-start(bf16[2,64,512]{2,1,0:T(8,128)(2,1)S(1)} %get-tuple-element.61), channel_id=1, source_target_pairs={{0,24},{4,28},{8,16},{12,20},{16,8},{20,12},{24,0},{28,4},{1,25},{... | collective-permute-start | bytes 393224 | tf_op jit(solution)/shard_map/ppermute | solution.py:356
  100.6 7.7 %collective-permute-start.18 = (bf16[2,64,512]{2,1,0:T(8,128)(2,1)S(1)}, bf16[2,64,512]{2,1,0:T(8,128)(2,1)S(1)}, u32[]{:S(2)}, u32[]{:S(2)}) collective-permute-start(bf16[2,64,512]{2,1,0:T(8,128)(2,1)S(1)} %get-tuple-element.62), channel_id=1, source_target_pairs={{0,8},{4,12},{8,0},{12,4},{16,24},{20,28},{24,16},{28,20},{1,9},{5... | collective-permute-start | bytes 393224 | tf_op jit(solution)/shard_map/ppermute | solution.py:356
  101.2 7.1 %collective-permute-start.19 = (bf16[2,64,512]{2,1,0:T(8,128)(2,1)S(1)}, bf16[2,64,512]{2,1,0:T(8,128)(2,1)S(1)}, u32[]{:S(2)}, u32[]{:S(2)}) collective-permute-start(bf16[2,64,512]{2,1,0:T(8,128)(2,1)S(1)} %get-tuple-element.63), channel_id=1, source_target_pairs={{0,16},{4,20},{8,24},{12,28},{16,0},{20,4},{24,8},{28,12},{1,17},{... | collective-permute-start | bytes 393224 | tf_op jit(solution)/shard_map/ppermute | solution.py:356
  103.1 7.9 %collective-permute-start.23 = (bf16[2,64,512]{2,1,0:T(8,128)(2,1)S(1)}, bf16[2,64,512]{2,1,0:T(8,128)(2,1)S(1)}, u32[]{:S(2)}, u32[]{:S(2)}) collective-permute-start(bf16[2,64,512]{2,1,0:T(8,128)(2,1)S(1)} %get-tuple-element.70), channel_id=1, source_target_pairs={{0,24},{4,28},{8,16},{12,20},{16,8},{20,12},{24,0},{28,4},{1,25},{... | collective-permute-start | bytes 393224 | tf_op jit(solution)/shard_map/ppermute | solution.py:356
  105.6 7.9 %collective-permute-start.24 = (bf16[2,64,512]{2,1,0:T(8,128)(2,1)S(1)}, bf16[2,64,512]{2,1,0:T(8,128)(2,1)S(1)}, u32[]{:S(2)}, u32[]{:S(2)}) collective-permute-start(bf16[2,64,512]{2,1,0:T(8,128)(2,1)S(1)} %get-tuple-element.71), channel_id=1, source_target_pairs={{0,8},{4,12},{8,0},{12,4},{16,24},{20,28},{24,16},{28,20},{1,9},{5... | collective-permute-start | bytes 393224 | tf_op jit(solution)/shard_map/ppermute | solution.py:356
  106.2 7.4 %collective-permute-start.25 = (bf16[2,64,512]{2,1,0:T(8,128)(2,1)S(1)}, bf16[2,64,512]{2,1,0:T(8,128)(2,1)S(1)}, u32[]{:S(2)}, u32[]{:S(2)}) collective-permute-start(bf16[2,64,512]{2,1,0:T(8,128)(2,1)S(1)} %get-tuple-element.72), channel_id=1, source_target_pairs={{0,16},{4,20},{8,24},{12,28},{16,0},{20,4},{24,8},{28,12},{1,17},{... | collective-permute-start | bytes 393224 | tf_op jit(solution)/shard_map/ppermute | solution.py:356
  (5 other events, 29.1 us)
